TPU v7x, 512 devices: a whole 4x4x16 slice. The times are simulated.
512 devices in a mesh: level: 8 (over z_lo), row: 8 (over x, z_hi), col: 8 (over y, core).
Axes of the slice: x: 4, y: 4, z: 16 (z_hi: 2, z_lo: 8; z = z_hi * 8 + z_lo), core: 2. Of those that a mesh axis runs over, the one named last changes fastest.
Arguments:
- leaf_blocks: bfloat16 [8, 24576, 2048], P('level', 'row', 'col'), may hold values from -3 to 3
- leaf_tiles: int32 [8], replicated, may hold values from 64 to 96, as said below
- leaf_maps: int32 [8, 96], replicated, may hold values from 0 to 127, as said below
- upper_maps: int32 [4, 128], replicated, may hold values from 0 to 127, as said below
- front_slots: int32 [6, 8], replicated, may hold values from 0 to 7, as said below
- pivot_diag: float32 [6, 256], replicated, may hold values from 96 to 192
Outputs:
- top_blocks: bfloat16 [8, 8192, 2048], P('level', 'row', 'col')
Inputs may be any that keep to these rules, and one draw needn't show every extreme that they name: `leaf_tiles`: each sibling pair 2i, 2i + 1 holds one block of exactly 96 tiles and one of fewer; some pair holds one of 64 tiles. `leaf_maps`: each row sends distinct leaf tiles to distinct front tiles. Cut the leaf tiles into aligned blocks of 12 and the front tiles into aligned blocks of 8; front block k belongs to row group k mod 8. From one leaf block exactly 2 tiles go to the blocks of each of four row groups and exactly 1 tile to each of the other four. `upper_maps`: each row is a permutation of the 128 tiles. Cut a lower front into aligned blocks of 8 tiles and the upper front into aligned blocks of 4; upper block k belongs to row group k mod 8. From one lower block exactly 1 tile goes to the blocks of each row group. `front_slots`: each row is a permutation of the window positions. The slot at position 0 of an upper front is at position 0 in neither of its two children.
All inputs are finite; a program needn't handle non-finite values.
Results may differ from a plain program's by a relative error of at most 0.009.
Values may be sent and summed in bfloat16 or wider, within the bound.
No kernel may reach another device: no remote copies, remote signals or barrier semaphores. Data moves between devices by JAX's collectives and lax.ppermute only.
A program may use at most 64 MiB of HBM per device.

v0:
```python
import jax
import jax.numpy as jnp
from jax import lax
from jax.sharding import PartitionSpec as P

TILE = 256
NPT = 128


def swapped(value, axis, bit):
    mask = 2**bit
    pairs = [(source, source ^ mask) for source in range(lax.axis_size(axis))]
    return lax.ppermute(value, axis, pairs)


def broadcast(value, axis, source):
    kept = jnp.where(lax.axis_index(axis) == source, value, 0).astype(value.dtype)
    return lax.psum(kept, axis)


def block_ranks(dest_rows):
    block_tiles = dest_rows.shape[1]
    positions = jnp.arange(block_tiles, dtype=jnp.int32)
    earlier = positions[None, :] < positions[:, None]
    same_row = dest_rows[:, :, None] == dest_rows[:, None, :]
    return jnp.sum(jnp.logical_and(same_row, earlier[None]), axis=2)


def pack_rows(tiles, live_tiles, child_map, own_block, row_count, capacity, front_local):
    block_tiles = tiles.shape[0]
    block_map = lax.dynamic_slice_in_dim(child_map, own_block * block_tiles, block_tiles, 0)
    dest_rows = block_map // front_local % row_count
    ranks = block_ranks(dest_rows[None])[0]
    wanted = jnp.arange(row_count * capacity, dtype=jnp.int32)
    slot_match = (dest_rows * capacity + ranks)[None, :] == wanted[:, None]
    source = jnp.sum(
        jnp.where(slot_match, jnp.arange(block_tiles, dtype=jnp.int32)[None, :], 0), axis=1
    )
    filled = jnp.logical_and(jnp.any(slot_match, axis=1), jnp.take(live_tiles, source))
    picked = jnp.take(tiles, source, axis=0)
    return jnp.where(filled[:, None, None], picked, jnp.zeros_like(picked))


def unpack_rows(
    received, child_map, block_tiles, capacity, block_count, wanted, row_count, front_local
):
    dest_rows = (child_map // front_local % row_count).reshape(block_count, block_tiles)
    ranks = block_ranks(dest_rows)
    slot_of = (jnp.arange(block_count, dtype=jnp.int32)[:, None] * capacity + ranks).reshape(-1)
    slot_match = child_map[None, :] == wanted[:, None]
    slot_index = jnp.sum(jnp.where(slot_match, slot_of[None, :], 0), axis=1)
    filled = jnp.any(slot_match, axis=1)
    picked = jnp.take(received, slot_index, axis=0)
    return jnp.where(filled[:, None, None], picked, jnp.zeros_like(picked))


def front_sum(partial_term, bit_count):
    summed = lax.psum(partial_term.astype(jnp.bfloat16), "row").astype(jnp.float32)
    for bit_index in range(bit_count):
        summed = summed + swapped(summed.astype(jnp.bfloat16), "level", bit_index).astype(
            summed.dtype
        )
    return summed


def merge_level(own_tiles, live_tiles, child_maps, own_block, bit_count, slot_place, diagonal):
    row_count = lax.axis_size("row")
    my_row = lax.axis_index("row")
    my_col = lax.axis_index("col")
    my_level = lax.axis_index("level")
    cube_count = 2**bit_count
    cube_pos = my_level % cube_count
    own_child = cube_pos // (cube_count // 2)
    front_local = NPT // (cube_count * row_count)
    block_tiles = own_tiles.shape[0]
    columns = own_tiles.shape[2]
    capacity = (block_tiles + row_count - 1) // row_count
    own_map = lax.dynamic_index_in_dim(child_maps, own_child, 0, keepdims=False)
    outgoing = pack_rows(
        own_tiles, live_tiles, own_map, own_block, row_count, capacity, front_local
    )
    arrived = lax.all_to_all(outgoing, "row", split_axis=0, concat_axis=0, tiled=True)
    local_tiles = jnp.arange(front_local, dtype=jnp.int32)
    my_device = cube_pos * row_count + my_row
    holding = arrived[None]
    for bit_index in range(bit_count):
        partner = swapped(holding, "level", bit_index)
        low_side = jnp.right_shift(my_level, bit_index) % 2 == 0
        lower_side = jnp.where(low_side, holding, partner)
        upper_side = jnp.where(low_side, partner, holding)
        holding = jnp.concatenate([lower_side, upper_side], axis=0)
    holding = holding.reshape(2, -1, TILE, columns)
    wanted = my_device * front_local + local_tiles
    block_count = cube_count // 2 * row_count
    first_part = unpack_rows(
        holding[0],
        child_maps[0],
        block_tiles,
        capacity,
        block_count,
        wanted,
        row_count,
        front_local,
    )
    second_part = unpack_rows(
        holding[1],
        child_maps[1],
        block_tiles,
        capacity,
        block_count,
        wanted,
        row_count,
        front_local,
    )
    assembled = first_part.astype(jnp.float32) + second_part.astype(jnp.float32)
    slot_here = columns // TILE
    slot_total = slot_here * lax.axis_size("col")
    positions = jnp.arange(slot_total, dtype=jnp.int32)
    pivot_slot = jnp.sum(jnp.where(slot_place == 0, positions, 0))
    pivot_col = pivot_slot // slot_here
    at_pivot = my_col == pivot_col
    on_top = my_device == 0
    column = assembled
    corner = column[0]
    corner_part = jnp.where(
        jnp.logical_and(at_pivot, on_top), (corner + corner.T) * 0.5, jnp.zeros_like(corner)
    )
    corner = front_sum(corner_part, bit_count) + jnp.diag(diagonal)
    factor = jnp.linalg.cholesky(corner)
    column = column.at[0].set(jnp.where(on_top, corner, column[0]))

    def solve_panel(stacked):
        solved = lax.linalg.triangular_solve(
            factor, stacked, left_side=False, lower=True, transpose_a=True
        )
        return solved.astype(jnp.bfloat16)

    def skip_panel(stacked):
        return jnp.zeros(stacked.shape, jnp.bfloat16)

    panel_rows = lax.cond(at_pivot, solve_panel, skip_panel, column.reshape(-1, TILE))
    panel_rows = broadcast(panel_rows, "col", pivot_col)
    spacing = NPT // slot_total
    my_places = lax.dynamic_slice_in_dim(slot_place, my_col * slot_here, slot_here, 0)
    window_tiles = my_places * spacing
    owned = window_tiles // front_local == my_device
    picked = jnp.take(
        panel_rows.reshape(front_local, TILE, TILE), window_tiles % front_local, axis=0
    )
    picked = jnp.where(owned[:, None, None], picked.astype(jnp.float32), jnp.zeros((), jnp.float32))
    chosen = front_sum(picked, bit_count).astype(jnp.bfloat16)
    update = jnp.einsum("ik,ljk->ilj", panel_rows, chosen, preferred_element_type=jnp.float32)
    result = assembled.reshape(-1, slot_here, TILE) - update
    local_rows = jnp.arange(front_local * TILE, dtype=jnp.int32)
    keep_rows = jnp.logical_or(jnp.logical_not(on_top), local_rows >= TILE)
    my_slots = my_col * slot_here + jnp.arange(slot_here, dtype=jnp.int32)
    keep_cols = my_slots != pivot_slot
    keep_mask = jnp.logical_and(keep_rows[:, None, None], keep_cols[None, :, None])
    result = jnp.where(keep_mask, result, jnp.zeros((), jnp.float32)).astype(jnp.bfloat16)
    return result.reshape(front_local, TILE, columns)


def body(leaf_blocks, leaf_tiles, leaf_maps, upper_maps, front_slots, pivot_diag):
    level_count = lax.axis_size("level")
    row_count = lax.axis_size("row")
    my_level = lax.axis_index("level")
    my_row = lax.axis_index("row")
    columns = leaf_blocks.shape[2]
    tile_data = leaf_blocks.reshape(-1, TILE, columns)
    leaf_count = tile_data.shape[0]
    tile_ids = my_row * leaf_count + jnp.arange(leaf_count, dtype=jnp.int32)
    live_rows = tile_ids < jnp.take(leaf_tiles, my_level)
    lower_index = my_level // 2
    pair_maps = lax.dynamic_slice_in_dim(leaf_maps, lower_index * 2, 2, 0)
    blocks = merge_level(
        tile_data,
        live_rows,
        pair_maps,
        my_row,
        1,
        jnp.take(front_slots, lower_index, axis=0),
        jnp.take(pivot_diag, lower_index, axis=0),
    )
    upper_index = level_count // 2 + my_level // 4
    child_maps = lax.dynamic_slice_in_dim(upper_maps, my_level // 4 * 2, 2, 0)
    own_block = my_level % 2 * row_count + my_row
    all_live = jnp.ones((blocks.shape[0],), jnp.bool_)
    blocks = merge_level(
        blocks,
        all_live,
        child_maps,
        own_block,
        2,
        jnp.take(front_slots, upper_index, axis=0),
        jnp.take(pivot_diag, upper_index, axis=0),
    )
    return blocks.reshape(1, -1, columns)


def solution(mesh):
    return jax.shard_map(
        body,
        mesh=mesh,
        in_specs=(P("level", "row", "col"), P(), P(), P(), P(), P()),
        out_specs=P("level", "row", "col"),
        check_vma=False,
    )
```

profile of v0, /device:TPU:1, one launch (start us, length us, event | category | flops | bytes accessed | tf_op | source)
XLA Modules:
  0.0 1340.0 jit_solution(4590332495306648243)
XLA Ops:
  16.7 18.1 %all-to-all-start = ((bf16[16,256,256]{2,1,0:T(8,128)(2,1)}), bf16[16,256,256]{2,1,0:T(8,128)(2,1)}, u32[]{:S(2)}, u32[]{:S(2)}) async-start(bf16[16,256,256]{2,1,0:T(8,128)(2,1)} %select_select_fusion.2), calls=%async_computation | async-start | bytes 4194304 | tf_op jit(solution)/shard_map/all_to_all | solution.py:82
  35.7 48.4 %all-to-all-done = bf16[16,256,256]{2,1,0:T(8,128)(2,1)} async-done(((bf16[16,256,256]{2,1,0:T(8,128)(2,1)}), bf16[16,256,256]{2,1,0:T(8,128)(2,1)}, u32[]{:S(2)}, u32[]{:S(2)}) %all-to-all-start) | async-done | bytes 2097184 | tf_op jit(solution)/shard_map/all_to_all | solution.py:82
  84.1 56.1 %collective-permute-start = (bf16[1,16,256,256]{3,2,1,0:T(8,128)(2,1)}, bf16[1,16,256,256]{3,2,1,0:T(8,128)(2,1)}, u32[]{:S(2)}, u32[]{:S(2)}) collective-permute-start(bf16[1,16,256,256]{3,2,1,0:T(8,128)(2,1)} %bitcast.27), channel_id=1, source_target_pairs={{0,64},{64,0},{128,192},{192,128},{256,320},{320,256},{384,448},{4... | collective-permute-start | bytes 6291464 | tf_op jit(solution)/shard_map/ppermute | solution.py:13
  144.6 40.1 %collective-permute-done = bf16[1,16,256,256]{3,2,1,0:T(8,128)(2,1)} collective-permute-done((bf16[1,16,256,256]{3,2,1,0:T(8,128)(2,1)}, bf16[1,16,256,256]{3,2,1,0:T(8,128)(2,1)}, u32[]{:S(2)}, u32[]{:S(2)}) %collective-permute-start) | collective-permute-done | bytes 2097184 | tf_op jit(solution)/shard_map/ppermute | solution.py:13
  184.7 4.5 select_bitcast_fusion.1
  201.0 137.9 %all-reduce.8.cloned.1.call-done = bf16[256,256]{0,1:T(8,128)(2,1)} async-done(((bf16[256,256]{0,1:T(8,128)(2,1)}), bf16[256,256]{0,1:T(8,128)(2,1)}) %all-reduce.8.cloned.1.call-update) | async-done | bytes 131088 | tf_op jit(solution)/shard_map/psum | solution.py:58
  346.0 11.7 cholesky.130
  358.4 9.8 custom-call.17
  368.6 12.4 cholesky.147
  383.8 110.7 %all-reduce.10.cloned.1.call-done = bf16[2048,256]{0,1:T(8,128)(2,1)} async-done(((bf16[2048,256]{0,1:T(8,128)(2,1)}), bf16[2048,256]{0,1:T(8,128)(2,1)}) %all-reduce.10.cloned.1.call-update) | async-done | bytes 1048592 | tf_op jit(solution)/shard_map/psum | solution.py:18
  499.3 145.4 %all-reduce.12.cloned.1.call-done = bf16[1,256,256]{2,1,0:T(8,128)(2,1)} async-done(((bf16[1,256,256]{2,1,0:T(8,128)(2,1)}), bf16[1,256,256]{2,1,0:T(8,128)(2,1)}) %all-reduce.12.cloned.1.call-update) | async-done | bytes 131088 | tf_op jit(solution)/shard_map/psum | solution.py:58
  655.5 21.8 %all_to_all.10 = bf16[8,256,256]{2,1,0:T(8,128)(2,1)S(1)} all-to-all(bf16[8,256,256]{2,1,0:T(8,128)(2,1)S(1)} %select_select_fusion.5), channel_id=1, replica_groups=mesh['level'=8,'row'=8,'col'=8] {'row'}, dimensions={0} | all-to-all | bytes 2097152 | tf_op jit(solution)/shard_map/all_to_all | solution.py:82
  677.3 31.7 %collective-permute-start.3 = (bf16[1,8,256,256]{3,2,1,0:T(8,128)(2,1)S(1)}, bf16[1,8,256,256]{3,2,1,0:T(8,128)(2,1)}, u32[]{:S(2)}, u32[]{:S(2)}) collective-permute-start(bf16[1,8,256,256]{3,2,1,0:T(8,128)(2,1)S(1)} %bitcast.199), channel_id=1, source_target_pairs={{0,64},{64,0},{128,192},{192,128},{256,320},{320,256},{384,448},{4... | collective-permute-start | bytes 3145736 | tf_op jit(solution)/shard_map/ppermute | solution.py:13
  709.2 26.4 %collective-permute-done.3 = bf16[1,8,256,256]{3,2,1,0:T(8,128)(2,1)} collective-permute-done((bf16[1,8,256,256]{3,2,1,0:T(8,128)(2,1)S(1)}, bf16[1,8,256,256]{3,2,1,0:T(8,128)(2,1)}, u32[]{:S(2)}, u32[]{:S(2)}) %collective-permute-start.3) | collective-permute-done | bytes 1048608 | tf_op jit(solution)/shard_map/ppermute | solution.py:13
  742.6 91.1 %collective-permute-done.4 = bf16[2,8,256,256]{3,2,1,0:T(8,128)(2,1)} collective-permute-done((bf16[2,8,256,256]{3,2,1,0:T(8,128)(2,1)}, bf16[2,8,256,256]{3,2,1,0:T(8,128)(2,1)}, u32[]{:S(2)}, u32[]{:S(2)}) %collective-permute-start.4) | collective-permute-done | bytes 2097184 | tf_op jit(solution)/shard_map/ppermute | solution.py:13
  833.7 4.2 broadcast_select_fusion.1
  845.2 148.1 %all-reduce.14.cloned.1.call-done = bf16[256,256]{0,1:T(8,128)(2,1)} async-done(((bf16[256,256]{0,1:T(8,128)(2,1)}), bf16[256,256]{0,1:T(8,128)(2,1)}) %all-reduce.14.cloned.1.call-update) | async-done | bytes 131088 | tf_op jit(solution)/shard_map/psum | solution.py:58
  1003.3 5.7 collective-permute-done.6
  1014.0 12.5 cholesky.164
  1027.2 11.3 custom-call.18
  1041.3 13.2 cholesky.181
  1057.5 108.8 %all-reduce.16.cloned.1.call-done = bf16[1024,256]{0,1:T(8,128)(2,1)} async-done(((bf16[1024,256]{0,1:T(8,128)(2,1)}), bf16[1024,256]{0,1:T(8,128)(2,1)}) %all-reduce.16.cloned.1.call-update) | async-done | bytes 524304 | tf_op jit(solution)/shard_map/psum | solution.py:18
  1169.9 146.0 %all-reduce.18.cloned.1.call-done = bf16[1,256,256]{2,1,0:T(8,128)(2,1)} async-done(((bf16[1,256,256]{2,1,0:T(8,128)(2,1)}), bf16[1,256,256]{2,1,0:T(8,128)(2,1)}) %all-reduce.18.cloned.1.call-update) | async-done | bytes 131088 | tf_op jit(solution)/shard_map/psum | solution.py:58
  1325.8 5.0 collective-permute-done.8
  (174 shorter events, 100.4 us)
Async XLA Ops:
  6.5 4.3 copy-start
  16.7 67.4 %all-to-all-start = ((bf16[16,256,256]{2,1,0:T(8,128)(2,1)}), bf16[16,256,256]{2,1,0:T(8,128)(2,1)}, u32[]{:S(2)}, u32[]{:S(2)}) async-start(bf16[16,256,256]{2,1,0:T(8,128)(2,1)} %select_select_fusion.2), calls=%async_computation | async-start | bytes 4194304 | tf_op jit(solution)/shard_map/all_to_all | solution.py:82
  34.8 304.1 %all-reduce.8.cloned.1.call-start = ((), (), s32[]{:S(2)}) async-start(), calls=%async_computation.2 | async-start | bytes 262144 | tf_op jit(solution)/shard_map/psum | solution.py:58
  84.1 100.6 %collective-permute-start = (bf16[1,16,256,256]{3,2,1,0:T(8,128)(2,1)}, bf16[1,16,256,256]{3,2,1,0:T(8,128)(2,1)}, u32[]{:S(2)}, u32[]{:S(2)}) collective-permute-start(bf16[1,16,256,256]{3,2,1,0:T(8,128)(2,1)} %bitcast.27), channel_id=1, source_target_pairs={{0,64},{64,0},{128,192},{192,128},{256,320},{320,256},{384,448},{4... | collective-permute-start | bytes 6291464 | tf_op jit(solution)/shard_map/ppermute | solution.py:13
  196.3 1.4 copy-start.1
  199.4 295.0 %all-reduce.10.cloned.1.call-start = ((), (), s32[]{:S(2)}) async-start(), calls=%async_computation.3 | async-start | bytes 2097152 | tf_op jit(solution)/shard_map/psum | solution.py:18
  338.9 5.9 collective-permute-start.1
  383.5 261.2 %all-reduce.12.cloned.1.call-start = ((), (), s32[]{:S(2)}) async-start(), calls=%async_computation.4 | async-start | bytes 262144 | tf_op jit(solution)/shard_map/psum | solution.py:58
  494.5 156.1 %copy-start.5 = (bf16[2048,256]{0,1:T(8,128)(2,1)S(1)}, bf16[2048,256]{0,1:T(8,128)(2,1)}, u32[]{:S(2)}) copy-start(bf16[2048,256]{0,1:T(8,128)(2,1)} %all-reduce.10.cloned.1.call-done) | copy-start | bytes 3145732
  498.5 494.8 %all-reduce.14.cloned.1.call-start = ((), (), s32[]{:S(2)}) async-start(), calls=%async_computation.5 | async-start | bytes 262144 | tf_op jit(solution)/shard_map/psum | solution.py:58
  644.7 5.9 collective-permute-start.2
  677.3 31.9 %copy-start.4 = (bf16[8,256,256]{2,1,0:T(8,128)(2,1)}, bf16[8,256,256]{2,1,0:T(8,128)(2,1)S(1)}, u32[]{:S(2)}) copy-start(bf16[8,256,256]{2,1,0:T(8,128)(2,1)S(1)} %all_to_all.10) | copy-start | bytes 3145732
  677.3 58.3 %collective-permute-start.3 = (bf16[1,8,256,256]{3,2,1,0:T(8,128)(2,1)S(1)}, bf16[1,8,256,256]{3,2,1,0:T(8,128)(2,1)}, u32[]{:S(2)}, u32[]{:S(2)}) collective-permute-start(bf16[1,8,256,256]{3,2,1,0:T(8,128)(2,1)S(1)} %bitcast.199), channel_id=1, source_target_pairs={{0,64},{64,0},{128,192},{192,128},{256,320},{320,256},{384,448},{4... | collective-permute-start | bytes 3145736 | tf_op jit(solution)/shard_map/ppermute | solution.py:13
  737.3 1.6 copy-start.2
  738.9 94.7 %collective-permute-start.4 = (bf16[2,8,256,256]{3,2,1,0:T(8,128)(2,1)}, bf16[2,8,256,256]{3,2,1,0:T(8,128)(2,1)}, u32[]{:S(2)}, u32[]{:S(2)}) collective-permute-start(bf16[2,8,256,256]{3,2,1,0:T(8,128)(2,1)} %pad_maximum_fusion.2), channel_id=1, source_target_pairs={{0,128},{64,192},{128,0},{192,64},{256,384},{320,448},{384,256},{4... | collective-permute-start | bytes 6291464 | tf_op jit(solution)/shard_map/ppermute | solution.py:13
  843.0 166.7 %copy-start.15 = (f32[1,256]{1,0:T(1,128)S(1)}, f32[1,256]{1,0:T(1,128)}, u32[]{:S(2)}) copy-start(f32[1,256]{1,0:T(1,128)} %get-tuple-element.445) | copy-start | bytes 3076
  845.2 321.1 %all-reduce.16.cloned.1.call-start = ((), (), s32[]{:S(2)}) async-start(), calls=%async_computation.6 | async-start | bytes 1048576 | tf_op jit(solution)/shard_map/psum | solution.py:18
  993.3 5.9 collective-permute-start.5
  999.2 9.9 copy-start.12
  1000.8 8.2 collective-permute-start.6
  1055.6 260.4 %all-reduce.18.cloned.1.call-start = ((), (), s32[]{:S(2)}) async-start(), calls=%async_computation.7 | async-start | bytes 262144 | tf_op jit(solution)/shard_map/psum | solution.py:58
  1166.2 164.6 %copy-start.7 = (bf16[1024,256]{0,1:T(8,128)(2,1)S(1)}, bf16[1024,256]{0,1:T(8,128)(2,1)}, u32[]{:S(2)}) copy-start(bf16[1024,256]{0,1:T(8,128)(2,1)} %all-reduce.16.cloned.1.call-done) | copy-start | bytes 1572868
  1315.9 5.9 collective-permute-start.7
  1322.8 8.0 collective-permute-start.8
  (6 other events, 5.0 us)
Sparse Core Ops, SparseCore 0:
  199.6 139.3 all-reduce.7
  383.6 110.8 all-reduce.9
  498.6 146.0 all-reduce.11
  845.3 147.9 all-reduce.13
  1055.7 110.5 all-reduce.15
  1170.1 145.8 all-reduce.17
where the time goes:
time: 1350 us; the launch traced here: 1340 us
  waiting for transfers between devices  1020 us (76%)
  starting transfers between devices  122 us (9%)
  other arithmetic  112 us (8%)
  local copies, waits for them, and re-layouts  31.4 us (2%)
  blocking collectives  21.8 us (2%)
  between operations  18.9 us (1%)
    psum x4, waiting for transfers between devices, front_sum(): lax.psum(partial_term.astype(jnp.bfloat16), 'row').astype(jnp.float32)  577 us
    psum x2, waiting for transfers between devices, broadcast(): return lax.psum(kept, axis)  219 us
    ppermute x9, waiting for transfers between devices, swapped(): return lax.ppermute(value, axis, pairs)  179 us
    ppermute x9, starting transfers between devices, swapped(): return lax.ppermute(value, axis, pairs)  104 us
    another operation x9, other arithmetic, merge_level(): factor = jnp.linalg.cholesky(corner)  71.5 us
    all_to_all x1, waiting for transfers between devices, merge_level(): lax.all_to_all(outgoing, 'row', split_axis=0, concat_axis=0, tiled=True)  48.4 us
  transfers between devices with their start and end apart: 16, of which 16 were waited for; matrix products, arithmetic and copies ran while one was open for 1% of the time, Pallas kernels for 0%

commit v1 on v0

v1 whole, which is shorter than its diff:
```python
import functools

import jax
import jax.numpy as jnp
from jax import lax
from jax.experimental import pallas as pl
from jax.experimental.pallas import tpu as pltpu
from jax.sharding import PartitionSpec as P

TILE = 256
NPT = 128
STEP = 32
GROUP = 128
HIGHEST = lax.Precision.HIGHEST
VMEM = pltpu.VMEM
SMEM = pltpu.SMEM
INTERPRET = False
F32 = jnp.float32
BF16 = jnp.bfloat16


def call(kernel, out_shape, in_spaces, out_space=None, scratch=(), flops=0, moved=0):
    return pl.pallas_call(
        kernel,
        out_shape=out_shape,
        in_specs=[pl.BlockSpec(memory_space=space) for space in in_spaces],
        out_specs=pl.BlockSpec(memory_space=out_space)
        if out_space is not None
        else [pl.BlockSpec(memory_space=VMEM) for _ in out_shape],
        scratch_shapes=list(scratch),
        compiler_params=pltpu.CompilerParams(vmem_limit_bytes=32 * 2**20),
        cost_estimate=pl.CostEstimate(flops=flops, bytes_accessed=moved, transcendentals=0),
        interpret=INTERPRET,
    )


def plan_kernel(meta_ref, tiles_ref, leaf_maps_ref, upper_maps_ref, place_ref):
    level, row = meta_ref[0], meta_ref[1]
    half = row % 2
    base = level // 4 * 4

    def one(index, carry):
        source, tile = index // 12, index % 12
        quad, across = source // 4, source % 4
        leaf = base + quad
        leaf_tile = (2 * across + half) * 12 + tile
        lower_tile = leaf_maps_ref[leaf, leaf_tile]
        upper_tile = upper_maps_ref[leaf // 2, lower_tile]
        kept = jnp.logical_and(leaf_tile < tiles_ref[leaf], lower_tile != 0)
        home_row = upper_tile // 4 % 8
        position = (upper_tile // 32 * 4 + home_row // 2) * 4 + upper_tile % 4
        other = (home_row % 2 != half).astype(jnp.int32)
        place_ref[index] = jnp.where(kept, position + 64 * other, 128)
        return carry

    lax.fori_loop(0, 192, one, 0)


def pick_kernel(meta_ref, tiles_ref, leaf_maps_ref, slots_ref, pivot_ref, out_ref):
    level, row, col = meta_ref[0], meta_ref[1], meta_ref[2]
    tile = pivot_ref.shape[1]
    wanted = (0, slots_ref[level // 2, col] * 16)
    parts, across, rows = out_ref.shape[1], out_ref.shape[0], out_ref.shape[2]
    for part in range(parts):

        def look(index, found):
            leaf_tile = row * 12 + index
            match = jnp.logical_and(
                leaf_maps_ref[level, leaf_tile] == wanted[part], leaf_tile < tiles_ref[level]
            )
            return jnp.where(match, index, found)

        found = lax.fori_loop(0, 12, look, jnp.int32(-1))
        value = pivot_ref[jnp.maximum(found, 0)]
        value = jnp.where(found >= 0, value, jnp.zeros_like(value))
        out_ref[:, part] = value.reshape(across, rows, tile)


def eliminate(pivot, panel_tile, diagonal, work_ref):
    tile = pivot.shape[0]
    width = 2 * tile
    rows = lax.broadcasted_iota(jnp.int32, (tile, tile), 0)
    columns = lax.broadcasted_iota(jnp.int32, (tile, tile), 1)
    work_ref[:, :tile] = (pivot + pivot.T) * 0.5 + jnp.where(rows == columns, diagonal, 0.0)
    work_ref[:, tile:] = panel_tile.T
    group = min(GROUP, tile)
    for start in range(0, tile, STEP):
        low = start // group * group
        offset = start - low
        block = work_ref[start : start + STEP, low:]
        row_ids = lax.broadcasted_iota(jnp.int32, block.shape, 0)
        for step in range(STEP):
            lane = offset + step
            column = block[:, lane : lane + 1]
            pivot_row = block[step : step + 1, :] * (1.0 / block[step : step + 1, lane : lane + 1])
            block = jnp.where(row_ids == step, pivot_row, block - column * pivot_row)
        work_ref[start : start + STEP, low:] = block
        factor = work_ref[:, low : low + group]
        fac_rows = lax.broadcasted_iota(jnp.int32, factor.shape, 0)
        fac_cols = lax.broadcasted_iota(jnp.int32, factor.shape, 1)
        own_row = jnp.logical_and(fac_rows >= start, fac_rows < start + STEP)
        own_col = jnp.logical_and(fac_cols >= offset, fac_cols < offset + STEP)
        factor = jnp.where(jnp.logical_and(own_col, jnp.logical_not(own_row)), factor, 0.0)
        pieces = [block]
        if offset:
            pieces.insert(0, jnp.zeros((offset, width - low), F32))
        if group - offset - STEP:
            pieces.append(jnp.zeros((group - offset - STEP, width - low), F32))
        spread = jnp.concatenate(pieces, axis=0) if len(pieces) > 1 else block
        work_ref[:, low:] = work_ref[:, low:] - jnp.dot(
            factor, spread, precision=HIGHEST, preferred_element_type=F32
        )
    return work_ref[:, tile:]


def pivot_slot_of(slots_ref, front):
    slot = jnp.int32(0)
    for index in range(8):
        slot = jnp.where(slots_ref[front, index] == 0, index, slot)
    return slot


def lower_kernel(meta_ref, slots_ref, diag_ref, gathered_ref, leaf_ref, pivot_ref, out_ref, work_ref):
    level, col = meta_ref[0], meta_ref[2]
    tile = leaf_ref.shape[1]
    pivot = gathered_ref[:, 0].reshape(tile, tile).astype(F32)
    chosen = gathered_ref[:, 1].reshape(tile, tile).astype(F32)
    front = level // 2
    solved = eliminate(pivot, chosen, diag_ref[pl.ds(front, 1), :], work_ref).astype(BF16)
    dropped = pivot_slot_of(slots_ref, front) == col

    def one(index, carry):
        update = jnp.dot(pivot_ref[index], solved, preferred_element_type=F32)
        result = leaf_ref[index].astype(F32) - update
        result = jnp.where(dropped, 0.0, result).astype(BF16)
        out_ref[:, index] = result.reshape(out_ref.shape[0], out_ref.shape[2], tile)
        return carry

    lax.fori_loop(0, 12, one, 0)


def sum_kernel(place_ref, chunks_ref, keep_ref, send_ref, total_ref):
    total_ref[...] = jnp.zeros_like(total_ref)

    def one(index, carry):
        place = place_ref[index]
        total_ref[place] = total_ref[place] + chunks_ref[index].astype(F32)
        return carry

    lax.fori_loop(0, 192, one, 0, unroll=4)
    keep_ref[...] = total_ref[:64]
    send_ref[...] = total_ref[64:128].astype(BF16)


def upper_kernel(meta_ref, slots_ref, diag_ref, gathered_ref, front_ref, pivot_ref, out_ref, work_ref):
    level, row, col = meta_ref[0], meta_ref[1], meta_ref[2]
    tile = front_ref.shape[1]
    pivot = gathered_ref[:, 0].reshape(tile, tile).astype(F32)
    chosen = gathered_ref[:, 1].reshape(tile, tile).astype(F32)
    front = 4 + level // 4
    solved = eliminate(pivot, chosen, diag_ref[pl.ds(front, 1), :], work_ref).astype(BF16)
    dropped = pivot_slot_of(slots_ref, front) == col
    update = jnp.dot(pivot_ref[...], solved, preferred_element_type=F32)
    result = jnp.where(dropped, 0.0, front_ref[...] - update)
    top = jnp.logical_and(
        lax.broadcasted_iota(jnp.int32, result.shape, 0) < tile // 16, row % 2 == 0
    )
    result = jnp.where(top, 0.0, result).astype(BF16)
    out_ref[...] = result.reshape(out_ref.shape)


def lane_groups(levels):
    groups = []
    for first in range(0, 8, levels):
        for half in range(2):
            groups.append(
                [
                    (first + level) * 8 + 2 * across + half
                    for level in range(levels)
                    for across in range(4)
                ]
            )
    return groups


def exchange(value, levels):
    return lax.all_to_all(
        value,
        ("level", "row"),
        split_axis=0,
        concat_axis=0,
        axis_index_groups=lane_groups(levels),
        tiled=True,
    )


def crossed(value):
    return lax.ppermute(value, "row", [(row, row ^ 1) for row in range(8)])


def spread_columns(value, slot):
    pieces = value.reshape(8, -1, value.shape[-1])
    pieces = lax.all_to_all(pieces, "col", split_axis=0, concat_axis=0, tiled=True)
    piece = lax.dynamic_index_in_dim(pieces, slot, 0, keepdims=True)
    pieces = lax.all_to_all(
        jnp.broadcast_to(piece, pieces.shape), "col", split_axis=0, concat_axis=0, tiled=True
    )
    return pieces.reshape(value.shape)


def body(leaf_blocks, leaf_tiles, leaf_maps, upper_maps, front_slots, pivot_diag):
    tile = leaf_blocks.shape[2]
    level = lax.axis_index("level")
    row = lax.axis_index("row")
    col = lax.axis_index("col")
    meta = jnp.stack([level, row, col]).astype(jnp.int32)
    positions = jnp.arange(8, dtype=jnp.int32)
    slots = jnp.sum(jnp.where(front_slots == 0, positions[None, :], 0), axis=1)
    lower_slot = lax.dynamic_index_in_dim(slots, level // 2, keepdims=False)
    upper_slot = lax.dynamic_index_in_dim(slots, 4 + level // 4, keepdims=False)
    upper_place = lax.dynamic_slice(front_slots, (4 + level // 4, col), (1, 1))[0, 0]
    eighth, sixteenth = tile // 8, tile // 16
    own = leaf_blocks.reshape(12, tile, tile)

    place = call(
        plan_kernel,
        jax.ShapeDtypeStruct((192,), jnp.int32),
        [SMEM] * 4,
        SMEM,
    )(meta, leaf_tiles, leaf_maps, upper_maps)

    pivot_column = spread_columns(own, lower_slot)
    picked = call(
        pick_kernel,
        jax.ShapeDtypeStruct((8, 2, eighth, tile), BF16),
        [SMEM] * 4 + [VMEM],
        VMEM,
        moved=2**21,
    )(meta, leaf_tiles, leaf_maps, front_slots, pivot_column)
    parts = jnp.sum(exchange(picked, 2).astype(F32), axis=0)
    parts = parts + crossed(parts.astype(BF16)).astype(F32)
    gathered = exchange(jnp.broadcast_to(parts.astype(BF16)[None], picked.shape), 2)
    routed = call(
        lower_kernel,
        jax.ShapeDtypeStruct((16, 12, sixteenth, tile), BF16),
        [SMEM, SMEM, VMEM, VMEM, VMEM, VMEM],
        VMEM,
        [pltpu.VMEM((tile, 2 * tile), F32)],
        flops=2**30,
        moved=2**23,
    )(meta, front_slots, pivot_diag, gathered, own, pivot_column)
    chunks = exchange(routed, 4).reshape(192, sixteenth, tile)
    keep, send = call(
        sum_kernel,
        (
            jax.ShapeDtypeStruct((64, sixteenth, tile), F32),
            jax.ShapeDtypeStruct((64, sixteenth, tile), BF16),
        ),
        [SMEM, VMEM],
        None,
        [pltpu.VMEM((129, sixteenth, tile), F32)],
        moved=2**22,
    )(place, chunks)
    front = keep + crossed(send).astype(F32)

    rounded = front.astype(BF16)
    pivot_column = spread_columns(rounded, upper_slot)
    parts = jnp.stack(
        [pivot_column[0], lax.dynamic_index_in_dim(pivot_column, upper_place * 8, 0, keepdims=False)]
    )
    parts = jnp.where(row % 2 == 0, parts, crossed(parts))
    gathered = exchange(jnp.broadcast_to(parts[None], (16,) + parts.shape), 4)
    finished = call(
        upper_kernel,
        jax.ShapeDtypeStruct((16, 4, sixteenth, tile), BF16),
        [SMEM, SMEM, VMEM, VMEM, VMEM, VMEM],
        VMEM,
        [pltpu.VMEM((tile, 2 * tile), F32)],
        flops=2**28,
        moved=2**22,
    )(
        meta,
        front_slots,
        pivot_diag,
        gathered,
        front.reshape(-1, tile),
        pivot_column.reshape(-1, tile),
    )
    result = exchange(finished, 4)
    return jnp.swapaxes(result, 0, 1).reshape(1, -1, tile)


def solution(mesh):
    return jax.shard_map(
        body,
        mesh=mesh,
        in_specs=(P("level", "row", "col"), P(), P(), P(), P(), P()),
        out_specs=P("level", "row", "col"),
        check_vma=False,
    )
```

time: 1350 us -> 325 us (0.24)
  waiting for transfers between devices: 1020 us -> 83.8 us
  other arithmetic: 112 us -> 1.24 us
  Pallas kernels: 0 us -> 69.8 us
  blocking collectives: 21.8 us -> 54.9 us
  local copies, waits for them, and re-layouts: 31.4 us -> 4.21 us
  starting transfers between devices: 122 us -> 103 us
  between operations: 18.9 us -> 4.2 us
    psum x6 -> x0, waiting for transfers between devices: 797 us -> none  [the longest x4 577 us: front_sum(): lax.psum(partial_term.astype(jnp.bfloat16), 'row').astype(jnp.float32)]
    ppermute x9 -> x3, waiting for transfers between devices: 179 us -> 9.55 us  [crossed(): return lax.ppermute(value, 'row', [(row, row ^ 1) for row in range(8)])]
    another operation x9 -> x2, other arithmetic: 71.5 us -> 0.08 us  [the longest x1 0.08 us: body(): meta = jnp.stack([level, row, col]).astype(jnp.int32)]
    pallas_call x0 -> x5, Pallas kernels: none -> 69.8 us  [the longest x1 29.5 us: body(): call(lower_kernel, jax.ShapeDtypeStruct((16, 12, sixteenth, tile), BF16),...]
    ppermute x9 -> x3, starting transfers between devices: 104 us -> 67.2 us  [crossed(): return lax.ppermute(value, 'row', [(row, row ^ 1) for row in range(8)])]
    all_to_all x1 -> x4, blocking collectives: 21.8 us -> 54.9 us  [exchange(): lax.all_to_all(value, ('level', 'row'), split_axis=0, concat_axis=0, axis...]
    all_to_all x1 -> x5, waiting for transfers between devices: 48.4 us -> 74.2 us  [the longest x2 29.1 us: spread_columns(): lax.all_to_all(jnp.broadcast_to(piece, pieces.shape), 'col', split_axis=0...]
    all_to_all x1 -> x5, starting transfers between devices: 18.1 us -> 36.2 us  [the longest x2 23.6 us: spread_columns(): lax.all_to_all(pieces, 'col', split_axis=0, concat_axis=0, tiled=True)]
  transfers between devices with their start and end apart: 16 -> 8, of which waited for: 16 -> 8; matrix products, arithmetic and copies ran while one was open for 1% -> 0% of each run, Pallas kernels for 0% -> 4%
where the time goes in v1:
time: 325 us; the launch traced here: 322 us
  starting transfers between devices  103 us (32%)
  waiting for transfers between devices  83.8 us (26%)
  Pallas kernels  69.8 us (21%)
  blocking collectives  54.9 us (17%)
  local copies, waits for them, and re-layouts  4.21 us (1%)
  between operations  4.2 us (1%)
    ppermute x3, starting transfers between devices, crossed(): return lax.ppermute(value, 'row', [(row, row ^ 1) for row in range(8)])  67.2 us
    all_to_all x4, blocking collectives, exchange(): lax.all_to_all(value, ('level', 'row'), split_axis=0, concat_axis=0, axis...  54.9 us
    pallas_call x1, Pallas kernels, body(): call(lower_kernel, jax.ShapeDtypeStruct((16, 12, sixteenth, tile), BF16),...  29.5 us
    all_to_all x2, waiting for transfers between devices, spread_columns(): lax.all_to_all(jnp.broadcast_to(piece, pieces.shape), 'col', split_axis=0...  29.1 us
    pallas_call x1, Pallas kernels, body(): call(upper_kernel, jax.ShapeDtypeStruct((16, 4, sixteenth, tile), BF16),...  26.3 us
    all_to_all x2, waiting for transfers between devices, spread_columns(): lax.all_to_all(pieces, 'col', split_axis=0, concat_axis=0, tiled=True)  26 us
    all_to_all x2, starting transfers between devices, spread_columns(): lax.all_to_all(pieces, 'col', split_axis=0, concat_axis=0, tiled=True)  23.6 us
    all_to_all x1, waiting for transfers between devices, exchange(): lax.all_to_all(value, ('level', 'row'), split_axis=0, concat_axis=0, axis...  19.2 us
  transfers between devices with their start and end apart: 8, of which 8 were waited for; matrix products, arithmetic and copies ran while one was open for 0% of the time, Pallas kernels for 4%

profile of v1, /device:TPU:1, one launch (start us, length us, event | category | flops | bytes accessed | tf_op | source)
XLA Modules:
  0.0 321.6 jit_solution(15390356982907914856)
XLA Ops:
  0.0 10.5 %all-to-all-start = ((bf16[8,384,256]{2,1,0:T(8,128)(2,1)}), bf16[8,384,256]{2,1,0:T(8,128)(2,1)S(1)}, u32[]{:S(2)}, u32[]{:S(2)}) async-start(bf16[8,384,256]{2,1,0:T(8,128)(2,1)} %bitcast.23), calls=%async_computation | async-start | bytes 3145728 | tf_op jit(solution)/shard_map/all_to_all | solution.py:203
  12.9 18.3 %all-to-all-done = bf16[8,384,256]{2,1,0:T(8,128)(2,1)S(1)} async-done(((bf16[8,384,256]{2,1,0:T(8,128)(2,1)}), bf16[8,384,256]{2,1,0:T(8,128)(2,1)S(1)}, u32[]{:S(2)}, u32[]{:S(2)}) %all-to-all-start) | async-done | bytes 1572896 | tf_op jit(solution)/shard_map/all_to_all | solution.py:203
  31.3 1.3 broadcast_in_dim.39
  32.5 4.5 %all-to-all-start.1 = ((bf16[8,384,256]{2,1,0:T(8,128)(2,1)}), bf16[8,384,256]{2,1,0:T(8,128)(2,1)S(1)}, u32[]{:S(2)}, u32[]{:S(2)}) async-start(bf16[8,384,256]{2,1,0:T(8,128)(2,1)} %broadcast_in_dim.39), calls=%async_computation.1 | async-start | bytes 3145728 | tf_op jit(solution)/shard_map/all_to_all | solution.py:205
  37.1 20.7 %all-to-all-done.1 = bf16[8,384,256]{2,1,0:T(8,128)(2,1)S(1)} async-done(((bf16[8,384,256]{2,1,0:T(8,128)(2,1)}), bf16[8,384,256]{2,1,0:T(8,128)(2,1)S(1)}, u32[]{:S(2)}, u32[]{:S(2)}) %all-to-all-start.1) | async-done | bytes 1572896 | tf_op jit(solution)/shard_map/all_to_all | solution.py:205
  58.8 8.5 %all_to_all.45 = bf16[8,2,32,256]{3,2,1,0:T(8,128)(2,1)S(1)} all-to-all(bf16[8,2,32,256]{3,2,1,0:T(8,128)(2,1)S(1)} %shard_map.65), channel_id=1, replica_groups={{0,16,32,48,64,80,96,112},{8,24,40,56,72,88,104,120},{128,144,160,176,1..., dimensions={0} | all-to-all | bytes 524288 | tf_op jit(solution)/shard_map/all_to_all | solution.py:187
  67.4 12.9 %collective-permute-start = (bf16[2,32,256]{2,1,0:T(8,128)(2,1)S(1)}, bf16[2,32,256]{2,1,0:T(8,128)(2,1)S(1)}, u32[]{:S(2)}, u32[]{:S(2)}) collective-permute-start(bf16[2,32,256]{2,1,0:T(8,128)(2,1)S(1)} %convert_element_type.19), channel_id=1, source_target_pairs={{0,8},{8,0},{16,24},{24,16},{32,40},{40,32},{48,56},{56,48},{1,9},... | collective-permute-start | bytes 98312 | tf_op jit(solution)/shard_map/ppermute | solution.py:198
  80.3 1.3 collective-permute-done
  81.7 8.5 %all_to_all.46.gathered_ref = bf16[8,2,32,256]{3,2,1,0:T(8,128)(2,1)S(1)} all-to-all(bf16[8,2,32,256]{3,2,1,0:T(8,128)(2,1)S(1)} %broadcast_in_dim.40), channel_id=1, replica_groups={{0,16,32,48,64,80,96,112},{8,24,40,56,72,88,104,120},{128,144,160,176,1..., dimensions={0} | all-to-all | bytes 524288 | tf_op jit(solution)/shard_map/all_to_all | solution.py:187
  90.2 29.5 %shard_map.66 = bf16[16,12,16,256]{3,2,1,0:T(8,128)(2,1)} custom-call(s32[3]{0:T(128)S(1)} %pad_add_fusion.meta_ref, s32[6,8]{1,0:T(8,128)S(1)} %copy-done.1, f32[6,256]{1,0:T(8,128)S(1)} %copy-done.2, bf16[8,2,32,256]{3,2,1,0:T(8,128)(2,1)S(1)} %all_to_all.46.gathered_ref, bf16[12,256,256]{2,1,0:T(8,128)(2,1)S(1)} %bitcast.24, ...), custom_call_target="tpu_custom_call" | custom-call | flops 1073741824 | bytes 8388608 | tf_op jit(solution)/shard_map/pallas_call | solution.py:243
  119.6 3.8 %all-to-all-start.4 = ((bf16[16,12,16,256]{3,2,1,0:T(8,128)(2,1)}), bf16[16,12,16,256]{3,2,1,0:T(8,128)(2,1)S(1)}, u32[]{:S(2)}, u32[]{:S(2)}) async-start(bf16[16,12,16,256]{3,2,1,0:T(8,128)(2,1)} %shard_map.66), calls=%async_computation.4 | async-start | bytes 3145728 | tf_op jit(solution)/shard_map/all_to_all | solution.py:187
  123.5 11.4 %shard_map.64.place_ref = s32[192]{0:T(256)S(1)} custom-call(s32[3]{0:T(128)S(1)} %pad_add_fusion.meta_ref, s32[8]{0:T(128)S(1)} %copy-done.4, s32[8,96]{1,0:T(8,128)S(1)} %copy-done.3, s32[4,128]{1,0:T(4,128)S(1)} %copy-done.5), custom_call_target="tpu_custom_call" | custom-call | tf_op jit(solution)/shard_map/pallas_call | solution.py:225
  134.9 19.2 %all-to-all-done.4 = bf16[16,12,16,256]{3,2,1,0:T(8,128)(2,1)S(1)} async-done(((bf16[16,12,16,256]{3,2,1,0:T(8,128)(2,1)}), bf16[16,12,16,256]{3,2,1,0:T(8,128)(2,1)S(1)}, u32[]{:S(2)}, u32[]{:S(2)}) %all-to-all-start.4) | async-done | bytes 1572896 | tf_op jit(solution)/shard_map/all_to_all | solution.py:187
  154.1 1.6 shard_map.67
  155.7 12.5 %collective-permute-start.1 = (bf16[64,16,256]{2,1,0:T(8,128)(2,1)S(1)}, bf16[64,16,256]{2,1,0:T(8,128)(2,1)S(1)}, u32[]{:S(2)}, u32[]{:S(2)}) collective-permute-start(bf16[64,16,256]{2,1,0:T(8,128)(2,1)S(1)} %get-tuple-element.8), channel_id=1, source_target_pairs={{0,8},{8,0},{16,24},{24,16},{32,40},{40,32},{48,56},{56,48},{1,9},... | collective-permute-start | bytes 1572872 | tf_op jit(solution)/shard_map/ppermute | solution.py:198
  168.2 7.2 %collective-permute-done.1 = bf16[64,16,256]{2,1,0:T(8,128)(2,1)S(1)} collective-permute-done((bf16[64,16,256]{2,1,0:T(8,128)(2,1)S(1)}, bf16[64,16,256]{2,1,0:T(8,128)(2,1)S(1)}, u32[]{:S(2)}, u32[]{:S(2)}) %collective-permute-start.1) | collective-permute-done | bytes 524320 | tf_op jit(solution)/shard_map/ppermute | solution.py:198
  176.3 13.1 %all-to-all-start.5 = ((bf16[8,128,256]{2,1,0:T(8,128)(2,1)}), bf16[8,128,256]{2,1,0:T(8,128)(2,1)S(1)}, u32[]{:S(2)}, u32[]{:S(2)}) async-start(bf16[8,128,256]{2,1,0:T(8,128)(2,1)} %bitcast.9), calls=%async_computation.5 | async-start | bytes 1048576 | tf_op jit(solution)/shard_map/all_to_all | solution.py:203
  191.3 7.6 %all-to-all-done.5 = bf16[8,128,256]{2,1,0:T(8,128)(2,1)S(1)} async-done(((bf16[8,128,256]{2,1,0:T(8,128)(2,1)}), bf16[8,128,256]{2,1,0:T(8,128)(2,1)S(1)}, u32[]{:S(2)}, u32[]{:S(2)}) %all-to-all-start.5) | async-done | bytes 524320 | tf_op jit(solution)/shard_map/all_to_all | solution.py:203
  199.8 4.3 %all-to-all-start.6 = ((bf16[8,128,256]{2,1,0:T(8,128)(2,1)}), bf16[8,128,256]{2,1,0:T(8,128)(2,1)S(1)}, u32[]{:S(2)}, u32[]{:S(2)}) async-start(bf16[8,128,256]{2,1,0:T(8,128)(2,1)} %broadcast_in_dim.42), calls=%async_computation.6 | async-start | bytes 1048576 | tf_op jit(solution)/shard_map/all_to_all | solution.py:205
  205.2 8.4 %all-to-all-done.6 = bf16[8,128,256]{2,1,0:T(8,128)(2,1)S(1)} async-done(((bf16[8,128,256]{2,1,0:T(8,128)(2,1)}), bf16[8,128,256]{2,1,0:T(8,128)(2,1)S(1)}, u32[]{:S(2)}, u32[]{:S(2)}) %all-to-all-start.6) | async-done | bytes 524320 | tf_op jit(solution)/shard_map/all_to_all | solution.py:205
  213.6 41.8 %collective-permute-start.2 = (bf16[2,16,256]{2,1,0:T(8,128)(2,1)S(1)}, bf16[2,16,256]{2,1,0:T(8,128)(2,1)S(1)}, u32[]{:S(2)}, u32[]{:S(2)}) collective-permute-start(bf16[2,16,256]{2,1,0:T(8,128)(2,1)S(1)} %pad_maximum_fusion), channel_id=1, source_target_pairs={{0,8},{8,0},{16,24},{24,16},{32,40},{40,32},{48,56},{56,48},{1,9},... | collective-permute-start | bytes 49160 | tf_op jit(solution)/shard_map/ppermute | solution.py:198
  256.6 23.6 %all_to_all.47.gathered_ref = bf16[16,2,16,256]{3,2,1,0:T(8,128)(2,1)S(1)} all-to-all(bf16[16,2,16,256]{3,2,1,0:T(8,128)(2,1)S(1)} %broadcast_in_dim.43), channel_id=1, replica_groups={{0,16,32,48,64,80,96,112,128,144,160,176,192,208,224,240},{8,24,40,56,7..., dimensions={0} | all-to-all | bytes 524288 | tf_op jit(solution)/shard_map/all_to_all | solution.py:187
  280.2 26.3 %shard_map.68 = bf16[16,4,16,256]{3,2,1,0:T(8,128)(2,1)S(1)} custom-call(s32[3]{0:T(128)S(1)} %pad_add_fusion.meta_ref, s32[6,8]{1,0:T(8,128)S(1)} %copy-done.1, f32[6,256]{1,0:T(8,128)S(1)} %copy-done.2, bf16[16,2,16,256]{3,2,1,0:T(8,128)(2,1)S(1)} %all_to_all.47.gathered_ref, f32[1024,256]{1,0:T(8,128)S(1)} %bitcast.25, bf16[1024,256]{1,0:T(8,128)(2,1)S(1)} %bitcast.27), custom_call_target="tpu_custom_call" | custom-call | flops 268435456 | bytes 4194304 | tf_op jit(solution)/shard_map/pallas_call | solution.py:273
  306.4 14.3 %all_to_all.48 = bf16[16,4,16,256]{3,2,1,0:T(8,128)(2,1)S(1)} all-to-all(bf16[16,4,16,256]{3,2,1,0:T(8,128)(2,1)S(1)} %shard_map.68), channel_id=1, replica_groups={{0,16,32,48,64,80,96,112,128,144,160,176,192,208,224,240},{8,24,40,56,7..., dimensions={0} | all-to-all | bytes 1048576 | tf_op jit(solution)/shard_map/all_to_all | solution.py:187
  (31 shorter events, 6.4 us)
Async XLA Ops:
  0.0 10.5 %copy-start.1 = (s32[6,8]{1,0:T(8,128)S(1)}, s32[6,8]{1,0:T(8,128)}, u32[]{:S(2)}) copy-start(s32[6,8]{1,0:T(8,128)} %slots_ref.5) | copy-start | bytes 580
  0.0 31.2 %all-to-all-start = ((bf16[8,384,256]{2,1,0:T(8,128)(2,1)}), bf16[8,384,256]{2,1,0:T(8,128)(2,1)S(1)}, u32[]{:S(2)}, u32[]{:S(2)}) async-start(bf16[8,384,256]{2,1,0:T(8,128)(2,1)} %bitcast.23), calls=%async_computation | async-start | bytes 3145728 | tf_op jit(solution)/shard_map/all_to_all | solution.py:203
  32.5 25.2 %copy-start.3 = (s32[8,96]{1,0:T(8,128)S(1)}, s32[8,96]{1,0:T(8,128)}, u32[]{:S(2)}) copy-start(s32[8,96]{1,0:T(8,128)} %leaf_maps_ref.3) | copy-start | bytes 9220
  32.5 25.2 %copy-start.4 = (s32[8]{0:T(128)S(1)}, s32[8]{0:T(128)}, u32[]{:S(2)}) copy-start(s32[8]{0:T(128)} %tiles_ref.3) | copy-start | bytes 100
  32.5 25.2 %all-to-all-start.1 = ((bf16[8,384,256]{2,1,0:T(8,128)(2,1)}), bf16[8,384,256]{2,1,0:T(8,128)(2,1)S(1)}, u32[]{:S(2)}, u32[]{:S(2)}) async-start(bf16[8,384,256]{2,1,0:T(8,128)(2,1)} %broadcast_in_dim.39), calls=%async_computation.1 | async-start | bytes 3145728 | tf_op jit(solution)/shard_map/all_to_all | solution.py:205
  57.8 32.4 %copy-start = (bf16[1,3072,256]{2,1,0:T(8,128)(2,1)S(1)}, bf16[1,3072,256]{2,1,0:T(8,128)(2,1)}, u32[]{:S(2)}) copy-start(bf16[1,3072,256]{2,1,0:T(8,128)(2,1)} %param.6) | copy-start | bytes 4718596
  57.8 32.4 %copy-start.2 = (f32[6,256]{1,0:T(8,128)S(1)}, f32[6,256]{1,0:T(8,128)}, u32[]{:S(2)}) copy-start(f32[6,256]{1,0:T(8,128)} %diag_ref.3) | copy-start | bytes 18436
  67.4 14.2 %collective-permute-start = (bf16[2,32,256]{2,1,0:T(8,128)(2,1)S(1)}, bf16[2,32,256]{2,1,0:T(8,128)(2,1)S(1)}, u32[]{:S(2)}, u32[]{:S(2)}) collective-permute-start(bf16[2,32,256]{2,1,0:T(8,128)(2,1)S(1)} %convert_element_type.19), channel_id=1, source_target_pairs={{0,8},{8,0},{16,24},{24,16},{32,40},{40,32},{48,56},{56,48},{1,9},... | collective-permute-start | bytes 98312 | tf_op jit(solution)/shard_map/ppermute | solution.py:198
  119.6 3.9 %copy-start.5 = (s32[4,128]{1,0:T(4,128)S(1)}, s32[4,128]{1,0:T(4,128)}, u32[]{:S(2)}) copy-start(s32[4,128]{1,0:T(4,128)} %upper_maps_ref.1) | copy-start | bytes 6148
  119.6 34.4 %all-to-all-start.4 = ((bf16[16,12,16,256]{3,2,1,0:T(8,128)(2,1)}), bf16[16,12,16,256]{3,2,1,0:T(8,128)(2,1)S(1)}, u32[]{:S(2)}, u32[]{:S(2)}) async-start(bf16[16,12,16,256]{3,2,1,0:T(8,128)(2,1)} %shard_map.66), calls=%async_computation.4 | async-start | bytes 3145728 | tf_op jit(solution)/shard_map/all_to_all | solution.py:187
  155.7 19.7 %collective-permute-start.1 = (bf16[64,16,256]{2,1,0:T(8,128)(2,1)S(1)}, bf16[64,16,256]{2,1,0:T(8,128)(2,1)S(1)}, u32[]{:S(2)}, u32[]{:S(2)}) collective-permute-start(bf16[64,16,256]{2,1,0:T(8,128)(2,1)S(1)} %get-tuple-element.8), channel_id=1, source_target_pairs={{0,8},{8,0},{16,24},{24,16},{32,40},{40,32},{48,56},{56,48},{1,9},... | collective-permute-start | bytes 1572872 | tf_op jit(solution)/shard_map/ppermute | solution.py:198
  176.3 22.6 %all-to-all-start.5 = ((bf16[8,128,256]{2,1,0:T(8,128)(2,1)}), bf16[8,128,256]{2,1,0:T(8,128)(2,1)S(1)}, u32[]{:S(2)}, u32[]{:S(2)}) async-start(bf16[8,128,256]{2,1,0:T(8,128)(2,1)} %bitcast.9), calls=%async_computation.5 | async-start | bytes 1048576 | tf_op jit(solution)/shard_map/all_to_all | solution.py:203
  199.8 13.8 %all-to-all-start.6 = ((bf16[8,128,256]{2,1,0:T(8,128)(2,1)}), bf16[8,128,256]{2,1,0:T(8,128)(2,1)S(1)}, u32[]{:S(2)}, u32[]{:S(2)}) async-start(bf16[8,128,256]{2,1,0:T(8,128)(2,1)} %broadcast_in_dim.42), calls=%async_computation.6 | async-start | bytes 1048576 | tf_op jit(solution)/shard_map/all_to_all | solution.py:205
  213.6 43.0 %collective-permute-start.2 = (bf16[2,16,256]{2,1,0:T(8,128)(2,1)S(1)}, bf16[2,16,256]{2,1,0:T(8,128)(2,1)S(1)}, u32[]{:S(2)}, u32[]{:S(2)}) collective-permute-start(bf16[2,16,256]{2,1,0:T(8,128)(2,1)S(1)} %pad_maximum_fusion), channel_id=1, source_target_pairs={{0,8},{8,0},{16,24},{24,16},{32,40},{40,32},{48,56},{56,48},{1,9},... | collective-permute-start | bytes 49160 | tf_op jit(solution)/shard_map/ppermute | solution.py:198

commit v2 on v1

v2 whole, which is shorter than its diff:
```python
import functools

import jax
import jax.numpy as jnp
from jax import lax
from jax.experimental import pallas as pl
from jax.experimental.pallas import tpu as pltpu
from jax.sharding import PartitionSpec as P

TILE = 256
NPT = 128
STEP = 32
GROUP = 128
AHEAD = 3
HIGHEST = lax.Precision.HIGHEST
VMEM = pltpu.VMEM
SMEM = pltpu.SMEM
INTERPRET = False
F32 = jnp.float32
BF16 = jnp.bfloat16


def call(kernel, out_shape, in_spaces, out_space=None, scratch=(), flops=0, moved=0):
    return pl.pallas_call(
        kernel,
        out_shape=out_shape,
        in_specs=[pl.BlockSpec(memory_space=space) for space in in_spaces],
        out_specs=pl.BlockSpec(memory_space=out_space)
        if out_space is not None
        else [pl.BlockSpec(memory_space=VMEM) for _ in out_shape],
        scratch_shapes=list(scratch),
        compiler_params=pltpu.CompilerParams(vmem_limit_bytes=32 * 2**20),
        cost_estimate=pl.CostEstimate(flops=flops, bytes_accessed=moved, transcendentals=0),
        interpret=INTERPRET,
    )


def plan_kernel(meta_ref, tiles_ref, leaf_maps_ref, upper_maps_ref, place_ref):
    level, row = meta_ref[0], meta_ref[1]
    half = row % 2
    base = level // 4 * 4

    def one(index, carry):
        source, tile = index // 12, index % 12
        quad, across = source // 4, source % 4
        leaf = base + quad
        leaf_tile = (2 * across + half) * 12 + tile
        lower_tile = leaf_maps_ref[leaf, leaf_tile]
        upper_tile = upper_maps_ref[leaf // 2, lower_tile]
        kept = jnp.logical_and(leaf_tile < tiles_ref[leaf], lower_tile != 0)
        home_row = upper_tile // 4 % 8
        position = (upper_tile // 32 * 4 + home_row // 2) * 4 + upper_tile % 4
        other = (home_row % 2 != half).astype(jnp.int32)
        place_ref[index] = jnp.where(kept, position + 64 * other, 128)
        return carry

    lax.fori_loop(0, 192, one, 0)


def share_kernel(meta_ref, tiles_ref, leaf_maps_ref, leaf_ref, out_ref):
    level, row = meta_ref[0], meta_ref[1]
    tile = leaf_ref.shape[1]
    across, rows = out_ref.shape[0], out_ref.shape[2]
    out_ref[...] = jnp.zeros_like(out_ref)

    def look(index, carry):
        leaf_tile = row * 12 + index
        lower_tile = leaf_maps_ref[level, leaf_tile]
        match = jnp.logical_and(lower_tile % 16 == 0, leaf_tile < tiles_ref[level])

        @pl.when(match)
        def _():
            out_ref[:, lower_tile // 16] = leaf_ref[index].reshape(across, rows, tile)

        return carry

    lax.fori_loop(0, 12, look, 0)


def combine_kernel(meta_ref, slots_ref, shares_ref, out_ref, total_ref):
    front = meta_ref[0] // 2
    total = shares_ref[0].astype(F32)
    for source in range(1, shares_ref.shape[0]):
        total = total + shares_ref[source].astype(F32)
    total_ref[...] = total.astype(BF16)
    for column in range(8):
        out_ref[column, 0] = total_ref[0]
        out_ref[column, 1] = total_ref[slots_ref[front, column]]


def split(value):
    high = value.astype(BF16).astype(F32)
    return high, value - high


def dot3(left, right, dims):
    left_high, left_low = (part.astype(BF16) for part in split(left))
    right_high, right_low = (part.astype(BF16) for part in split(right))
    product = functools.partial(
        lax.dot_general, dimension_numbers=(dims, ((), ())), preferred_element_type=F32
    )
    return (product(left_low, right_high) + product(left_high, right_low)) + product(
        left_high, right_high
    )


def invert(work_ref):
    tile = work_ref.shape[0]
    group = min(GROUP, tile)
    groups = tile // group
    ids = lax.broadcasted_iota(jnp.int32, (STEP, group), 0)
    lanes = lax.broadcasted_iota(jnp.int32, (1, group), 1)
    for start in range(0, tile, STEP):
        own = start // group
        offset = start - own * group
        rows = slice(start, start + STEP)
        block = [work_ref[rows, k * group : (k + 1) * group] for k in range(groups)]

        def column(step):
            lane = offset + step
            return jnp.broadcast_to(block[own][:, lane : lane + 1], (STEP, group))

        ahead = [column(step) for step in range(AHEAD)]
        for step in range(STEP):
            if step + AHEAD < STEP:
                ahead.append(column(step + AHEAD))
            here = ahead.pop(0)
            inverse = 1.0 / here[step : step + 1]
            pivot_row = ids == step
            pivot_lane = lanes == offset + step
            for k in range(len(ahead)):
                scaled = ahead[k][step : step + 1] * inverse
                ahead[k] = jnp.where(pivot_row, scaled, ahead[k] - here * scaled)
            for k in range(groups):
                value = block[k]
                scaled = value[step : step + 1]
                if k == own:
                    scaled = jnp.where(pivot_lane, 1.0, scaled)
                    value = jnp.where(pivot_lane, 0.0, value)
                scaled = scaled * inverse
                block[k] = jnp.where(pivot_row, scaled, value - here * scaled)
        factor = work_ref[:, own * group : (own + 1) * group]
        fac_rows = lax.broadcasted_iota(jnp.int32, factor.shape, 0)
        fac_cols = lax.broadcasted_iota(jnp.int32, factor.shape, 1)
        own_row = jnp.logical_and(fac_rows >= start, fac_rows < start + STEP)
        own_col = jnp.logical_and(fac_cols >= offset, fac_cols < offset + STEP)
        work_ref[:, own * group : (own + 1) * group] = jnp.where(own_col, 0.0, factor)
        factor = jnp.where(jnp.logical_and(own_col, jnp.logical_not(own_row)), factor, 0.0)
        whole = jnp.concatenate(block, axis=1)
        if group >= 4 * STEP:
            high, low = split(factor)
            factor = high + pltpu.roll(high, STEP, 1) + pltpu.roll(low, 2 * STEP, 1)
            whole_high, whole_low = (part.astype(BF16) for part in split(whole))
            pieces = [jnp.zeros((STEP, tile), BF16) for _ in range(group // STEP)]
            place = offset // STEP
            for shift, part in enumerate((whole_high, whole_low, whole_high)):
                pieces[(place + shift) % len(pieces)] = part
            update = jnp.dot(
                factor.astype(BF16), jnp.concatenate(pieces, axis=0), preferred_element_type=F32
            )
        else:
            update = jnp.dot(
                factor[:, offset : offset + STEP], whole, precision=HIGHEST, preferred_element_type=F32
            )
        work_ref[...] = work_ref[...] - update
        work_ref[rows, :] = whole


def solve_kernel(front_of, meta_ref, diag_ref, gathered_ref, out_ref, work_ref):
    tile = out_ref.shape[0]
    pivot = gathered_ref[:, 0].reshape(tile, tile).astype(F32)
    chosen = gathered_ref[:, 1].reshape(tile, tile).astype(F32)
    rows = lax.broadcasted_iota(jnp.int32, (tile, tile), 0)
    columns = lax.broadcasted_iota(jnp.int32, (tile, tile), 1)
    diagonal = diag_ref[pl.ds(front_of(meta_ref[0]), 1), :]
    work_ref[...] = (pivot + pivot.T) * 0.5 + jnp.where(rows == columns, diagonal, 0.0)
    invert(work_ref)
    out_ref[...] = dot3(work_ref[...], chosen, ((1,), (1,))).astype(BF16)


def lower_front(level):
    return level // 2


def upper_front(level):
    return 4 + level // 4


def solve(front_of, meta, diagonals, gathered):
    tile = gathered.shape[-1]
    return call(
        functools.partial(solve_kernel, front_of),
        jax.ShapeDtypeStruct((tile, tile), BF16),
        [SMEM, VMEM, VMEM],
        VMEM,
        [pltpu.VMEM((tile, tile), F32)],
        flops=2**29,
        moved=2**22,
    )(meta, diagonals, gathered)


def pivot_slot_of(slots_ref, front):
    slot = jnp.int32(0)
    for index in range(8):
        slot = jnp.where(slots_ref[front, index] == 0, index, slot)
    return slot


def lower_kernel(
    meta_ref, slots_ref, place_ref, chunks_ref, pivot_ref, solved_ref, keep_ref, send_ref, share_ref, total_ref, update_ref
):
    level, row, col = meta_ref[0], meta_ref[1], meta_ref[2]
    total_ref[...] = jnp.zeros_like(total_ref)
    half = chunks_ref.shape[0] // 2
    for child in range(2):
        dropped = pivot_slot_of(slots_ref, level // 4 * 2 + child) == col
        pivot = pivot_ref[child * half : (child + 1) * half]
        update = jnp.dot(
            pivot.reshape(-1, pivot.shape[-1]), solved_ref[child], preferred_element_type=F32
        )
        update_ref[...] = update.reshape(update_ref.shape)

        def one(index, carry):
            place = jnp.where(dropped, 128, place_ref[child * half + index])
            value = chunks_ref[child * half + index].astype(F32) - update_ref[index]
            total_ref[place] = total_ref[place] + value
            return carry

        lax.fori_loop(0, half, one, 0, unroll=4)
    keep_ref[...] = total_ref[:64]
    send_ref[...] = total_ref[64:128].astype(BF16)
    first = row % 2 * 64
    for column in range(8):
        share_ref[column, 0] = total_ref[first].astype(BF16)
        share_ref[column, 1] = total_ref[first + 8 * slots_ref[4 + level // 4, column]].astype(BF16)


def upper_kernel(meta_ref, slots_ref, front_ref, pivot_ref, solved_ref, out_ref):
    level, row, col = meta_ref[0], meta_ref[1], meta_ref[2]
    tile = front_ref.shape[1]
    dropped = pivot_slot_of(slots_ref, 4 + level // 4) == col
    update = jnp.dot(pivot_ref[...], solved_ref[...], preferred_element_type=F32)
    result = jnp.where(dropped, 0.0, front_ref[...] - update)
    top = jnp.logical_and(
        lax.broadcasted_iota(jnp.int32, result.shape, 0) < tile // 16, row % 2 == 0
    )
    result = jnp.where(top, 0.0, result).astype(BF16)
    out_ref[...] = result.reshape(out_ref.shape)


def lane_groups(levels):
    groups = []
    for first in range(0, 8, levels):
        for half in range(2):
            groups.append(
                [
                    (first + level) * 8 + 2 * across + half
                    for level in range(levels)
                    for across in range(4)
                ]
            )
    return groups


def exchange(value, levels):
    return lax.all_to_all(
        value,
        ("level", "row"),
        split_axis=0,
        concat_axis=0,
        axis_index_groups=lane_groups(levels),
        tiled=True,
    )


def crossed(value):
    return lax.ppermute(value, "row", [(row, row ^ 1) for row in range(8)])


def over_columns(value):
    return lax.all_to_all(value, "col", split_axis=0, concat_axis=0, tiled=True)


def spread_columns(value, slot):
    pieces = over_columns(value.reshape(8, -1, value.shape[-1]))
    piece = lax.dynamic_index_in_dim(pieces, slot, 0, keepdims=True)
    return over_columns(jnp.broadcast_to(piece, pieces.shape)).reshape(value.shape)


def gather_tiles(shares, slot, levels):
    parts = lax.dynamic_index_in_dim(over_columns(shares), slot, 0, keepdims=False)
    parts = (parts.astype(F32) + crossed(parts).astype(F32)).astype(BF16)
    return exchange(jnp.broadcast_to(parts[None], (4 * levels,) + parts.shape), levels)


def body(leaf_blocks, leaf_tiles, leaf_maps, upper_maps, front_slots, pivot_diag):
    tile = leaf_blocks.shape[2]
    level = lax.axis_index("level")
    row = lax.axis_index("row")
    col = lax.axis_index("col")
    meta = jnp.stack([level, row, col]).astype(jnp.int32)
    positions = jnp.arange(8, dtype=jnp.int32)
    slots = jnp.sum(jnp.where(front_slots == 0, positions[None, :], 0), axis=1)

    def slot_of(front):
        return lax.dynamic_index_in_dim(slots, front, keepdims=False)

    eighth, sixteenth = tile // 8, tile // 16
    own = leaf_blocks.reshape(12, tile, tile)

    shares = call(
        share_kernel,
        jax.ShapeDtypeStruct((8, 8, eighth, tile), BF16),
        [SMEM] * 3 + [VMEM],
        VMEM,
        moved=2**21,
    )(meta, leaf_tiles, leaf_maps, own)
    shares = exchange(shares, 2)
    chunks = jnp.swapaxes(own.reshape(12, 16, sixteenth, tile), 0, 1)
    chunks = exchange(chunks, 4).reshape(192, sixteenth, tile)
    place = call(
        plan_kernel,
        jax.ShapeDtypeStruct((192,), jnp.int32),
        [SMEM] * 4,
        SMEM,
    )(meta, leaf_tiles, leaf_maps, upper_maps)
    shares = call(
        combine_kernel,
        jax.ShapeDtypeStruct((8, 2, eighth, tile), BF16),
        [SMEM, SMEM, VMEM],
        VMEM,
        [pltpu.VMEM((8, eighth, tile), BF16)],
        moved=2**21,
    )(meta, front_slots, shares)
    gathered = gather_tiles(shares, slot_of(level // 2), 2)
    pivot_columns = spread_columns(chunks, slot_of(level // 4 * 2 + col // 4))
    solved = solve(lower_front, meta, pivot_diag, gathered)
    other = lax.ppermute(solved, "level", [(index, index ^ 2) for index in range(8)])
    first_child = level // 2 % 2 == 0
    solved = jnp.where(first_child, jnp.stack([solved, other]), jnp.stack([other, solved]))
    keep, send, shares = call(
        lower_kernel,
        (
            jax.ShapeDtypeStruct((64, sixteenth, tile), F32),
            jax.ShapeDtypeStruct((64, sixteenth, tile), BF16),
            jax.ShapeDtypeStruct((8, 2, sixteenth, tile), BF16),
        ),
        [SMEM, SMEM, SMEM, VMEM, VMEM, VMEM],
        None,
        [pltpu.VMEM((129, sixteenth, tile), F32), pltpu.VMEM((96, sixteenth, tile), F32)],
        flops=2**29,
        moved=2**23,
    )(meta, front_slots, place, chunks, pivot_columns, solved)

    upper_slot = slot_of(4 + level // 4)
    gathered = gather_tiles(shares, upper_slot, 4)
    front = keep + crossed(send).astype(F32)
    pivot_columns = spread_columns(front.astype(BF16), upper_slot)
    solved = solve(upper_front, meta, pivot_diag, gathered)
    finished = call(
        upper_kernel,
        jax.ShapeDtypeStruct((16, 4, sixteenth, tile), BF16),
        [SMEM, SMEM, VMEM, VMEM, VMEM],
        VMEM,
        flops=2**28,
        moved=2**22,
    )(meta, front_slots, front.reshape(-1, tile), pivot_columns.reshape(-1, tile), solved)
    result = exchange(finished, 4)
    return jnp.swapaxes(result, 0, 1).reshape(1, -1, tile)


def solution(mesh):
    return jax.shard_map(
        body,
        mesh=mesh,
        in_specs=(P("level", "row", "col"), P(), P(), P(), P(), P()),
        out_specs=P("level", "row", "col"),
        check_vma=False,
    )
```

time: 325 us -> 284 us (0.87)
  waiting for transfers between devices: 83.8 us -> 37.6 us
  Pallas kernels: 69.8 us -> 37.8 us
  blocking collectives: 54.9 us -> 75.8 us
  starting transfers between devices: 103 us -> 115 us
  local copies, waits for them, and re-layouts: 4.21 us -> 8.02 us
    all_to_all x4 -> x6, waiting for transfers between devices: 55 us -> 10.2 us  [over_columns(): return lax.all_to_all(value, 'col', split_axis=0, concat_axis=0, tiled=True)]
    pallas_call x1, Pallas kernels: 26.3 us -> 0.9 us  [body(): call(upper_kernel, jax.ShapeDtypeStruct((16, 4, sixteenth, tile), BF16),...]
    all_to_all x4 -> x3, blocking collectives: 54.9 us -> 75.8 us  [exchange(): lax.all_to_all(value, ('level', 'row'), split_axis=0, concat_axis=0, axis...]
    all_to_all x4 -> x6, starting transfers between devices: 32.4 us -> 39.1 us  [over_columns(): return lax.all_to_all(value, 'col', split_axis=0, concat_axis=0, tiled=True)]
    pallas_call x3 -> x5, Pallas kernels: 32.1 us -> 25.6 us  [the longest x2 18.5 us: solve(): call(functools.partial(solve_kernel, front_of), jax.ShapeDtypeStruct((til...]
    all_to_all x1 -> x2, waiting for transfers between devices: 19.2 us -> 13.2 us  [exchange(): lax.all_to_all(value, ('level', 'row'), split_axis=0, concat_axis=0, axis...]
    ppermute x3, waiting for transfers between devices: 9.55 us -> 14.2 us  [crossed(): return lax.ppermute(value, 'row', [(row, row ^ 1) for row in range(8)])]
    all_to_all x1 -> x2, starting transfers between devices: 3.84 us -> 7.09 us  [exchange(): lax.all_to_all(value, ('level', 'row'), split_axis=0, concat_axis=0, axis...]
  transfers between devices with their start and end apart: 8 -> 12, of which waited for: 8 -> 8; matrix products, arithmetic and copies ran while one was open for 0% -> 1% of each run, Pallas kernels for 4% -> 11%
where the time goes in v2:
time: 284 us; the launch traced here: 281 us
  starting transfers between devices  115 us (40%)
  blocking collectives  75.8 us (27%)
  Pallas kernels  37.8 us (13%)
  waiting for transfers between devices  37.6 us (13%)
  local copies, waits for them, and re-layouts  8.02 us (3%)
  between operations  5.99 us (2%)
    all_to_all x3, blocking collectives, exchange(): lax.all_to_all(value, ('level', 'row'), split_axis=0, concat_axis=0, axis...  75.8 us
    ppermute x3, starting transfers between devices, crossed(): return lax.ppermute(value, 'row', [(row, row ^ 1) for row in range(8)])  65.6 us
    all_to_all x6, starting transfers between devices, over_columns(): return lax.all_to_all(value, 'col', split_axis=0, concat_axis=0, tiled=True)  39.1 us
    pallas_call x2, Pallas kernels, solve(): call(functools.partial(solve_kernel, front_of), jax.ShapeDtypeStruct((til...  18.5 us
    ppermute x3, waiting for transfers between devices, crossed(): return lax.ppermute(value, 'row', [(row, row ^ 1) for row in range(8)])  14.2 us
    all_to_all x2, waiting for transfers between devices, exchange(): lax.all_to_all(value, ('level', 'row'), split_axis=0, concat_axis=0, axis...  13.2 us
    pallas_call x1, Pallas kernels, body(): call(plan_kernel, jax.ShapeDtypeStruct((192,), jnp.int32), [SMEM] * 4, SMEM)  11.4 us
    all_to_all x6, waiting for transfers between devices, over_columns(): return lax.all_to_all(value, 'col', split_axis=0, concat_axis=0, tiled=True)  10.2 us
  transfers between devices with their start and end apart: 12, of which 8 were waited for; matrix products, arithmetic and copies ran while one was open for 1% of the time, Pallas kernels for 11%

profile of v2, /device:TPU:1, one launch (start us, length us, event | category | flops | bytes accessed | tf_op | source)
XLA Modules:
  0.0 281.4 jit_solution(7833896837379763228)
XLA Ops:
  3.8 17.7 %all_to_all.55.shares_ref = bf16[8,8,32,256]{3,2,1,0:T(8,128)(2,1)S(1)} all-to-all(bf16[8,8,32,256]{3,2,1,0:T(8,128)(2,1)S(1)} %shard_map.65), channel_id=1, replica_groups={{0,16,32,48,64,80,96,112},{8,24,40,56,72,88,104,120},{128,144,160,176,1..., dimensions={0} | all-to-all | bytes 2097152 | tf_op jit(solution)/shard_map/all_to_all | solution.py:266
  23.0 9.7 %all-to-all-start.4 = ((bf16[8,2,32,256]{3,2,1,0:T(8,128)(2,1)}), bf16[8,2,32,256]{3,2,1,0:T(8,128)(2,1)S(1)}, u32[]{:S(2)}, u32[]{:S(2)}) async-start(bf16[8,2,32,256]{3,2,1,0:T(8,128)(2,1)} %shard_map.66), calls=%async_computation.4 | async-start | bytes 524288 | tf_op jit(solution)/shard_map/all_to_all | solution.py:281
  32.8 6.3 %all-to-all-done.4 = bf16[8,2,32,256]{3,2,1,0:T(8,128)(2,1)S(1)} async-done(((bf16[8,2,32,256]{3,2,1,0:T(8,128)(2,1)}), bf16[8,2,32,256]{3,2,1,0:T(8,128)(2,1)S(1)}, u32[]{:S(2)}, u32[]{:S(2)}) %all-to-all-start.4) | async-done | bytes 262176 | tf_op jit(solution)/shard_map/all_to_all | solution.py:281
  39.2 41.1 %all_to_all.56 = bf16[16,12,16,256]{3,2,1,0:T(8,128)(2,1)} all-to-all(bf16[16,12,16,256]{3,2,1,0:T(8,128)(2,1)S(1)} %bitcast.39), channel_id=1, replica_groups={{0,16,32,48,64,80,96,112,128,144,160,176,192,208,224,240},{8,24,40,56,7..., dimensions={0} | all-to-all | bytes 3145728 | tf_op jit(solution)/shard_map/all_to_all | solution.py:266
  80.3 6.3 %all-to-all-start.1 = ((bf16[8,384,256]{2,1,0:T(8,128)(2,1)}), bf16[8,384,256]{2,1,0:T(8,128)(2,1)S(1)}, u32[]{:S(2)}, u32[]{:S(2)}) async-start(bf16[8,384,256]{2,1,0:T(8,128)(2,1)} %bitcast.6), calls=%async_computation.1 | async-start | bytes 3145728 | tf_op jit(solution)/shard_map/all_to_all | solution.py:281
  89.4 12.7 %collective-permute-start = (bf16[2,32,256]{2,1,0:T(8,128)(2,1)S(1)}, bf16[2,32,256]{2,1,0:T(8,128)(2,1)S(1)}, u32[]{:S(2)}, u32[]{:S(2)}) collective-permute-start(bf16[2,32,256]{2,1,0:T(8,128)(2,1)S(1)} %dynamic-slice_bitcast_fusion.2), channel_id=1, source_target_pairs={{0,8},{8,0},{16,24},{24,16},{32,40},{40,32},{48,56},{56,48},{1,9},... | collective-permute-start | bytes 98312 | tf_op jit(solution)/shard_map/ppermute | solution.py:277
  103.7 3.6 %all-to-all-done.1 = bf16[8,384,256]{2,1,0:T(8,128)(2,1)S(1)} async-done(((bf16[8,384,256]{2,1,0:T(8,128)(2,1)}), bf16[8,384,256]{2,1,0:T(8,128)(2,1)S(1)}, u32[]{:S(2)}, u32[]{:S(2)}) %all-to-all-start.1) | async-done | bytes 1572896 | tf_op jit(solution)/shard_map/all_to_all | solution.py:281
  108.1 3.5 %all-to-all-start.5 = ((bf16[8,2,32,256]{3,2,1,0:T(8,128)(2,1)}), bf16[8,2,32,256]{3,2,1,0:T(8,128)(2,1)S(1)}, u32[]{:S(2)}, u32[]{:S(2)}) async-start(bf16[8,2,32,256]{3,2,1,0:T(8,128)(2,1)} %broadcast_in_dim.40), calls=%async_computation.5 | async-start | bytes 524288 | tf_op jit(solution)/shard_map/all_to_all | solution.py:266
  113.7 4.0 %all-to-all-done.5.gathered_ref = bf16[8,2,32,256]{3,2,1,0:T(8,128)(2,1)S(1)} async-done(((bf16[8,2,32,256]{3,2,1,0:T(8,128)(2,1)}), bf16[8,2,32,256]{3,2,1,0:T(8,128)(2,1)S(1)}, u32[]{:S(2)}, u32[]{:S(2)}) %all-to-all-start.5) | async-done | bytes 262176 | tf_op jit(solution)/shard_map/all_to_all | solution.py:266
  118.9 5.9 %all-to-all-start.2 = ((bf16[8,384,256]{2,1,0:T(8,128)(2,1)}), bf16[8,384,256]{2,1,0:T(8,128)(2,1)S(1)}, u32[]{:S(2)}, u32[]{:S(2)}) async-start(bf16[8,384,256]{2,1,0:T(8,128)(2,1)} %broadcast_in_dim.39), calls=%async_computation.2 | async-start | bytes 3145728 | tf_op jit(solution)/shard_map/all_to_all | solution.py:281
  124.8 9.3 %shard_map.67 = bf16[256,256]{1,0:T(8,128)(2,1)S(1)} custom-call(s32[3]{0:T(128)S(1)} %pad_add_fusion.meta_ref, f32[6,256]{1,0:T(8,128)S(1)} %copy-done.8, bf16[8,2,32,256]{3,2,1,0:T(8,128)(2,1)S(1)} %all-to-all-done.5.gathered_ref), custom_call_target="tpu_custom_call" | custom-call | flops 536870912 | bytes 4194304 | tf_op jit(solution)/shard_map/pallas_call | solution.py:191
  134.1 3.2 %collective-permute-start.1 = (bf16[256,256]{1,0:T(8,128)(2,1)S(1)}, bf16[256,256]{1,0:T(8,128)(2,1)S(1)}, u32[]{:S(2)}, u32[]{:S(2)}) collective-permute-start(bf16[256,256]{1,0:T(8,128)(2,1)S(1)} %shard_map.67), channel_id=1, source_target_pairs={{0,128},{64,192},{128,0},{192,64},{256,384},{320,448},{384,256},{4... | collective-permute-start | bytes 393224 | tf_op jit(solution)/shard_map/ppermute | solution.py:338
  137.4 11.4 %shard_map.64.place_ref = s32[192]{0:T(256)S(1)} custom-call(s32[3]{0:T(128)S(1)} %pad_add_fusion.meta_ref, s32[8]{0:T(128)S(1)} %copy-done.6, s32[8,96]{1,0:T(8,128)S(1)} %copy-done.4, s32[4,128]{1,0:T(4,128)S(1)} %copy-done.7), custom_call_target="tpu_custom_call" | custom-call | tf_op jit(solution)/shard_map/pallas_call | solution.py:321
  148.8 4.6 %shard_map.68 = (f32[64,16,256]{2,1,0:T(8,128)S(1)}, bf16[64,16,256]{2,1,0:T(8,128)(2,1)S(1)}, bf16[8,2,16,256]{3,2,1,0:T(8,128)(2,1)}) custom-call(s32[3]{0:T(128)S(1)} %pad_add_fusion.meta_ref, s32[6,8]{1,0:T(8,128)S(1)} %copy-done.2, s32[192]{0:T(256)S(1)} %shard_map.64.place_ref, bf16[192,16,256]{2,1,0:T(8,128)(2,1)} %bitcast.5.chunks_ref, ...), custom_call_target="tpu_custom_call" | custom-call | flops 536870912 | bytes 8388608 | tf_op jit(solution)/shard_map/pallas_call | solution.py:341
  153.4 12.7 %collective-permute-start.2 = (bf16[64,16,256]{2,1,0:T(8,128)(2,1)S(1)}, bf16[64,16,256]{2,1,0:T(8,128)(2,1)S(1)}, u32[]{:S(2)}, u32[]{:S(2)}) collective-permute-start(bf16[64,16,256]{2,1,0:T(8,128)(2,1)S(1)} %get-tuple-element.9), channel_id=1, source_target_pairs={{0,8},{8,0},{16,24},{24,16},{32,40},{40,32},{48,56},{56,48},{1,9},... | collective-permute-start | bytes 1572872 | tf_op jit(solution)/shard_map/ppermute | solution.py:277
  166.1 5.2 %all-to-all-start.8 = ((bf16[8,2,16,256]{3,2,1,0:T(8,128)(2,1)}), bf16[8,2,16,256]{3,2,1,0:T(8,128)(2,1)S(1)}, u32[]{:S(2)}, u32[]{:S(2)}) async-start(bf16[8,2,16,256]{3,2,1,0:T(8,128)(2,1)} %get-tuple-element.10), calls=%async_computation.8 | async-start | bytes 262144 | tf_op jit(solution)/shard_map/all_to_all | solution.py:281
  171.4 11.5 %collective-permute-done.2 = bf16[64,16,256]{2,1,0:T(8,128)(2,1)S(1)} collective-permute-done((bf16[64,16,256]{2,1,0:T(8,128)(2,1)S(1)}, bf16[64,16,256]{2,1,0:T(8,128)(2,1)S(1)}, u32[]{:S(2)}, u32[]{:S(2)}) %collective-permute-start.2) | collective-permute-done | bytes 524320 | tf_op jit(solution)/shard_map/ppermute | solution.py:277
  183.8 5.2 %all-to-all-start.6 = ((bf16[8,128,256]{2,1,0:T(8,128)(2,1)}), bf16[8,128,256]{2,1,0:T(8,128)(2,1)S(1)}, u32[]{:S(2)}, u32[]{:S(2)}) async-start(bf16[8,128,256]{2,1,0:T(8,128)(2,1)} %bitcast.16), calls=%async_computation.6 | async-start | bytes 1048576 | tf_op jit(solution)/shard_map/all_to_all | solution.py:281
  190.7 40.1 %collective-permute-start.3 = (bf16[2,16,256]{2,1,0:T(8,128)(2,1)S(1)}, bf16[2,16,256]{2,1,0:T(8,128)(2,1)S(1)}, u32[]{:S(2)}, u32[]{:S(2)}) collective-permute-start(bf16[2,16,256]{2,1,0:T(8,128)(2,1)S(1)} %dynamic-slice_bitcast_fusion.3), channel_id=1, source_target_pairs={{0,8},{8,0},{16,24},{24,16},{32,40},{40,32},{48,56},{56,48},{1,9},... | collective-permute-start | bytes 49160 | tf_op jit(solution)/shard_map/ppermute | solution.py:277
  232.7 3.6 %all-to-all-start.9 = ((bf16[16,2,16,256]{3,2,1,0:T(8,128)(2,1)}), bf16[16,2,16,256]{3,2,1,0:T(8,128)(2,1)S(1)}, u32[]{:S(2)}, u32[]{:S(2)}) async-start(bf16[16,2,16,256]{3,2,1,0:T(8,128)(2,1)} %broadcast_in_dim.43), calls=%async_computation.9 | async-start | bytes 524288 | tf_op jit(solution)/shard_map/all_to_all | solution.py:266
  236.3 9.2 %all-to-all-done.9.gathered_ref = bf16[16,2,16,256]{3,2,1,0:T(8,128)(2,1)S(1)} async-done(((bf16[16,2,16,256]{3,2,1,0:T(8,128)(2,1)}), bf16[16,2,16,256]{3,2,1,0:T(8,128)(2,1)S(1)}, u32[]{:S(2)}, u32[]{:S(2)}) %all-to-all-start.9) | async-done | bytes 262176 | tf_op jit(solution)/shard_map/all_to_all | solution.py:266
  246.4 6.9 %all-to-all-start.7 = ((bf16[8,128,256]{2,1,0:T(8,128)(2,1)}), bf16[8,128,256]{2,1,0:T(8,128)(2,1)S(1)}, u32[]{:S(2)}, u32[]{:S(2)}) async-start(bf16[8,128,256]{2,1,0:T(8,128)(2,1)} %broadcast_in_dim.42), calls=%async_computation.7 | async-start | bytes 1048576 | tf_op jit(solution)/shard_map/all_to_all | solution.py:281
  253.3 9.3 %shard_map.69.solved_ref = bf16[256,256]{1,0:T(8,128)(2,1)S(1)} custom-call(s32[3]{0:T(128)S(1)} %pad_add_fusion.meta_ref, f32[6,256]{1,0:T(8,128)S(1)} %copy-done.8, bf16[16,2,16,256]{3,2,1,0:T(8,128)(2,1)S(1)} %all-to-all-done.9.gathered_ref), custom_call_target="tpu_custom_call" | custom-call | flops 536870912 | bytes 4194304 | tf_op jit(solution)/shard_map/pallas_call | solution.py:191
  263.7 16.9 %all_to_all.57 = bf16[16,4,16,256]{3,2,1,0:T(8,128)(2,1)S(1)} all-to-all(bf16[16,4,16,256]{3,2,1,0:T(8,128)(2,1)S(1)} %shard_map.70), channel_id=1, replica_groups={{0,16,32,48,64,80,96,112,128,144,160,176,192,208,224,240},{8,24,40,56,7..., dimensions={0} | all-to-all | bytes 1048576 | tf_op jit(solution)/shard_map/all_to_all | solution.py:266
  (45 shorter events, 15.5 us)
Async XLA Ops:
  0.1 1.4 copy-start
  1.5 0.7 copy-start.3
  2.2 0.7 copy-start.5
  3.8 17.7 %copy-start.2 = (s32[6,8]{1,0:T(8,128)S(1)}, s32[6,8]{1,0:T(8,128)}, u32[]{:S(2)}) copy-start(s32[6,8]{1,0:T(8,128)} %slots_ref.5) | copy-start | bytes 580
  3.8 28.9 %copy-start.1 = (bf16[1,3072,256]{2,1,0:T(8,128)(2,1)S(1)}, bf16[1,3072,256]{2,1,0:T(8,128)(2,1)}, u32[]{:S(2)}) copy-start(bf16[1,3072,256]{2,1,0:T(8,128)(2,1)} %param.6) | copy-start | bytes 4718596
  23.0 16.2 %all-to-all-start.4 = ((bf16[8,2,32,256]{3,2,1,0:T(8,128)(2,1)}), bf16[8,2,32,256]{3,2,1,0:T(8,128)(2,1)S(1)}, u32[]{:S(2)}, u32[]{:S(2)}) async-start(bf16[8,2,32,256]{3,2,1,0:T(8,128)(2,1)} %shard_map.66), calls=%async_computation.4 | async-start | bytes 524288 | tf_op jit(solution)/shard_map/all_to_all | solution.py:281
  80.3 27.0 %all-to-all-start.1 = ((bf16[8,384,256]{2,1,0:T(8,128)(2,1)}), bf16[8,384,256]{2,1,0:T(8,128)(2,1)S(1)}, u32[]{:S(2)}, u32[]{:S(2)}) async-start(bf16[8,384,256]{2,1,0:T(8,128)(2,1)} %bitcast.6), calls=%async_computation.1 | async-start | bytes 3145728 | tf_op jit(solution)/shard_map/all_to_all | solution.py:281
  89.4 14.3 %collective-permute-start = (bf16[2,32,256]{2,1,0:T(8,128)(2,1)S(1)}, bf16[2,32,256]{2,1,0:T(8,128)(2,1)S(1)}, u32[]{:S(2)}, u32[]{:S(2)}) collective-permute-start(bf16[2,32,256]{2,1,0:T(8,128)(2,1)S(1)} %dynamic-slice_bitcast_fusion.2), channel_id=1, source_target_pairs={{0,8},{8,0},{16,24},{24,16},{32,40},{40,32},{48,56},{56,48},{1,9},... | collective-permute-start | bytes 98312 | tf_op jit(solution)/shard_map/ppermute | solution.py:277
  108.1 9.6 %all-to-all-start.5 = ((bf16[8,2,32,256]{3,2,1,0:T(8,128)(2,1)}), bf16[8,2,32,256]{3,2,1,0:T(8,128)(2,1)S(1)}, u32[]{:S(2)}, u32[]{:S(2)}) async-start(bf16[8,2,32,256]{3,2,1,0:T(8,128)(2,1)} %broadcast_in_dim.40), calls=%async_computation.5 | async-start | bytes 524288 | tf_op jit(solution)/shard_map/all_to_all | solution.py:266
  118.9 5.9 %copy-start.8 = (f32[6,256]{1,0:T(8,128)S(1)}, f32[6,256]{1,0:T(8,128)}, u32[]{:S(2)}) copy-start(f32[6,256]{1,0:T(8,128)} %diag_ref.3) | copy-start | bytes 18436
  118.9 29.9 %all-to-all-start.2 = ((bf16[8,384,256]{2,1,0:T(8,128)(2,1)}), bf16[8,384,256]{2,1,0:T(8,128)(2,1)S(1)}, u32[]{:S(2)}, u32[]{:S(2)}) async-start(bf16[8,384,256]{2,1,0:T(8,128)(2,1)} %broadcast_in_dim.39), calls=%async_computation.2 | async-start | bytes 3145728 | tf_op jit(solution)/shard_map/all_to_all | solution.py:281
  124.8 12.5 %copy-start.4 = (s32[8,96]{1,0:T(8,128)S(1)}, s32[8,96]{1,0:T(8,128)}, u32[]{:S(2)}) copy-start(s32[8,96]{1,0:T(8,128)} %leaf_maps_ref.3) | copy-start | bytes 9220
  124.8 12.5 %copy-start.6 = (s32[8]{0:T(128)S(1)}, s32[8]{0:T(128)}, u32[]{:S(2)}) copy-start(s32[8]{0:T(128)} %tiles_ref.3) | copy-start | bytes 100
  124.8 12.6 %copy-start.7 = (s32[4,128]{1,0:T(4,128)S(1)}, s32[4,128]{1,0:T(4,128)}, u32[]{:S(2)}) copy-start(s32[4,128]{1,0:T(4,128)} %upper_maps_ref.1) | copy-start | bytes 6148
  134.1 14.6 %collective-permute-start.1 = (bf16[256,256]{1,0:T(8,128)(2,1)S(1)}, bf16[256,256]{1,0:T(8,128)(2,1)S(1)}, u32[]{:S(2)}, u32[]{:S(2)}) collective-permute-start(bf16[256,256]{1,0:T(8,128)(2,1)S(1)} %shard_map.67), channel_id=1, source_target_pairs={{0,128},{64,192},{128,0},{192,64},{256,384},{320,448},{384,256},{4... | collective-permute-start | bytes 393224 | tf_op jit(solution)/shard_map/ppermute | solution.py:338
  153.4 29.5 %collective-permute-start.2 = (bf16[64,16,256]{2,1,0:T(8,128)(2,1)S(1)}, bf16[64,16,256]{2,1,0:T(8,128)(2,1)S(1)}, u32[]{:S(2)}, u32[]{:S(2)}) collective-permute-start(bf16[64,16,256]{2,1,0:T(8,128)(2,1)S(1)} %get-tuple-element.9), channel_id=1, source_target_pairs={{0,8},{8,0},{16,24},{24,16},{32,40},{40,32},{48,56},{56,48},{1,9},... | collective-permute-start | bytes 1572872 | tf_op jit(solution)/shard_map/ppermute | solution.py:277
  166.1 17.7 %all-to-all-start.8 = ((bf16[8,2,16,256]{3,2,1,0:T(8,128)(2,1)}), bf16[8,2,16,256]{3,2,1,0:T(8,128)(2,1)S(1)}, u32[]{:S(2)}, u32[]{:S(2)}) async-start(bf16[8,2,16,256]{3,2,1,0:T(8,128)(2,1)} %get-tuple-element.10), calls=%async_computation.8 | async-start | bytes 262144 | tf_op jit(solution)/shard_map/all_to_all | solution.py:281
  183.8 48.2 %all-to-all-start.6 = ((bf16[8,128,256]{2,1,0:T(8,128)(2,1)}), bf16[8,128,256]{2,1,0:T(8,128)(2,1)S(1)}, u32[]{:S(2)}, u32[]{:S(2)}) async-start(bf16[8,128,256]{2,1,0:T(8,128)(2,1)} %bitcast.16), calls=%async_computation.6 | async-start | bytes 1048576 | tf_op jit(solution)/shard_map/all_to_all | solution.py:281
  190.7 41.2 %collective-permute-start.3 = (bf16[2,16,256]{2,1,0:T(8,128)(2,1)S(1)}, bf16[2,16,256]{2,1,0:T(8,128)(2,1)S(1)}, u32[]{:S(2)}, u32[]{:S(2)}) collective-permute-start(bf16[2,16,256]{2,1,0:T(8,128)(2,1)S(1)} %dynamic-slice_bitcast_fusion.3), channel_id=1, source_target_pairs={{0,8},{8,0},{16,24},{24,16},{32,40},{40,32},{48,56},{56,48},{1,9},... | collective-permute-start | bytes 49160 | tf_op jit(solution)/shard_map/ppermute | solution.py:277
  232.7 12.8 %all-to-all-start.9 = ((bf16[16,2,16,256]{3,2,1,0:T(8,128)(2,1)}), bf16[16,2,16,256]{3,2,1,0:T(8,128)(2,1)S(1)}, u32[]{:S(2)}, u32[]{:S(2)}) async-start(bf16[16,2,16,256]{3,2,1,0:T(8,128)(2,1)} %broadcast_in_dim.43), calls=%async_computation.9 | async-start | bytes 524288 | tf_op jit(solution)/shard_map/all_to_all | solution.py:266
  246.4 16.3 %all-to-all-start.7 = ((bf16[8,128,256]{2,1,0:T(8,128)(2,1)}), bf16[8,128,256]{2,1,0:T(8,128)(2,1)S(1)}, u32[]{:S(2)}, u32[]{:S(2)}) async-start(bf16[8,128,256]{2,1,0:T(8,128)(2,1)} %broadcast_in_dim.42), calls=%async_computation.7 | async-start | bytes 1048576 | tf_op jit(solution)/shard_map/all_to_all | solution.py:281

commit v3 on v2

--- a/solution.py
+++ b/solution.py
@@ -36,25 +36,21 @@
 
 
 def plan_kernel(meta_ref, tiles_ref, leaf_maps_ref, upper_maps_ref, place_ref):
-    level, row = meta_ref[0], meta_ref[1]
-    half = row % 2
-    base = level // 4 * 4
-
-    def one(index, carry):
-        source, tile = index // 12, index % 12
-        quad, across = source // 4, source % 4
-        leaf = base + quad
-        leaf_tile = (2 * across + half) * 12 + tile
-        lower_tile = leaf_maps_ref[leaf, leaf_tile]
-        upper_tile = upper_maps_ref[leaf // 2, lower_tile]
-        kept = jnp.logical_and(leaf_tile < tiles_ref[leaf], lower_tile != 0)
-        home_row = upper_tile // 4 % 8
-        position = (upper_tile // 32 * 4 + home_row // 2) * 4 + upper_tile % 4
-        other = (home_row % 2 != half).astype(jnp.int32)
-        place_ref[index] = jnp.where(kept, position + 64 * other, 128)
-        return carry
-
-    lax.fori_loop(0, 192, one, 0)
+    half = meta_ref[1] & 1
+    base = meta_ref[0] & 4
+    for source in range(16):
+        leaf = base + source // 4
+        front = (base >> 1) + source // 8
+        live = tiles_ref[leaf]
+        first = (2 * (source % 4) + half) * 12
+        for tile in range(12):
+            lower_tile = leaf_maps_ref[leaf, first + tile]
+            upper_tile = upper_maps_ref[front, lower_tile]
+            home_row = (upper_tile >> 2) & 7
+            position = ((upper_tile >> 5) << 4) + ((home_row >> 1) << 2) + (upper_tile & 3)
+            position = position + (((home_row & 1) ^ half) << 6)
+            kept = jnp.logical_and(first + tile < live, lower_tile != 0)
+            place_ref[source * 12 + tile] = jnp.where(kept, position, 128)
 
 
 def share_kernel(meta_ref, tiles_ref, leaf_maps_ref, leaf_ref, out_ref):
@@ -77,15 +73,11 @@
     lax.fori_loop(0, 12, look, 0)
 
 
-def combine_kernel(meta_ref, slots_ref, shares_ref, out_ref, total_ref):
-    front = meta_ref[0] // 2
+def combine_kernel(shares_ref, out_ref):
     total = shares_ref[0].astype(F32)
     for source in range(1, shares_ref.shape[0]):
         total = total + shares_ref[source].astype(F32)
-    total_ref[...] = total.astype(BF16)
-    for column in range(8):
-        out_ref[column, 0] = total_ref[0]
-        out_ref[column, 1] = total_ref[slots_ref[front, column]]
+    out_ref[...] = total.astype(BF16)
 
 
 def split(value):
@@ -166,16 +158,21 @@
         work_ref[rows, :] = whole
 
 
-def solve_kernel(front_of, meta_ref, diag_ref, gathered_ref, out_ref, work_ref):
+def solve_kernel(front_of, place_of, meta_ref, diag_ref, gathered_ref, out_ref, work_ref, chosen_ref):
     tile = out_ref.shape[0]
-    pivot = gathered_ref[:, 0].reshape(tile, tile).astype(F32)
-    chosen = gathered_ref[:, 1].reshape(tile, tile).astype(F32)
+    count, length = gathered_ref.shape[0], gathered_ref.shape[2]
+    place = place_of(meta_ref)
+    for piece in range(count):
+        rows = pl.ds(pl.multiple_of((place ^ piece) * length, length), length)
+        work_ref[rows, :] = gathered_ref[piece, 0].astype(F32)
+        chosen_ref[rows, :] = gathered_ref[piece, 1].astype(F32)
+    pivot = work_ref[...]
     rows = lax.broadcasted_iota(jnp.int32, (tile, tile), 0)
     columns = lax.broadcasted_iota(jnp.int32, (tile, tile), 1)
     diagonal = diag_ref[pl.ds(front_of(meta_ref[0]), 1), :]
     work_ref[...] = (pivot + pivot.T) * 0.5 + jnp.where(rows == columns, diagonal, 0.0)
     invert(work_ref)
-    out_ref[...] = dot3(work_ref[...], chosen, ((1,), (1,))).astype(BF16)
+    out_ref[...] = dot3(work_ref[...], chosen_ref[...], ((1,), (1,))).astype(BF16)
 
 
 def lower_front(level):
@@ -186,14 +183,22 @@
     return 4 + level // 4
 
 
-def solve(front_of, meta, diagonals, gathered):
+def pair_place(meta_ref):
+    return (meta_ref[0] & 1) * 4 + (meta_ref[1] >> 1)
+
+
+def no_place(meta_ref):
+    return jnp.int32(0)
+
+
+def solve(front_of, place_of, meta, diagonals, gathered):
     tile = gathered.shape[-1]
     return call(
-        functools.partial(solve_kernel, front_of),
+        functools.partial(solve_kernel, front_of, place_of),
         jax.ShapeDtypeStruct((tile, tile), BF16),
         [SMEM, VMEM, VMEM],
         VMEM,
-        [pltpu.VMEM((tile, tile), F32)],
+        [pltpu.VMEM((tile, tile), F32), pltpu.VMEM((tile, tile), F32)],
         flops=2**29,
         moved=2**22,
     )(meta, diagonals, gathered)
@@ -207,7 +212,7 @@
 
 
 def lower_kernel(
-    meta_ref, slots_ref, place_ref, chunks_ref, pivot_ref, solved_ref, keep_ref, send_ref, share_ref, total_ref, update_ref
+    meta_ref, slots_ref, place_ref, chunks_ref, pivot_ref, solved_ref, keep_ref, send_ref, spread_ref, total_ref, update_ref
 ):
     level, row, col = meta_ref[0], meta_ref[1], meta_ref[2]
     total_ref[...] = jnp.zeros_like(total_ref)
@@ -230,17 +235,25 @@
     keep_ref[...] = total_ref[:64]
     send_ref[...] = total_ref[64:128].astype(BF16)
     first = row % 2 * 64
+    length, tile = total_ref.shape[1], total_ref.shape[2]
     for column in range(8):
-        share_ref[column, 0] = total_ref[first].astype(BF16)
-        share_ref[column, 1] = total_ref[first + 8 * slots_ref[4 + level // 4, column]].astype(BF16)
-
-
-def upper_kernel(meta_ref, slots_ref, front_ref, pivot_ref, solved_ref, out_ref):
+        for part in range(2):
+            value = total_ref[part * 64 + column * 8 : part * 64 + column * 8 + 8]
+            spread_ref[column, part * 8 * length : (part + 1) * 8 * length] = value.astype(
+                BF16
+            ).reshape(8 * length, tile)
+        panel_tile = first + 8 * slots_ref[4 + level // 4, column]
+        spread_ref[column, 16 * length : 17 * length] = total_ref[first].astype(BF16)
+        spread_ref[column, 17 * length : 18 * length] = total_ref[panel_tile].astype(BF16)
+
+
+def upper_kernel(meta_ref, slots_ref, keep_ref, sent_ref, pivot_ref, solved_ref, out_ref):
     level, row, col = meta_ref[0], meta_ref[1], meta_ref[2]
-    tile = front_ref.shape[1]
+    tile = keep_ref.shape[1]
     dropped = pivot_slot_of(slots_ref, 4 + level // 4) == col
     update = jnp.dot(pivot_ref[...], solved_ref[...], preferred_element_type=F32)
-    result = jnp.where(dropped, 0.0, front_ref[...] - update)
+    front = keep_ref[...] + sent_ref[...].astype(F32)
+    result = jnp.where(dropped, 0.0, front - update)
     top = jnp.logical_and(
         lax.broadcasted_iota(jnp.int32, result.shape, 0) < tile // 16, row % 2 == 0
     )
@@ -273,24 +286,24 @@
     )
 
 
-def crossed(value):
-    return lax.ppermute(value, "row", [(row, row ^ 1) for row in range(8)])
-
-
 def over_columns(value):
     return lax.all_to_all(value, "col", split_axis=0, concat_axis=0, tiled=True)
 
 
-def spread_columns(value, slot):
-    pieces = over_columns(value.reshape(8, -1, value.shape[-1]))
-    piece = lax.dynamic_index_in_dim(pieces, slot, 0, keepdims=True)
-    return over_columns(jnp.broadcast_to(piece, pieces.shape)).reshape(value.shape)
-
-
-def gather_tiles(shares, slot, levels):
-    parts = lax.dynamic_index_in_dim(over_columns(shares), slot, 0, keepdims=False)
-    parts = (parts.astype(F32) + crossed(parts).astype(F32)).astype(BF16)
-    return exchange(jnp.broadcast_to(parts[None], (4 * levels,) + parts.shape), levels)
+def swapped(value, axis, mask):
+    return lax.ppermute(value, axis, [(index, index ^ mask) for index in range(8)])
+
+
+def tied(first, second):
+    return lax.optimization_barrier((first, second))
+
+
+def picked(pieces, slot):
+    return lax.dynamic_index_in_dim(pieces, slot, 0, keepdims=False)
+
+
+def repeated(value, count):
+    return jnp.broadcast_to(value[None], (count,) + value.shape)
 
 
 def body(leaf_blocks, leaf_tiles, leaf_maps, upper_maps, front_slots, pivot_diag):
@@ -301,10 +314,6 @@
     meta = jnp.stack([level, row, col]).astype(jnp.int32)
     positions = jnp.arange(8, dtype=jnp.int32)
     slots = jnp.sum(jnp.where(front_slots == 0, positions[None, :], 0), axis=1)
-
-    def slot_of(front):
-        return lax.dynamic_index_in_dim(slots, front, keepdims=False)
-
     eighth, sixteenth = tile // 8, tile // 16
     own = leaf_blocks.reshape(12, tile, tile)
 
@@ -317,54 +326,79 @@
     )(meta, leaf_tiles, leaf_maps, own)
     shares = exchange(shares, 2)
     chunks = jnp.swapaxes(own.reshape(12, 16, sixteenth, tile), 0, 1)
-    chunks = exchange(chunks, 4).reshape(192, sixteenth, tile)
+    chunks, shares = tied(chunks, shares)
+    chunks = exchange(chunks, 4).reshape(8, -1, tile)
     place = call(
         plan_kernel,
         jax.ShapeDtypeStruct((192,), jnp.int32),
         [SMEM] * 4,
         SMEM,
     )(meta, leaf_tiles, leaf_maps, upper_maps)
+
     shares = call(
         combine_kernel,
-        jax.ShapeDtypeStruct((8, 2, eighth, tile), BF16),
-        [SMEM, SMEM, VMEM],
+        jax.ShapeDtypeStruct((8, eighth, tile), BF16),
+        [VMEM],
         VMEM,
-        [pltpu.VMEM((8, eighth, tile), BF16)],
         moved=2**21,
-    )(meta, front_slots, shares)
-    gathered = gather_tiles(shares, slot_of(level // 2), 2)
-    pivot_columns = spread_columns(chunks, slot_of(level // 4 * 2 + col // 4))
-    solved = solve(lower_front, meta, pivot_diag, gathered)
-    other = lax.ppermute(solved, "level", [(index, index ^ 2) for index in range(8)])
+    )(shares)
+    away = col ^ picked(slots, level // 2)
+    for mask in (1, 2, 4):
+        shares = jnp.where(away & mask == 0, shares, swapped(shares, "col", mask))
+    my_tile = lax.dynamic_slice(front_slots, (level // 2, col), (1, 1))[0, 0]
+    parts = jnp.stack([shares[0], picked(shares, my_tile)])
+    parts = (parts.astype(F32) + swapped(parts, "row", 1).astype(F32)).astype(BF16)
+
+    chunks, parts = tied(chunks, parts)
+    pieces = over_columns(chunks)
+    gathered = parts[None]
+    for axis, mask in (("row", 2), ("row", 4), ("level", 1)):
+        gathered = jnp.concatenate([gathered, swapped(gathered, axis, mask)], axis=0)
+    piece = picked(pieces, picked(slots, level // 4 * 2 + col // 4))
+    piece, gathered = tied(piece, gathered)
+    pivot_columns = over_columns(repeated(piece, 8)).reshape(192, sixteenth, tile)
+    solved = solve(lower_front, pair_place, meta, pivot_diag, gathered)
+    other = swapped(solved, "level", 2)
     first_child = level // 2 % 2 == 0
     solved = jnp.where(first_child, jnp.stack([solved, other]), jnp.stack([other, solved]))
-    keep, send, shares = call(
+    keep, send, spread = call(
         lower_kernel,
         (
             jax.ShapeDtypeStruct((64, sixteenth, tile), F32),
             jax.ShapeDtypeStruct((64, sixteenth, tile), BF16),
-            jax.ShapeDtypeStruct((8, 2, sixteenth, tile), BF16),
+            jax.ShapeDtypeStruct((8, 18 * sixteenth, tile), BF16),
         ),
         [SMEM, SMEM, SMEM, VMEM, VMEM, VMEM],
         None,
         [pltpu.VMEM((129, sixteenth, tile), F32), pltpu.VMEM((96, sixteenth, tile), F32)],
         flops=2**29,
         moved=2**23,
-    )(meta, front_slots, place, chunks, pivot_columns, solved)
-
-    upper_slot = slot_of(4 + level // 4)
-    gathered = gather_tiles(shares, upper_slot, 4)
-    front = keep + crossed(send).astype(F32)
-    pivot_columns = spread_columns(front.astype(BF16), upper_slot)
-    solved = solve(upper_front, meta, pivot_diag, gathered)
+    )(meta, front_slots, place, chunks.reshape(192, sixteenth, tile), pivot_columns, solved)
+
+    spread = picked(over_columns(spread), picked(slots, 4 + level // 4)).astype(F32)
+    passed = swapped(spread[8 * sixteenth :].astype(BF16), "row", 1).astype(F32)
+    piece = (spread[: 8 * sixteenth] + passed[: 8 * sixteenth]).astype(BF16)
+    parts = (spread[16 * sixteenth :] + passed[8 * sixteenth :]).astype(BF16)
+    gathered = exchange(repeated(parts.reshape(2, sixteenth, tile), 16), 4)
+    piece, gathered = tied(piece, gathered)
+    pivot_columns = over_columns(repeated(piece, 8)).reshape(-1, tile)
+    solved = solve(upper_front, no_place, meta, pivot_diag, gathered)
+    sent = swapped(send, "row", 1)
     finished = call(
         upper_kernel,
         jax.ShapeDtypeStruct((16, 4, sixteenth, tile), BF16),
-        [SMEM, SMEM, VMEM, VMEM, VMEM],
+        [SMEM, SMEM, VMEM, VMEM, VMEM, VMEM],
         VMEM,
         flops=2**28,
         moved=2**22,
-    )(meta, front_slots, front.reshape(-1, tile), pivot_columns.reshape(-1, tile), solved)
+    )(
+        meta,
+        front_slots,
+        keep.reshape(-1, tile),
+        sent.reshape(-1, tile),
+        pivot_columns,
+        solved,
+    )
     result = exchange(finished, 4)
     return jnp.swapaxes(result, 0, 1).reshape(1, -1, tile)
 

time: 284 us -> 261 us (0.919)
  the two profiles are of different devices: /device:TPU:1 before, /device:TPU:128 now
where the time goes in v3:
time: 261 us; the launch traced here: 260 us
  starting transfers between devices  87.2 us (33%)
  waiting for transfers between devices  73.3 us (28%)
  blocking collectives  55.2 us (21%)
  Pallas kernels  28.4 us (11%)
  local copies, waits for them, and re-layouts  9.02 us (3%)
  between operations  6.81 us (3%)
    ppermute x10, starting transfers between devices, swapped(): lax.ppermute(value, axis, [(index, index ^ mask) for index in range(8)])  58.6 us
    all_to_all x2, blocking collectives, exchange(): lax.all_to_all(value, ('level', 'row'), split_axis=0, concat_axis=0, axis...  55.2 us
    ppermute x10, waiting for transfers between devices, swapped(): lax.ppermute(value, axis, [(index, index ^ mask) for index in range(8)])  29.6 us
    all_to_all x2, waiting for transfers between devices, exchange(): lax.all_to_all(value, ('level', 'row'), split_axis=0, concat_axis=0, axis...  27.7 us
    pallas_call x2, Pallas kernels, solve(): call(functools.partial(solve_kernel, front_of, place_of), jax.ShapeDtypeS...  18.7 us
    all_to_all x4, starting transfers between devices, over_columns(): return lax.all_to_all(value, 'col', split_axis=0, concat_axis=0, tiled=True)  17.5 us
    all_to_all x4, waiting for transfers between devices, over_columns(): return lax.all_to_all(value, 'col', split_axis=0, concat_axis=0, tiled=True)  16.1 us
    all_to_all x2, starting transfers between devices, exchange(): lax.all_to_all(value, ('level', 'row'), split_axis=0, concat_axis=0, axis...  11.1 us
  transfers between devices with their start and end apart: 16, of which 11 were waited for; matrix products, arithmetic and copies ran while one was open for 1% of the time, Pallas kernels for 8%

profile of v3, /device:TPU:128, one launch (start us, length us, event | category | flops | bytes accessed | tf_op | source)
XLA Modules:
  0.0 260.4 jit_solution(8804288871487795843)
XLA Ops:
  3.8 21.2 %all_to_all.40.shares_ref = bf16[8,8,32,256]{3,2,1,0:T(8,128)(2,1)S(1)} all-to-all(bf16[8,8,32,256]{3,2,1,0:T(8,128)(2,1)S(1)} %shard_map.65), channel_id=1, replica_groups={{0,16,32,48,64,80,96,112},{8,24,40,56,72,88,104,120},{128,144,160,176,1..., dimensions={0} | all-to-all | bytes 2097152 | tf_op jit(solution)/shard_map/all_to_all | solution.py:279
  26.3 5.7 %all-to-all-start.1 = ((bf16[16,12,16,256]{3,2,1,0:T(8,128)(2,1)}), bf16[16,12,16,256]{3,2,1,0:T(8,128)(2,1)}, u32[]{:S(2)}, u32[]{:S(2)}) async-start(bf16[16,12,16,256]{3,2,1,0:T(8,128)(2,1)} %copy.11), calls=%async_computation.1 | async-start | bytes 3145728 | tf_op jit(solution)/shard_map/all_to_all | solution.py:279
  39.1 4.3 %collective-permute-done.1 = bf16[8,32,256]{2,1,0:T(8,128)(2,1)S(1)} collective-permute-done((bf16[8,32,256]{2,1,0:T(8,128)(2,1)S(1)}, bf16[8,32,256]{2,1,0:T(8,128)(2,1)S(1)}, u32[]{:S(2)}, u32[]{:S(2)}) %collective-permute-start.1) | collective-permute-done | bytes 131104 | tf_op jit(solution)/shard_map/ppermute | solution.py:294
  43.5 5.1 %collective-permute-start.2 = (bf16[8,32,256]{2,1,0:T(8,128)(2,1)S(1)}, bf16[8,32,256]{2,1,0:T(8,128)(2,1)S(1)}, u32[]{:S(2)}, u32[]{:S(2)}) collective-permute-start(bf16[8,32,256]{2,1,0:T(8,128)(2,1)S(1)} %broadcast_select_fusion.1), channel_id=1, source_target_pairs={{0,4},{1,5},{2,6},{3,7},{4,0},{5,1},{6,2},{7,3},{8,12},{9,13},{10,... | collective-permute-start | bytes 393224 | tf_op jit(solution)/shard_map/ppermute | solution.py:294
  52.1 8.9 %collective-permute-start.3 = (bf16[2,32,256]{2,1,0:T(8,128)(2,1)S(1)}, bf16[2,32,256]{2,1,0:T(8,128)(2,1)S(1)}, u32[]{:S(2)}, u32[]{:S(2)}) collective-permute-start(bf16[2,32,256]{2,1,0:T(8,128)(2,1)S(1)} %pad_maximum_fusion.3), channel_id=1, source_target_pairs={{0,8},{8,0},{16,24},{24,16},{32,40},{40,32},{48,56},{56,48},{1,9},... | collective-permute-start | bytes 98312 | tf_op jit(solution)/shard_map/ppermute | solution.py:294
  61.0 5.7 %collective-permute-done.3 = bf16[2,32,256]{2,1,0:T(8,128)(2,1)S(1)} collective-permute-done((bf16[2,32,256]{2,1,0:T(8,128)(2,1)S(1)}, bf16[2,32,256]{2,1,0:T(8,128)(2,1)S(1)}, u32[]{:S(2)}, u32[]{:S(2)}) %collective-permute-start.3) | collective-permute-done | bytes 32800 | tf_op jit(solution)/shard_map/ppermute | solution.py:294
  66.8 4.5 %all-to-all-start.2 = ((bf16[8,384,256]{2,1,0:T(8,128)(2,1)}), bf16[8,384,256]{2,1,0:T(8,128)(2,1)S(1)}, u32[]{:S(2)}, u32[]{:S(2)}) async-start(bf16[8,384,256]{2,1,0:T(8,128)(2,1)} %bitcast.6), calls=%async_computation.2 | async-start | bytes 3145728 | tf_op jit(solution)/shard_map/all_to_all | solution.py:290
  71.3 4.2 %collective-permute-start.4 = (bf16[1,2,32,256]{3,2,1,0:T(8,128)(2,1)S(1)}, bf16[1,2,32,256]{3,2,1,0:T(8,128)(2,1)S(1)}, u32[]{:S(2)}, u32[]{:S(2)}) collective-permute-start(bf16[1,2,32,256]{3,2,1,0:T(8,128)(2,1)S(1)} %bitcast.43), channel_id=1, source_target_pairs={{0,16},{8,24},{16,0},{24,8},{32,48},{40,56},{48,32},{56,40},{1,17}... | collective-permute-start | bytes 98312 | tf_op jit(solution)/shard_map/ppermute | solution.py:294
  77.6 5.1 %collective-permute-start.5 = (bf16[2,2,32,256]{3,2,1,0:T(8,128)(2,1)S(1)}, bf16[2,2,32,256]{3,2,1,0:T(8,128)(2,1)S(1)}, u32[]{:S(2)}, u32[]{:S(2)}) collective-permute-start(bf16[2,2,32,256]{3,2,1,0:T(8,128)(2,1)S(1)} %pad_maximum_fusion.2), channel_id=1, source_target_pairs={{0,32},{8,40},{16,48},{24,56},{32,0},{40,8},{48,16},{56,24},{1,33}... | collective-permute-start | bytes 196616 | tf_op jit(solution)/shard_map/ppermute | solution.py:294
  85.2 6.3 %collective-permute-start.6 = (bf16[4,2,32,256]{3,2,1,0:T(8,128)(2,1)S(1)}, bf16[4,2,32,256]{3,2,1,0:T(8,128)(2,1)S(1)}, u32[]{:S(2)}, u32[]{:S(2)}) collective-permute-start(bf16[4,2,32,256]{3,2,1,0:T(8,128)(2,1)S(1)} %pad_maximum_fusion.1), channel_id=1, source_target_pairs={{0,64},{64,0},{128,192},{192,128},{256,320},{320,256},{384,448},{4... | collective-permute-start | bytes 393224 | tf_op jit(solution)/shard_map/ppermute | solution.py:294
  95.8 4.9 %all-to-all-start.3 = ((bf16[8,384,256]{2,1,0:T(8,128)(2,1)}), bf16[8,384,256]{2,1,0:T(8,128)(2,1)S(1)}, u32[]{:S(2)}, u32[]{:S(2)}) async-start(bf16[8,384,256]{2,1,0:T(8,128)(2,1)} %broadcast_in_dim.35), calls=%async_computation.3 | async-start | bytes 3145728 | tf_op jit(solution)/shard_map/all_to_all | solution.py:290
  100.8 9.4 %shard_map.67 = bf16[256,256]{1,0:T(8,128)(2,1)S(1)} custom-call(s32[3]{0:T(128)S(1)} %pad_add_fusion.meta_ref, f32[6,256]{1,0:T(8,128)S(1)} %copy-done.7, bf16[8,2,32,256]{3,2,1,0:T(8,128)(2,1)S(1)} %pad_maximum_fusion.gathered_ref), custom_call_target="tpu_custom_call" | custom-call | flops 536870912 | bytes 4194304 | tf_op jit(solution)/shard_map/pallas_call | solution.py:196
  110.2 5.7 %collective-permute-start.7 = (bf16[256,256]{1,0:T(8,128)(2,1)S(1)}, bf16[256,256]{1,0:T(8,128)(2,1)S(1)}, u32[]{:S(2)}, u32[]{:S(2)}) collective-permute-start(bf16[256,256]{1,0:T(8,128)(2,1)S(1)} %shard_map.67), channel_id=1, source_target_pairs={{0,128},{64,192},{128,0},{192,64},{256,384},{320,448},{384,256},{4... | collective-permute-start | bytes 393224 | tf_op jit(solution)/shard_map/ppermute | solution.py:294
  118.9 4.0 %collective-permute-done.7 = bf16[256,256]{1,0:T(8,128)(2,1)S(1)} collective-permute-done((bf16[256,256]{1,0:T(8,128)(2,1)S(1)}, bf16[256,256]{1,0:T(8,128)(2,1)S(1)}, u32[]{:S(2)}, u32[]{:S(2)}) %collective-permute-start.7) | collective-permute-done | bytes 131104 | tf_op jit(solution)/shard_map/ppermute | solution.py:294
  122.9 4.9 %shard_map.68 = (f32[64,16,256]{2,1,0:T(8,128)S(1)}, bf16[64,16,256]{2,1,0:T(8,128)(2,1)S(1)}, bf16[8,288,256]{2,1,0:T(8,128)(2,1)}) custom-call(s32[3]{0:T(128)S(1)} %pad_add_fusion.meta_ref, s32[6,8]{1,0:T(8,128)S(1)} %copy-done.1, s32[192]{0:T(256)S(1)} %shard_map.64.place_ref, bf16[192,16,256]{2,1,0:T(8,128)(2,1)} %bitcast.9.chunks_ref, ...), custom_call_target="tpu_custom_call" | custom-call | flops 536870912 | bytes 8388608 | tf_op jit(solution)/shard_map/pallas_call | solution.py:364
  127.8 4.4 %all-to-all-start.4 = ((bf16[8,288,256]{2,1,0:T(8,128)(2,1)}), bf16[8,288,256]{2,1,0:T(8,128)(2,1)S(1)}, u32[]{:S(2)}, u32[]{:S(2)}) async-start(bf16[8,288,256]{2,1,0:T(8,128)(2,1)} %get-tuple-element.24), calls=%async_computation.4 | async-start | bytes 2359296 | tf_op jit(solution)/shard_map/all_to_all | solution.py:290
  134.3 15.3 %all-to-all-done.4 = bf16[8,288,256]{2,1,0:T(8,128)(2,1)S(1)} async-done(((bf16[8,288,256]{2,1,0:T(8,128)(2,1)}), bf16[8,288,256]{2,1,0:T(8,128)(2,1)S(1)}, u32[]{:S(2)}, u32[]{:S(2)}) %all-to-all-start.4) | async-done | bytes 1179680 | tf_op jit(solution)/shard_map/all_to_all | solution.py:290
  149.6 8.5 %collective-permute-start.9 = (bf16[160,256]{1,0:T(8,128)(2,1)S(1)}, bf16[160,256]{1,0:T(8,128)(2,1)S(1)}, u32[]{:S(2)}, u32[]{:S(2)}) collective-permute-start(bf16[160,256]{1,0:T(8,128)(2,1)S(1)} %dynamic-slice_bitcast_fusion.1), channel_id=1, source_target_pairs={{0,8},{8,0},{16,24},{24,16},{32,40},{40,32},{48,56},{56,48},{1,9},... | collective-permute-start | bytes 245768 | tf_op jit(solution)/shard_map/ppermute | solution.py:294
  158.2 8.7 %collective-permute-done.9 = bf16[160,256]{1,0:T(8,128)(2,1)S(1)} collective-permute-done((bf16[160,256]{1,0:T(8,128)(2,1)S(1)}, bf16[160,256]{1,0:T(8,128)(2,1)S(1)}, u32[]{:S(2)}, u32[]{:S(2)}) %collective-permute-start.9) | collective-permute-done | bytes 81952 | tf_op jit(solution)/shard_map/ppermute | solution.py:294
  167.7 5.4 %all-to-all-start.5 = ((bf16[16,2,16,256]{3,2,1,0:T(8,128)(2,1)}), bf16[16,2,16,256]{3,2,1,0:T(8,128)(2,1)S(1)}, u32[]{:S(2)}, u32[]{:S(2)}) async-start(bf16[16,2,16,256]{3,2,1,0:T(8,128)(2,1)} %broadcast_in_dim.37), calls=%async_computation.5 | async-start | bytes 524288 | tf_op jit(solution)/shard_map/all_to_all | solution.py:279
  173.1 9.3 %collective-permute-start.8 = (bf16[64,16,256]{2,1,0:T(8,128)(2,1)S(1)}, bf16[64,16,256]{2,1,0:T(8,128)(2,1)S(1)}, u32[]{:S(2)}, u32[]{:S(2)}) collective-permute-start(bf16[64,16,256]{2,1,0:T(8,128)(2,1)S(1)} %get-tuple-element.23), channel_id=1, source_target_pairs={{0,8},{8,0},{16,24},{24,16},{32,40},{40,32},{48,56},{56,48},{1,9},... | collective-permute-start | bytes 1572872 | tf_op jit(solution)/shard_map/ppermute | solution.py:294
  182.4 27.7 %all-to-all-done.5.gathered_ref = bf16[16,2,16,256]{3,2,1,0:T(8,128)(2,1)S(1)} async-done(((bf16[16,2,16,256]{3,2,1,0:T(8,128)(2,1)}), bf16[16,2,16,256]{3,2,1,0:T(8,128)(2,1)S(1)}, u32[]{:S(2)}, u32[]{:S(2)}) %all-to-all-start.5) | async-done | bytes 262176 | tf_op jit(solution)/shard_map/all_to_all | solution.py:279
  214.6 9.3 %shard_map.69.solved_ref = bf16[256,256]{1,0:T(8,128)(2,1)S(1)} custom-call(s32[3]{0:T(128)S(1)} %pad_add_fusion.meta_ref, f32[6,256]{1,0:T(8,128)S(1)} %copy-done.7, bf16[16,2,16,256]{3,2,1,0:T(8,128)(2,1)S(1)} %all-to-all-done.5.gathered_ref), custom_call_target="tpu_custom_call" | custom-call | flops 536870912 | bytes 4194304 | tf_op jit(solution)/shard_map/pallas_call | solution.py:196
  225.6 34.0 %all_to_all.41 = bf16[16,4,16,256]{3,2,1,0:T(8,128)(2,1)S(1)} all-to-all(bf16[16,4,16,256]{3,2,1,0:T(8,128)(2,1)S(1)} %shard_map.70), channel_id=1, replica_groups={{0,16,32,48,64,80,96,112,128,144,160,176,192,208,224,240},{8,24,40,56,7..., dimensions={0} | all-to-all | bytes 1048576 | tf_op jit(solution)/shard_map/all_to_all | solution.py:279
  (58 shorter events, 30.9 us)
Async XLA Ops:
  0.1 1.4 copy-start
  1.5 0.7 copy-start.2
  2.2 0.7 copy-start.4
  26.3 7.8 %copy-start.1 = (s32[6,8]{1,0:T(8,128)S(1)}, s32[6,8]{1,0:T(8,128)}, u32[]{:S(2)}) copy-start(s32[6,8]{1,0:T(8,128)} %slots_ref.3) | copy-start | bytes 580
  26.3 40.5 %all-to-all-start.1 = ((bf16[16,12,16,256]{3,2,1,0:T(8,128)(2,1)}), bf16[16,12,16,256]{3,2,1,0:T(8,128)(2,1)}, u32[]{:S(2)}, u32[]{:S(2)}) async-start(bf16[16,12,16,256]{3,2,1,0:T(8,128)(2,1)} %copy.11), calls=%async_computation.1 | async-start | bytes 3145728 | tf_op jit(solution)/shard_map/all_to_all | solution.py:279
  32.1 3.5 %collective-permute-start = (bf16[8,32,256]{2,1,0:T(8,128)(2,1)S(1)}, bf16[8,32,256]{2,1,0:T(8,128)(2,1)S(1)}, u32[]{:S(2)}, u32[]{:S(2)}) collective-permute-start(bf16[8,32,256]{2,1,0:T(8,128)(2,1)S(1)} %shard_map.66), channel_id=1, source_target_pairs={{0,1},{1,0},{2,3},{3,2},{4,5},{5,4},{6,7},{7,6},{8,9},{9,8},{10,11... | collective-permute-start | bytes 393224 | tf_op jit(solution)/shard_map/ppermute | solution.py:294
  35.6 7.8 %collective-permute-start.1 = (bf16[8,32,256]{2,1,0:T(8,128)(2,1)S(1)}, bf16[8,32,256]{2,1,0:T(8,128)(2,1)S(1)}, u32[]{:S(2)}, u32[]{:S(2)}) collective-permute-start(bf16[8,32,256]{2,1,0:T(8,128)(2,1)S(1)} %broadcast_select_fusion), channel_id=1, source_target_pairs={{0,2},{1,3},{2,0},{3,1},{4,6},{5,7},{6,4},{7,5},{8,10},{9,11},{10,... | collective-permute-start | bytes 393224 | tf_op jit(solution)/shard_map/ppermute | solution.py:294
  43.5 8.6 %collective-permute-start.2 = (bf16[8,32,256]{2,1,0:T(8,128)(2,1)S(1)}, bf16[8,32,256]{2,1,0:T(8,128)(2,1)S(1)}, u32[]{:S(2)}, u32[]{:S(2)}) collective-permute-start(bf16[8,32,256]{2,1,0:T(8,128)(2,1)S(1)} %broadcast_select_fusion.1), channel_id=1, source_target_pairs={{0,4},{1,5},{2,6},{3,7},{4,0},{5,1},{6,2},{7,3},{8,12},{9,13},{10,... | collective-permute-start | bytes 393224 | tf_op jit(solution)/shard_map/ppermute | solution.py:294
  52.1 14.6 %collective-permute-start.3 = (bf16[2,32,256]{2,1,0:T(8,128)(2,1)S(1)}, bf16[2,32,256]{2,1,0:T(8,128)(2,1)S(1)}, u32[]{:S(2)}, u32[]{:S(2)}) collective-permute-start(bf16[2,32,256]{2,1,0:T(8,128)(2,1)S(1)} %pad_maximum_fusion.3), channel_id=1, source_target_pairs={{0,8},{8,0},{16,24},{24,16},{32,40},{40,32},{48,56},{56,48},{1,9},... | collective-permute-start | bytes 98312 | tf_op jit(solution)/shard_map/ppermute | solution.py:294
  66.8 27.8 %all-to-all-start.2 = ((bf16[8,384,256]{2,1,0:T(8,128)(2,1)}), bf16[8,384,256]{2,1,0:T(8,128)(2,1)S(1)}, u32[]{:S(2)}, u32[]{:S(2)}) async-start(bf16[8,384,256]{2,1,0:T(8,128)(2,1)} %bitcast.6), calls=%async_computation.2 | async-start | bytes 3145728 | tf_op jit(solution)/shard_map/all_to_all | solution.py:290
  71.3 6.3 %collective-permute-start.4 = (bf16[1,2,32,256]{3,2,1,0:T(8,128)(2,1)S(1)}, bf16[1,2,32,256]{3,2,1,0:T(8,128)(2,1)S(1)}, u32[]{:S(2)}, u32[]{:S(2)}) collective-permute-start(bf16[1,2,32,256]{3,2,1,0:T(8,128)(2,1)S(1)} %bitcast.43), channel_id=1, source_target_pairs={{0,16},{8,24},{16,0},{24,8},{32,48},{40,56},{48,32},{56,40},{1,17}... | collective-permute-start | bytes 98312 | tf_op jit(solution)/shard_map/ppermute | solution.py:294
  77.6 7.7 %collective-permute-start.5 = (bf16[2,2,32,256]{3,2,1,0:T(8,128)(2,1)S(1)}, bf16[2,2,32,256]{3,2,1,0:T(8,128)(2,1)S(1)}, u32[]{:S(2)}, u32[]{:S(2)}) collective-permute-start(bf16[2,2,32,256]{3,2,1,0:T(8,128)(2,1)S(1)} %pad_maximum_fusion.2), channel_id=1, source_target_pairs={{0,32},{8,40},{16,48},{24,56},{32,0},{40,8},{48,16},{56,24},{1,33}... | collective-permute-start | bytes 196616 | tf_op jit(solution)/shard_map/ppermute | solution.py:294
  85.2 9.3 %collective-permute-start.6 = (bf16[4,2,32,256]{3,2,1,0:T(8,128)(2,1)S(1)}, bf16[4,2,32,256]{3,2,1,0:T(8,128)(2,1)S(1)}, u32[]{:S(2)}, u32[]{:S(2)}) collective-permute-start(bf16[4,2,32,256]{3,2,1,0:T(8,128)(2,1)S(1)} %pad_maximum_fusion.1), channel_id=1, source_target_pairs={{0,64},{64,0},{128,192},{192,128},{256,320},{320,256},{384,448},{4... | collective-permute-start | bytes 393224 | tf_op jit(solution)/shard_map/ppermute | solution.py:294
  95.8 4.9 %copy-start.7 = (f32[6,256]{1,0:T(8,128)S(1)}, f32[6,256]{1,0:T(8,128)}, u32[]{:S(2)}) copy-start(f32[6,256]{1,0:T(8,128)} %diag_ref.3) | copy-start | bytes 18436
  95.8 27.1 %all-to-all-start.3 = ((bf16[8,384,256]{2,1,0:T(8,128)(2,1)}), bf16[8,384,256]{2,1,0:T(8,128)(2,1)S(1)}, u32[]{:S(2)}, u32[]{:S(2)}) async-start(bf16[8,384,256]{2,1,0:T(8,128)(2,1)} %broadcast_in_dim.35), calls=%async_computation.3 | async-start | bytes 3145728 | tf_op jit(solution)/shard_map/all_to_all | solution.py:290
  100.8 15.2 %copy-start.3 = (s32[8,96]{1,0:T(8,128)S(1)}, s32[8,96]{1,0:T(8,128)}, u32[]{:S(2)}) copy-start(s32[8,96]{1,0:T(8,128)} %leaf_maps_ref.3) | copy-start | bytes 9220
  100.8 15.2 %copy-start.5 = (s32[8]{0:T(128)S(1)}, s32[8]{0:T(128)}, u32[]{:S(2)}) copy-start(s32[8]{0:T(128)} %tiles_ref.3) | copy-start | bytes 100
  100.8 15.2 %copy-start.6 = (s32[4,128]{1,0:T(4,128)S(1)}, s32[4,128]{1,0:T(4,128)}, u32[]{:S(2)}) copy-start(s32[4,128]{1,0:T(4,128)} %upper_maps_ref.1) | copy-start | bytes 6148
  110.2 12.7 %collective-permute-start.7 = (bf16[256,256]{1,0:T(8,128)(2,1)S(1)}, bf16[256,256]{1,0:T(8,128)(2,1)S(1)}, u32[]{:S(2)}, u32[]{:S(2)}) collective-permute-start(bf16[256,256]{1,0:T(8,128)(2,1)S(1)} %shard_map.67), channel_id=1, source_target_pairs={{0,128},{64,192},{128,0},{192,64},{256,384},{320,448},{384,256},{4... | collective-permute-start | bytes 393224 | tf_op jit(solution)/shard_map/ppermute | solution.py:294
  127.8 21.8 %all-to-all-start.4 = ((bf16[8,288,256]{2,1,0:T(8,128)(2,1)}), bf16[8,288,256]{2,1,0:T(8,128)(2,1)S(1)}, u32[]{:S(2)}, u32[]{:S(2)}) async-start(bf16[8,288,256]{2,1,0:T(8,128)(2,1)} %get-tuple-element.24), calls=%async_computation.4 | async-start | bytes 2359296 | tf_op jit(solution)/shard_map/all_to_all | solution.py:290
  149.6 17.3 %collective-permute-start.9 = (bf16[160,256]{1,0:T(8,128)(2,1)S(1)}, bf16[160,256]{1,0:T(8,128)(2,1)S(1)}, u32[]{:S(2)}, u32[]{:S(2)}) collective-permute-start(bf16[160,256]{1,0:T(8,128)(2,1)S(1)} %dynamic-slice_bitcast_fusion.1), channel_id=1, source_target_pairs={{0,8},{8,0},{16,24},{24,16},{32,40},{40,32},{48,56},{56,48},{1,9},... | collective-permute-start | bytes 245768 | tf_op jit(solution)/shard_map/ppermute | solution.py:294
  167.7 42.4 %all-to-all-start.5 = ((bf16[16,2,16,256]{3,2,1,0:T(8,128)(2,1)}), bf16[16,2,16,256]{3,2,1,0:T(8,128)(2,1)S(1)}, u32[]{:S(2)}, u32[]{:S(2)}) async-start(bf16[16,2,16,256]{3,2,1,0:T(8,128)(2,1)} %broadcast_in_dim.37), calls=%async_computation.5 | async-start | bytes 524288 | tf_op jit(solution)/shard_map/all_to_all | solution.py:279
  173.1 50.7 %collective-permute-start.8 = (bf16[64,16,256]{2,1,0:T(8,128)(2,1)S(1)}, bf16[64,16,256]{2,1,0:T(8,128)(2,1)S(1)}, u32[]{:S(2)}, u32[]{:S(2)}) collective-permute-start(bf16[64,16,256]{2,1,0:T(8,128)(2,1)S(1)} %get-tuple-element.23), channel_id=1, source_target_pairs={{0,8},{8,0},{16,24},{24,16},{32,40},{40,32},{48,56},{56,48},{1,9},... | collective-permute-start | bytes 1572872 | tf_op jit(solution)/shard_map/ppermute | solution.py:294
  210.9 13.8 %all-to-all-start.6 = ((bf16[8,128,256]{2,1,0:T(8,128)(2,1)}), bf16[8,128,256]{2,1,0:T(8,128)(2,1)S(1)}, u32[]{:S(2)}, u32[]{:S(2)}) async-start(bf16[8,128,256]{2,1,0:T(8,128)(2,1)} %broadcast_in_dim.38), calls=%async_computation.6 | async-start | bytes 1048576 | tf_op jit(solution)/shard_map/all_to_all | solution.py:290

commit v4 on v3

--- a/solution.py
+++ b/solution.py
@@ -247,12 +247,13 @@
         spread_ref[column, 17 * length : 18 * length] = total_ref[panel_tile].astype(BF16)
 
 
-def upper_kernel(meta_ref, slots_ref, keep_ref, sent_ref, pivot_ref, solved_ref, out_ref):
+def upper_kernel(meta_ref, slots_ref, keep_ref, ups_ref, downs_ref, pivot_ref, solved_ref, out_ref):
     level, row, col = meta_ref[0], meta_ref[1], meta_ref[2]
     tile = keep_ref.shape[1]
     dropped = pivot_slot_of(slots_ref, 4 + level // 4) == col
     update = jnp.dot(pivot_ref[...], solved_ref[...], preferred_element_type=F32)
-    front = keep_ref[...] + sent_ref[...].astype(F32)
+    sent = jnp.concatenate([ups_ref[...], downs_ref[...]], axis=0)
+    front = keep_ref[...] + sent.astype(F32)
     result = jnp.where(dropped, 0.0, front - update)
     top = jnp.logical_and(
         lax.broadcasted_iota(jnp.int32, result.shape, 0) < tile // 16, row % 2 == 0
@@ -294,8 +295,17 @@
     return lax.ppermute(value, axis, [(index, index ^ mask) for index in range(8)])
 
 
-def tied(first, second):
-    return lax.optimization_barrier((first, second))
+def hopped(value, way):
+    pairs = []
+    for level in range(8):
+        target = (level + 4) % 8
+        turn = int(level >= 4) if way > 0 else int(level < 4)
+        pairs += [(level * 8 + row, target * 8 + (row ^ turn)) for row in range(8)]
+    return lax.ppermute(value, ("level", "row"), pairs)
+
+
+def tied(*values):
+    return lax.optimization_barrier(values)
 
 
 def picked(pieces, slot):
@@ -375,7 +385,10 @@
         moved=2**23,
     )(meta, front_slots, place, chunks.reshape(192, sixteenth, tile), pivot_columns, solved)
 
-    spread = picked(over_columns(spread), picked(slots, 4 + level // 4)).astype(F32)
+    ups, downs = hopped(send[:32], 1), hopped(send[32:], -1)
+    spread = picked(over_columns(spread), picked(slots, 4 + level // 4))
+    spread, ups, downs = tied(spread, ups, downs)
+    spread = spread.astype(F32)
     passed = swapped(spread[8 * sixteenth :].astype(BF16), "row", 1).astype(F32)
     piece = (spread[: 8 * sixteenth] + passed[: 8 * sixteenth]).astype(BF16)
     parts = (spread[16 * sixteenth :] + passed[8 * sixteenth :]).astype(BF16)
@@ -383,11 +396,11 @@
     piece, gathered = tied(piece, gathered)
     pivot_columns = over_columns(repeated(piece, 8)).reshape(-1, tile)
     solved = solve(upper_front, no_place, meta, pivot_diag, gathered)
-    sent = swapped(send, "row", 1)
+    ups, downs = hopped(ups, 1), hopped(downs, -1)
     finished = call(
         upper_kernel,
         jax.ShapeDtypeStruct((16, 4, sixteenth, tile), BF16),
-        [SMEM, SMEM, VMEM, VMEM, VMEM, VMEM],
+        [SMEM, SMEM, VMEM, VMEM, VMEM, VMEM, VMEM],
         VMEM,
         flops=2**28,
         moved=2**22,
@@ -395,7 +408,8 @@
         meta,
         front_slots,
         keep.reshape(-1, tile),
-        sent.reshape(-1, tile),
+        ups.reshape(-1, tile),
+        downs.reshape(-1, tile),
         pivot_columns,
         solved,
     )

time: 261 us -> 269 us (1.031)
  the two profiles are of different devices: /device:TPU:128 before, /device:TPU:1 now
where the time goes in v4:
time: 269 us; the launch traced here: 267 us
  starting transfers between devices  123 us (46%)
  waiting for transfers between devices  64.7 us (24%)
  blocking collectives  34.4 us (13%)
  Pallas kernels  28.4 us (11%)
  local copies, waits for them, and re-layouts  9.76 us (4%)
  between operations  6.78 us (3%)
    ppermute x9, starting transfers between devices, swapped(): lax.ppermute(value, axis, [(index, index ^ mask) for index in range(8)])  51.1 us
    all_to_all x2, blocking collectives, exchange(): lax.all_to_all(value, ('level', 'row'), split_axis=0, concat_axis=0, axis...  34.4 us
    ppermute x4, waiting for transfers between devices, hopped(): return lax.ppermute(value, ('level', 'row'), pairs)  32.4 us
    all_to_all x2, starting transfers between devices, exchange(): lax.all_to_all(value, ('level', 'row'), split_axis=0, concat_axis=0, axis...  25.5 us
    all_to_all x4, starting transfers between devices, over_columns(): return lax.all_to_all(value, 'col', split_axis=0, concat_axis=0, tiled=True)  23.5 us
    ppermute x4, starting transfers between devices, hopped(): return lax.ppermute(value, ('level', 'row'), pairs)  22.6 us
    ppermute x9, waiting for transfers between devices, swapped(): lax.ppermute(value, axis, [(index, index ^ mask) for index in range(8)])  18.7 us
    pallas_call x2, Pallas kernels, solve(): call(functools.partial(solve_kernel, front_of, place_of), jax.ShapeDtypeS...  18.7 us
  transfers between devices with their start and end apart: 19, of which 14 were waited for; matrix products, arithmetic and copies ran while one was open for 1% of the time, Pallas kernels for 8%

profile of v4, /device:TPU:1, one launch (start us, length us, event | category | flops | bytes accessed | tf_op | source)
XLA Modules:
  0.0 267.1 jit_solution(4588831392883363169)
XLA Ops:
  3.8 17.5 %all_to_all.40.shares_ref = bf16[8,8,32,256]{3,2,1,0:T(8,128)(2,1)S(1)} all-to-all(bf16[8,8,32,256]{3,2,1,0:T(8,128)(2,1)S(1)} %shard_map.65), channel_id=1, replica_groups={{0,16,32,48,64,80,96,112},{8,24,40,56,72,88,104,120},{128,144,160,176,1..., dimensions={0} | all-to-all | bytes 2097152 | tf_op jit(solution)/shard_map/all_to_all | solution.py:280
  22.6 8.7 %all-to-all-start.1 = ((bf16[16,12,16,256]{3,2,1,0:T(8,128)(2,1)}), bf16[16,12,16,256]{3,2,1,0:T(8,128)(2,1)}, u32[]{:S(2)}, u32[]{:S(2)}) async-start(bf16[16,12,16,256]{3,2,1,0:T(8,128)(2,1)} %copy.11), calls=%async_computation.1 | async-start | bytes 3145728 | tf_op jit(solution)/shard_map/all_to_all | solution.py:280
  31.5 4.0 %collective-permute-start = (bf16[8,32,256]{2,1,0:T(8,128)(2,1)S(1)}, bf16[8,32,256]{2,1,0:T(8,128)(2,1)S(1)}, u32[]{:S(2)}, u32[]{:S(2)}) collective-permute-start(bf16[8,32,256]{2,1,0:T(8,128)(2,1)S(1)} %shard_map.66), channel_id=1, source_target_pairs={{0,1},{1,0},{2,3},{3,2},{4,5},{5,4},{6,7},{7,6},{8,9},{9,8},{10,11... | collective-permute-start | bytes 393224 | tf_op jit(solution)/shard_map/ppermute | solution.py:295
  40.3 3.9 %collective-permute-done.1 = bf16[8,32,256]{2,1,0:T(8,128)(2,1)S(1)} collective-permute-done((bf16[8,32,256]{2,1,0:T(8,128)(2,1)S(1)}, bf16[8,32,256]{2,1,0:T(8,128)(2,1)S(1)}, u32[]{:S(2)}, u32[]{:S(2)}) %collective-permute-start.1) | collective-permute-done | bytes 131104 | tf_op jit(solution)/shard_map/ppermute | solution.py:295
  44.3 4.8 %collective-permute-start.2 = (bf16[8,32,256]{2,1,0:T(8,128)(2,1)S(1)}, bf16[8,32,256]{2,1,0:T(8,128)(2,1)S(1)}, u32[]{:S(2)}, u32[]{:S(2)}) collective-permute-start(bf16[8,32,256]{2,1,0:T(8,128)(2,1)S(1)} %broadcast_select_fusion.1), channel_id=1, source_target_pairs={{0,4},{1,5},{2,6},{3,7},{4,0},{5,1},{6,2},{7,3},{8,12},{9,13},{10,... | collective-permute-start | bytes 393224 | tf_op jit(solution)/shard_map/ppermute | solution.py:295
  52.2 13.4 %collective-permute-start.3 = (bf16[2,32,256]{2,1,0:T(8,128)(2,1)S(1)}, bf16[2,32,256]{2,1,0:T(8,128)(2,1)S(1)}, u32[]{:S(2)}, u32[]{:S(2)}) collective-permute-start(bf16[2,32,256]{2,1,0:T(8,128)(2,1)S(1)} %pad_maximum_fusion.3), channel_id=1, source_target_pairs={{0,8},{8,0},{16,24},{24,16},{32,40},{40,32},{48,56},{56,48},{1,9},... | collective-permute-start | bytes 98312 | tf_op jit(solution)/shard_map/ppermute | solution.py:295
  67.6 7.4 %all-to-all-start.2 = ((bf16[8,384,256]{2,1,0:T(8,128)(2,1)}), bf16[8,384,256]{2,1,0:T(8,128)(2,1)S(1)}, u32[]{:S(2)}, u32[]{:S(2)}) async-start(bf16[8,384,256]{2,1,0:T(8,128)(2,1)} %bitcast.6), calls=%async_computation.2 | async-start | bytes 3145728 | tf_op jit(solution)/shard_map/all_to_all | solution.py:291
  79.9 4.7 %collective-permute-start.5 = (bf16[2,2,32,256]{3,2,1,0:T(8,128)(2,1)S(1)}, bf16[2,2,32,256]{3,2,1,0:T(8,128)(2,1)S(1)}, u32[]{:S(2)}, u32[]{:S(2)}) collective-permute-start(bf16[2,2,32,256]{3,2,1,0:T(8,128)(2,1)S(1)} %pad_maximum_fusion.2), channel_id=1, source_target_pairs={{0,32},{8,40},{16,48},{24,56},{32,0},{40,8},{48,16},{56,24},{1,33}... | collective-permute-start | bytes 196616 | tf_op jit(solution)/shard_map/ppermute | solution.py:295
  96.9 4.6 %all-to-all-start.3 = ((bf16[8,384,256]{2,1,0:T(8,128)(2,1)}), bf16[8,384,256]{2,1,0:T(8,128)(2,1)S(1)}, u32[]{:S(2)}, u32[]{:S(2)}) async-start(bf16[8,384,256]{2,1,0:T(8,128)(2,1)} %broadcast_in_dim.35), calls=%async_computation.3 | async-start | bytes 3145728 | tf_op jit(solution)/shard_map/all_to_all | solution.py:291
  101.6 9.4 %shard_map.67 = bf16[256,256]{1,0:T(8,128)(2,1)S(1)} custom-call(s32[3]{0:T(128)S(1)} %pad_add_fusion.meta_ref, f32[6,256]{1,0:T(8,128)S(1)} %copy-done.7, bf16[8,2,32,256]{3,2,1,0:T(8,128)(2,1)S(1)} %pad_maximum_fusion.gathered_ref), custom_call_target="tpu_custom_call" | custom-call | flops 536870912 | bytes 4194304 | tf_op jit(solution)/shard_map/pallas_call | solution.py:196
  111.0 4.7 %collective-permute-start.7 = (bf16[256,256]{1,0:T(8,128)(2,1)S(1)}, bf16[256,256]{1,0:T(8,128)(2,1)S(1)}, u32[]{:S(2)}, u32[]{:S(2)}) collective-permute-start(bf16[256,256]{1,0:T(8,128)(2,1)S(1)} %shard_map.67), channel_id=1, source_target_pairs={{0,128},{64,192},{128,0},{192,64},{256,384},{320,448},{384,256},{4... | collective-permute-start | bytes 393224 | tf_op jit(solution)/shard_map/ppermute | solution.py:295
  122.4 4.9 %shard_map.68 = (f32[64,16,256]{2,1,0:T(8,128)S(1)}, bf16[64,16,256]{2,1,0:T(8,128)(2,1)S(1)}, bf16[8,288,256]{2,1,0:T(8,128)(2,1)}) custom-call(s32[3]{0:T(128)S(1)} %pad_add_fusion.meta_ref, s32[6,8]{1,0:T(8,128)S(1)} %copy-done.1, s32[192]{0:T(256)S(1)} %shard_map.64.place_ref, bf16[192,16,256]{2,1,0:T(8,128)(2,1)} %bitcast.9.chunks_ref, ...), custom_call_target="tpu_custom_call" | custom-call | flops 536870912 | bytes 8388608 | tf_op jit(solution)/shard_map/pallas_call | solution.py:374
  127.3 5.2 %all-to-all-start.4 = ((bf16[8,288,256]{2,1,0:T(8,128)(2,1)}), bf16[8,288,256]{2,1,0:T(8,128)(2,1)S(1)}, u32[]{:S(2)}, u32[]{:S(2)}) async-start(bf16[8,288,256]{2,1,0:T(8,128)(2,1)} %get-tuple-element.26), calls=%async_computation.4 | async-start | bytes 2359296 | tf_op jit(solution)/shard_map/all_to_all | solution.py:291
  133.2 11.3 %collective-permute-start.9 = (bf16[32,16,256]{2,1,0:T(8,128)(2,1)}, bf16[32,16,256]{2,1,0:T(8,128)(2,1)S(1)}, u32[]{:S(2)}, u32[]{:S(2)}) collective-permute-start(bf16[32,16,256]{2,1,0:T(8,128)(2,1)} %get-tuple-element.33), channel_id=1, source_target_pairs={{0,264},{8,256},{16,280},{24,272},{32,296},{40,288},{48,312},{56,3... | collective-permute-start | bytes 786440 | tf_op jit(solution)/shard_map/ppermute | solution.py:304
  149.0 18.1 %collective-permute-done.9 = bf16[32,16,256]{2,1,0:T(8,128)(2,1)S(1)} collective-permute-done((bf16[32,16,256]{2,1,0:T(8,128)(2,1)}, bf16[32,16,256]{2,1,0:T(8,128)(2,1)S(1)}, u32[]{:S(2)}, u32[]{:S(2)}) %collective-permute-start.9) | collective-permute-done | bytes 262176 | tf_op jit(solution)/shard_map/ppermute | solution.py:304
  167.2 10.2 %collective-permute-start.12 = (bf16[160,256]{1,0:T(8,128)(2,1)S(1)}, bf16[160,256]{1,0:T(8,128)(2,1)S(1)}, u32[]{:S(2)}, u32[]{:S(2)}) collective-permute-start(bf16[160,256]{1,0:T(8,128)(2,1)S(1)} %slice.29), channel_id=1, source_target_pairs={{0,8},{8,0},{16,24},{24,16},{32,40},{40,32},{48,56},{56,48},{1,9},... | collective-permute-start | bytes 245768 | tf_op jit(solution)/shard_map/ppermute | solution.py:295
  177.4 3.8 %collective-permute-done.12 = bf16[160,256]{1,0:T(8,128)(2,1)S(1)} collective-permute-done((bf16[160,256]{1,0:T(8,128)(2,1)S(1)}, bf16[160,256]{1,0:T(8,128)(2,1)S(1)}, u32[]{:S(2)}, u32[]{:S(2)}) %collective-permute-start.12) | collective-permute-done | bytes 81952 | tf_op jit(solution)/shard_map/ppermute | solution.py:295
  181.9 16.8 %all-to-all-start.5 = ((bf16[16,2,16,256]{3,2,1,0:T(8,128)(2,1)}), bf16[16,2,16,256]{3,2,1,0:T(8,128)(2,1)S(1)}, u32[]{:S(2)}, u32[]{:S(2)}) async-start(bf16[16,2,16,256]{3,2,1,0:T(8,128)(2,1)} %broadcast_in_dim.37), calls=%async_computation.5 | async-start | bytes 524288 | tf_op jit(solution)/shard_map/all_to_all | solution.py:280
  198.8 9.7 %all-to-all-done.5.gathered_ref = bf16[16,2,16,256]{3,2,1,0:T(8,128)(2,1)S(1)} async-done(((bf16[16,2,16,256]{3,2,1,0:T(8,128)(2,1)}), bf16[16,2,16,256]{3,2,1,0:T(8,128)(2,1)S(1)}, u32[]{:S(2)}, u32[]{:S(2)}) %all-to-all-start.5) | async-done | bytes 262176 | tf_op jit(solution)/shard_map/all_to_all | solution.py:280
  209.3 6.3 %all-to-all-start.6 = ((bf16[8,128,256]{2,1,0:T(8,128)(2,1)}), bf16[8,128,256]{2,1,0:T(8,128)(2,1)S(1)}, u32[]{:S(2)}, u32[]{:S(2)}) async-start(bf16[8,128,256]{2,1,0:T(8,128)(2,1)} %broadcast_in_dim.38), calls=%async_computation.6 | async-start | bytes 1048576 | tf_op jit(solution)/shard_map/all_to_all | solution.py:291
  217.9 7.1 %collective-permute-start.11 = (bf16[32,16,256]{2,1,0:T(8,128)(2,1)S(1)}, bf16[32,16,256]{2,1,0:T(8,128)(2,1)S(1)}, u32[]{:S(2)}, u32[]{:S(2)}) collective-permute-start(bf16[32,16,256]{2,1,0:T(8,128)(2,1)S(1)} %collective-permute-done.9), channel_id=1, source_target_pairs={{0,264},{8,256},{16,280},{24,272},{32,296},{40,288},{48,312},{56,3... | collective-permute-start | bytes 786440 | tf_op jit(solution)/shard_map/ppermute | solution.py:304
  225.0 9.3 %shard_map.69.solved_ref = bf16[256,256]{1,0:T(8,128)(2,1)S(1)} custom-call(s32[3]{0:T(128)S(1)} %pad_add_fusion.meta_ref, f32[6,256]{1,0:T(8,128)S(1)} %copy-done.7, bf16[16,2,16,256]{3,2,1,0:T(8,128)(2,1)S(1)} %all-to-all-done.5.gathered_ref), custom_call_target="tpu_custom_call" | custom-call | flops 536870912 | bytes 4194304 | tf_op jit(solution)/shard_map/pallas_call | solution.py:196
  234.2 11.9 %collective-permute-done.10 = bf16[32,16,256]{2,1,0:T(8,128)(2,1)S(1)} collective-permute-done((bf16[32,16,256]{2,1,0:T(8,128)(2,1)}, bf16[32,16,256]{2,1,0:T(8,128)(2,1)S(1)}, u32[]{:S(2)}, u32[]{:S(2)}) %collective-permute-start.10) | collective-permute-done | bytes 262176 | tf_op jit(solution)/shard_map/ppermute | solution.py:304
  249.4 16.8 %all_to_all.41 = bf16[16,4,16,256]{3,2,1,0:T(8,128)(2,1)S(1)} all-to-all(bf16[16,4,16,256]{3,2,1,0:T(8,128)(2,1)S(1)} %shard_map.70), channel_id=1, replica_groups={{0,16,32,48,64,80,96,112,128,144,160,176,192,208,224,240},{8,24,40,56,7..., dimensions={0} | all-to-all | bytes 1048576 | tf_op jit(solution)/shard_map/all_to_all | solution.py:280
  (66 shorter events, 45.7 us)
Async XLA Ops:
  22.6 13.0 %copy-start.1 = (s32[6,8]{1,0:T(8,128)S(1)}, s32[6,8]{1,0:T(8,128)}, u32[]{:S(2)}) copy-start(s32[6,8]{1,0:T(8,128)} %slots_ref.3) | copy-start | bytes 580
  22.6 44.9 %all-to-all-start.1 = ((bf16[16,12,16,256]{3,2,1,0:T(8,128)(2,1)}), bf16[16,12,16,256]{3,2,1,0:T(8,128)(2,1)}, u32[]{:S(2)}, u32[]{:S(2)}) async-start(bf16[16,12,16,256]{3,2,1,0:T(8,128)(2,1)} %copy.11), calls=%async_computation.1 | async-start | bytes 3145728 | tf_op jit(solution)/shard_map/all_to_all | solution.py:280
  31.5 5.6 %collective-permute-start = (bf16[8,32,256]{2,1,0:T(8,128)(2,1)S(1)}, bf16[8,32,256]{2,1,0:T(8,128)(2,1)S(1)}, u32[]{:S(2)}, u32[]{:S(2)}) collective-permute-start(bf16[8,32,256]{2,1,0:T(8,128)(2,1)S(1)} %shard_map.66), channel_id=1, source_target_pairs={{0,1},{1,0},{2,3},{3,2},{4,5},{5,4},{6,7},{7,6},{8,9},{9,8},{10,11... | collective-permute-start | bytes 393224 | tf_op jit(solution)/shard_map/ppermute | solution.py:295
  37.1 7.1 %collective-permute-start.1 = (bf16[8,32,256]{2,1,0:T(8,128)(2,1)S(1)}, bf16[8,32,256]{2,1,0:T(8,128)(2,1)S(1)}, u32[]{:S(2)}, u32[]{:S(2)}) collective-permute-start(bf16[8,32,256]{2,1,0:T(8,128)(2,1)S(1)} %broadcast_select_fusion), channel_id=1, source_target_pairs={{0,2},{1,3},{2,0},{3,1},{4,6},{5,7},{6,4},{7,5},{8,10},{9,11},{10,... | collective-permute-start | bytes 393224 | tf_op jit(solution)/shard_map/ppermute | solution.py:295
  44.3 7.9 %collective-permute-start.2 = (bf16[8,32,256]{2,1,0:T(8,128)(2,1)S(1)}, bf16[8,32,256]{2,1,0:T(8,128)(2,1)S(1)}, u32[]{:S(2)}, u32[]{:S(2)}) collective-permute-start(bf16[8,32,256]{2,1,0:T(8,128)(2,1)S(1)} %broadcast_select_fusion.1), channel_id=1, source_target_pairs={{0,4},{1,5},{2,6},{3,7},{4,0},{5,1},{6,2},{7,3},{8,12},{9,13},{10,... | collective-permute-start | bytes 393224 | tf_op jit(solution)/shard_map/ppermute | solution.py:295
  52.2 15.4 %collective-permute-start.3 = (bf16[2,32,256]{2,1,0:T(8,128)(2,1)S(1)}, bf16[2,32,256]{2,1,0:T(8,128)(2,1)S(1)}, u32[]{:S(2)}, u32[]{:S(2)}) collective-permute-start(bf16[2,32,256]{2,1,0:T(8,128)(2,1)S(1)} %pad_maximum_fusion.3), channel_id=1, source_target_pairs={{0,8},{8,0},{16,24},{24,16},{32,40},{40,32},{48,56},{56,48},{1,9},... | collective-permute-start | bytes 98312 | tf_op jit(solution)/shard_map/ppermute | solution.py:295
  67.6 28.1 %all-to-all-start.2 = ((bf16[8,384,256]{2,1,0:T(8,128)(2,1)}), bf16[8,384,256]{2,1,0:T(8,128)(2,1)S(1)}, u32[]{:S(2)}, u32[]{:S(2)}) async-start(bf16[8,384,256]{2,1,0:T(8,128)(2,1)} %bitcast.6), calls=%async_computation.2 | async-start | bytes 3145728 | tf_op jit(solution)/shard_map/all_to_all | solution.py:291
  74.9 5.0 %collective-permute-start.4 = (bf16[1,2,32,256]{3,2,1,0:T(8,128)(2,1)S(1)}, bf16[1,2,32,256]{3,2,1,0:T(8,128)(2,1)S(1)}, u32[]{:S(2)}, u32[]{:S(2)}) collective-permute-start(bf16[1,2,32,256]{3,2,1,0:T(8,128)(2,1)S(1)} %bitcast.37), channel_id=1, source_target_pairs={{0,16},{8,24},{16,0},{24,8},{32,48},{40,56},{48,32},{56,40},{1,17}... | collective-permute-start | bytes 98312 | tf_op jit(solution)/shard_map/ppermute | solution.py:295
  79.9 6.5 %collective-permute-start.5 = (bf16[2,2,32,256]{3,2,1,0:T(8,128)(2,1)S(1)}, bf16[2,2,32,256]{3,2,1,0:T(8,128)(2,1)S(1)}, u32[]{:S(2)}, u32[]{:S(2)}) collective-permute-start(bf16[2,2,32,256]{3,2,1,0:T(8,128)(2,1)S(1)} %pad_maximum_fusion.2), channel_id=1, source_target_pairs={{0,32},{8,40},{16,48},{24,56},{32,0},{40,8},{48,16},{56,24},{1,33}... | collective-permute-start | bytes 196616 | tf_op jit(solution)/shard_map/ppermute | solution.py:295
  86.5 6.0 %collective-permute-start.6 = (bf16[4,2,32,256]{3,2,1,0:T(8,128)(2,1)S(1)}, bf16[4,2,32,256]{3,2,1,0:T(8,128)(2,1)S(1)}, u32[]{:S(2)}, u32[]{:S(2)}) collective-permute-start(bf16[4,2,32,256]{3,2,1,0:T(8,128)(2,1)S(1)} %pad_maximum_fusion.1), channel_id=1, source_target_pairs={{0,64},{64,0},{128,192},{192,128},{256,320},{320,256},{384,448},{4... | collective-permute-start | bytes 393224 | tf_op jit(solution)/shard_map/ppermute | solution.py:295
  96.9 4.6 %copy-start.7 = (f32[6,256]{1,0:T(8,128)S(1)}, f32[6,256]{1,0:T(8,128)}, u32[]{:S(2)}) copy-start(f32[6,256]{1,0:T(8,128)} %diag_ref.3) | copy-start | bytes 18436
  96.9 25.5 %all-to-all-start.3 = ((bf16[8,384,256]{2,1,0:T(8,128)(2,1)}), bf16[8,384,256]{2,1,0:T(8,128)(2,1)S(1)}, u32[]{:S(2)}, u32[]{:S(2)}) async-start(bf16[8,384,256]{2,1,0:T(8,128)(2,1)} %broadcast_in_dim.35), calls=%async_computation.3 | async-start | bytes 3145728 | tf_op jit(solution)/shard_map/all_to_all | solution.py:291
  101.5 14.2 %copy-start.3 = (s32[8,96]{1,0:T(8,128)S(1)}, s32[8,96]{1,0:T(8,128)}, u32[]{:S(2)}) copy-start(s32[8,96]{1,0:T(8,128)} %leaf_maps_ref.3) | copy-start | bytes 9220
  101.5 14.2 %copy-start.5 = (s32[8]{0:T(128)S(1)}, s32[8]{0:T(128)}, u32[]{:S(2)}) copy-start(s32[8]{0:T(128)} %tiles_ref.3) | copy-start | bytes 100
  101.6 14.2 %copy-start.6 = (s32[4,128]{1,0:T(4,128)S(1)}, s32[4,128]{1,0:T(4,128)}, u32[]{:S(2)}) copy-start(s32[4,128]{1,0:T(4,128)} %upper_maps_ref.1) | copy-start | bytes 6148
  111.0 11.4 %collective-permute-start.7 = (bf16[256,256]{1,0:T(8,128)(2,1)S(1)}, bf16[256,256]{1,0:T(8,128)(2,1)S(1)}, u32[]{:S(2)}, u32[]{:S(2)}) collective-permute-start(bf16[256,256]{1,0:T(8,128)(2,1)S(1)} %shard_map.67), channel_id=1, source_target_pairs={{0,128},{64,192},{128,0},{192,64},{256,384},{320,448},{384,256},{4... | collective-permute-start | bytes 393224 | tf_op jit(solution)/shard_map/ppermute | solution.py:295
  127.3 21.7 %all-to-all-start.4 = ((bf16[8,288,256]{2,1,0:T(8,128)(2,1)}), bf16[8,288,256]{2,1,0:T(8,128)(2,1)S(1)}, u32[]{:S(2)}, u32[]{:S(2)}) async-start(bf16[8,288,256]{2,1,0:T(8,128)(2,1)} %get-tuple-element.26), calls=%async_computation.4 | async-start | bytes 2359296 | tf_op jit(solution)/shard_map/all_to_all | solution.py:291
  133.2 33.9 %collective-permute-start.9 = (bf16[32,16,256]{2,1,0:T(8,128)(2,1)}, bf16[32,16,256]{2,1,0:T(8,128)(2,1)S(1)}, u32[]{:S(2)}, u32[]{:S(2)}) collective-permute-start(bf16[32,16,256]{2,1,0:T(8,128)(2,1)} %get-tuple-element.33), channel_id=1, source_target_pairs={{0,264},{8,256},{16,280},{24,272},{32,296},{40,288},{48,312},{56,3... | collective-permute-start | bytes 786440 | tf_op jit(solution)/shard_map/ppermute | solution.py:304
  144.5 22.6 %collective-permute-start.8 = (bf16[32,16,256]{2,1,0:T(8,128)(2,1)S(1)}, bf16[32,16,256]{2,1,0:T(8,128)(2,1)}, u32[]{:S(2)}, u32[]{:S(2)}) collective-permute-start(bf16[32,16,256]{2,1,0:T(8,128)(2,1)S(1)} %get-tuple-element.34), channel_id=1, source_target_pairs={{0,256},{8,264},{16,272},{24,280},{32,288},{40,296},{48,304},{56,3... | collective-permute-start | bytes 786440 | tf_op jit(solution)/shard_map/ppermute | solution.py:304
  167.2 14.0 %collective-permute-start.12 = (bf16[160,256]{1,0:T(8,128)(2,1)S(1)}, bf16[160,256]{1,0:T(8,128)(2,1)S(1)}, u32[]{:S(2)}, u32[]{:S(2)}) collective-permute-start(bf16[160,256]{1,0:T(8,128)(2,1)S(1)} %slice.29), channel_id=1, source_target_pairs={{0,8},{8,0},{16,24},{24,16},{32,40},{40,32},{48,56},{56,48},{1,9},... | collective-permute-start | bytes 245768 | tf_op jit(solution)/shard_map/ppermute | solution.py:295
  181.9 26.5 %all-to-all-start.5 = ((bf16[16,2,16,256]{3,2,1,0:T(8,128)(2,1)}), bf16[16,2,16,256]{3,2,1,0:T(8,128)(2,1)S(1)}, u32[]{:S(2)}, u32[]{:S(2)}) async-start(bf16[16,2,16,256]{3,2,1,0:T(8,128)(2,1)} %broadcast_in_dim.37), calls=%async_computation.5 | async-start | bytes 524288 | tf_op jit(solution)/shard_map/all_to_all | solution.py:280
  209.3 39.2 %all-to-all-start.6 = ((bf16[8,128,256]{2,1,0:T(8,128)(2,1)}), bf16[8,128,256]{2,1,0:T(8,128)(2,1)S(1)}, u32[]{:S(2)}, u32[]{:S(2)}) async-start(bf16[8,128,256]{2,1,0:T(8,128)(2,1)} %broadcast_in_dim.38), calls=%async_computation.6 | async-start | bytes 1048576 | tf_op jit(solution)/shard_map/all_to_all | solution.py:291
  215.6 30.6 %collective-permute-start.10 = (bf16[32,16,256]{2,1,0:T(8,128)(2,1)}, bf16[32,16,256]{2,1,0:T(8,128)(2,1)S(1)}, u32[]{:S(2)}, u32[]{:S(2)}) collective-permute-start(bf16[32,16,256]{2,1,0:T(8,128)(2,1)} %collective-permute-done.8), channel_id=1, source_target_pairs={{0,256},{8,264},{16,272},{24,280},{32,288},{40,296},{48,304},{56,3... | collective-permute-start | bytes 786440 | tf_op jit(solution)/shard_map/ppermute | solution.py:304
  217.9 30.6 %collective-permute-start.11 = (bf16[32,16,256]{2,1,0:T(8,128)(2,1)S(1)}, bf16[32,16,256]{2,1,0:T(8,128)(2,1)S(1)}, u32[]{:S(2)}, u32[]{:S(2)}) collective-permute-start(bf16[32,16,256]{2,1,0:T(8,128)(2,1)S(1)} %collective-permute-done.9), channel_id=1, source_target_pairs={{0,264},{8,256},{16,280},{24,272},{32,296},{40,288},{48,312},{56,3... | collective-permute-start | bytes 786440 | tf_op jit(solution)/shard_map/ppermute | solution.py:304
  (3 other events, 2.8 us)

commit v5 on v3

--- a/solution.py
+++ b/solution.py
@@ -48,7 +48,7 @@
             upper_tile = upper_maps_ref[front, lower_tile]
             home_row = (upper_tile >> 2) & 7
             position = ((upper_tile >> 5) << 4) + ((home_row >> 1) << 2) + (upper_tile & 3)
-            position = position + (((home_row & 1) ^ half) << 6)
+            position = position + ((home_row & 1) << 6)
             kept = jnp.logical_and(first + tile < live, lower_tile != 0)
             place_ref[source * 12 + tile] = jnp.where(kept, position, 128)
 
@@ -187,8 +187,8 @@
     return (meta_ref[0] & 1) * 4 + (meta_ref[1] >> 1)
 
 
-def no_place(meta_ref):
-    return jnp.int32(0)
+def quad_place(meta_ref):
+    return (meta_ref[0] & 3) * 4 + (meta_ref[1] >> 1)
 
 
 def solve(front_of, place_of, meta, diagonals, gathered):
@@ -212,9 +212,9 @@
 
 
 def lower_kernel(
-    meta_ref, slots_ref, place_ref, chunks_ref, pivot_ref, solved_ref, keep_ref, send_ref, spread_ref, total_ref, update_ref
+    meta_ref, slots_ref, place_ref, chunks_ref, pivot_ref, solved_ref, halves_ref, share_ref, total_ref, update_ref
 ):
-    level, row, col = meta_ref[0], meta_ref[1], meta_ref[2]
+    level, col = meta_ref[0], meta_ref[2]
     total_ref[...] = jnp.zeros_like(total_ref)
     half = chunks_ref.shape[0] // 2
     for child in range(2):
@@ -232,27 +232,18 @@
             return carry
 
         lax.fori_loop(0, half, one, 0, unroll=4)
-    keep_ref[...] = total_ref[:64]
-    send_ref[...] = total_ref[64:128].astype(BF16)
-    first = row % 2 * 64
-    length, tile = total_ref.shape[1], total_ref.shape[2]
-    for column in range(8):
-        for part in range(2):
-            value = total_ref[part * 64 + column * 8 : part * 64 + column * 8 + 8]
-            spread_ref[column, part * 8 * length : (part + 1) * 8 * length] = value.astype(
-                BF16
-            ).reshape(8 * length, tile)
-        panel_tile = first + 8 * slots_ref[4 + level // 4, column]
-        spread_ref[column, 16 * length : 17 * length] = total_ref[first].astype(BF16)
-        spread_ref[column, 17 * length : 18 * length] = total_ref[panel_tile].astype(BF16)
-
-
-def upper_kernel(meta_ref, slots_ref, keep_ref, sent_ref, pivot_ref, solved_ref, out_ref):
+    halves_ref[0] = total_ref[:64].astype(BF16)
+    halves_ref[1] = total_ref[64:128].astype(BF16)
+    for tile in range(8):
+        share_ref[tile] = total_ref[8 * tile].astype(BF16)
+
+
+def upper_kernel(meta_ref, slots_ref, halves_ref, pivot_ref, solved_ref, out_ref):
     level, row, col = meta_ref[0], meta_ref[1], meta_ref[2]
-    tile = keep_ref.shape[1]
+    tile = halves_ref.shape[2]
     dropped = pivot_slot_of(slots_ref, 4 + level // 4) == col
     update = jnp.dot(pivot_ref[...], solved_ref[...], preferred_element_type=F32)
-    front = keep_ref[...] + sent_ref[...].astype(F32)
+    front = halves_ref[0].astype(F32) + halves_ref[1].astype(F32)
     result = jnp.where(dropped, 0.0, front - update)
     top = jnp.logical_and(
         lax.broadcasted_iota(jnp.int32, result.shape, 0) < tile // 16, row % 2 == 0
@@ -304,6 +295,20 @@
 
 def repeated(value, count):
     return jnp.broadcast_to(value[None], (count,) + value.shape)
+
+
+def own_parts(shares, away, my_tile):
+    for mask in (1, 2, 4):
+        shares = jnp.where(away & mask == 0, shares, swapped(shares, "col", mask))
+    parts = jnp.stack([shares[0], picked(shares, my_tile)])
+    return (parts.astype(F32) + swapped(parts, "row", 1).astype(F32)).astype(BF16)
+
+
+def doubled(parts, steps):
+    gathered = parts[None]
+    for axis, mask in steps:
+        gathered = jnp.concatenate([gathered, swapped(gathered, axis, mask)], axis=0)
+    return gathered
 
 
 def body(leaf_blocks, leaf_tiles, leaf_maps, upper_maps, front_slots, pivot_diag):
@@ -342,18 +347,12 @@
         VMEM,
         moved=2**21,
     )(shares)
-    away = col ^ picked(slots, level // 2)
-    for mask in (1, 2, 4):
-        shares = jnp.where(away & mask == 0, shares, swapped(shares, "col", mask))
-    my_tile = lax.dynamic_slice(front_slots, (level // 2, col), (1, 1))[0, 0]
-    parts = jnp.stack([shares[0], picked(shares, my_tile)])
-    parts = (parts.astype(F32) + swapped(parts, "row", 1).astype(F32)).astype(BF16)
-
+    front = level // 2
+    my_tile = lax.dynamic_slice(front_slots, (front, col), (1, 1))[0, 0]
+    parts = own_parts(shares, col ^ picked(slots, front), my_tile)
     chunks, parts = tied(chunks, parts)
     pieces = over_columns(chunks)
-    gathered = parts[None]
-    for axis, mask in (("row", 2), ("row", 4), ("level", 1)):
-        gathered = jnp.concatenate([gathered, swapped(gathered, axis, mask)], axis=0)
+    gathered = doubled(parts, (("row", 2), ("row", 4), ("level", 1)))
     piece = picked(pieces, picked(slots, level // 4 * 2 + col // 4))
     piece, gathered = tied(piece, gathered)
     pivot_columns = over_columns(repeated(piece, 8)).reshape(192, sixteenth, tile)
@@ -361,12 +360,11 @@
     other = swapped(solved, "level", 2)
     first_child = level // 2 % 2 == 0
     solved = jnp.where(first_child, jnp.stack([solved, other]), jnp.stack([other, solved]))
-    keep, send, spread = call(
+    halves, shares = call(
         lower_kernel,
         (
-            jax.ShapeDtypeStruct((64, sixteenth, tile), F32),
-            jax.ShapeDtypeStruct((64, sixteenth, tile), BF16),
-            jax.ShapeDtypeStruct((8, 18 * sixteenth, tile), BF16),
+            jax.ShapeDtypeStruct((2, 64, sixteenth, tile), BF16),
+            jax.ShapeDtypeStruct((8, sixteenth, tile), BF16),
         ),
         [SMEM, SMEM, SMEM, VMEM, VMEM, VMEM],
         None,
@@ -375,30 +373,33 @@
         moved=2**23,
     )(meta, front_slots, place, chunks.reshape(192, sixteenth, tile), pivot_columns, solved)
 
-    spread = picked(over_columns(spread), picked(slots, 4 + level // 4)).astype(F32)
-    passed = swapped(spread[8 * sixteenth :].astype(BF16), "row", 1).astype(F32)
-    piece = (spread[: 8 * sixteenth] + passed[: 8 * sixteenth]).astype(BF16)
-    parts = (spread[16 * sixteenth :] + passed[8 * sixteenth :]).astype(BF16)
-    gathered = exchange(repeated(parts.reshape(2, sixteenth, tile), 16), 4)
+    halves = lax.all_to_all(
+        halves.reshape(2, -1, tile),
+        "row",
+        split_axis=0,
+        concat_axis=0,
+        axis_index_groups=[[0, 1], [2, 3], [4, 5], [6, 7]],
+        tiled=True,
+    )
+    front = 4 + level // 4
+    my_tile = lax.dynamic_slice(front_slots, (front, col), (1, 1))[0, 0]
+    upper_slot = picked(slots, front)
+    parts = own_parts(shares, col ^ upper_slot, my_tile)
+    halves, parts = tied(halves, parts)
+    rounded = (halves[0].astype(F32) + halves[1].astype(F32)).astype(BF16)
+    piece = picked(over_columns(rounded.reshape(8, -1, tile)), upper_slot)
+    gathered = doubled(parts, (("row", 2), ("row", 4), ("level", 1), ("level", 2)))
     piece, gathered = tied(piece, gathered)
     pivot_columns = over_columns(repeated(piece, 8)).reshape(-1, tile)
-    solved = solve(upper_front, no_place, meta, pivot_diag, gathered)
-    sent = swapped(send, "row", 1)
+    solved = solve(upper_front, quad_place, meta, pivot_diag, gathered)
     finished = call(
         upper_kernel,
         jax.ShapeDtypeStruct((16, 4, sixteenth, tile), BF16),
-        [SMEM, SMEM, VMEM, VMEM, VMEM, VMEM],
+        [SMEM, SMEM, VMEM, VMEM, VMEM],
         VMEM,
         flops=2**28,
         moved=2**22,
-    )(
-        meta,
-        front_slots,
-        keep.reshape(-1, tile),
-        sent.reshape(-1, tile),
-        pivot_columns,
-        solved,
-    )
+    )(meta, front_slots, halves, pivot_columns, solved)
     result = exchange(finished, 4)
     return jnp.swapaxes(result, 0, 1).reshape(1, -1, tile)
 

time: 261 us -> 265 us (1.015)
  the two profiles are of different devices: /device:TPU:128 before, /device:TPU:1 now
where the time goes in v5:
time: 265 us; the launch traced here: 263 us
  starting transfers between devices  134 us (51%)
  waiting for transfers between devices  47.2 us (18%)
  blocking collectives  33.9 us (13%)
  Pallas kernels  28.3 us (11%)
  between operations  9.2 us (3%)
  local copies, waits for them, and re-layouts  8.41 us (3%)
    ppermute x16, starting transfers between devices, swapped(): lax.ppermute(value, axis, [(index, index ^ mask) for index in range(8)])  83.9 us
    ppermute x16, waiting for transfers between devices, swapped(): lax.ppermute(value, axis, [(index, index ^ mask) for index in range(8)])  44.1 us
    all_to_all x2, blocking collectives, exchange(): lax.all_to_all(value, ('level', 'row'), split_axis=0, concat_axis=0, axis...  33.9 us
    all_to_all x4, starting transfers between devices, over_columns(): return lax.all_to_all(value, 'col', split_axis=0, concat_axis=0, tiled=True)  27.8 us
    pallas_call x2, Pallas kernels, solve(): call(functools.partial(solve_kernel, front_of, place_of), jax.ShapeDtypeS...  18.8 us
    all_to_all x1, starting transfers between devices, body(): lax.all_to_all(halves.reshape(2, -1, tile), 'row', split_axis=0, concat_a...  14 us
    all_to_all x1, starting transfers between devices, exchange(): lax.all_to_all(value, ('level', 'row'), split_axis=0, concat_axis=0, axis...  8.69 us
  transfers between devices with their start and end apart: 22, of which 16 were waited for; matrix products, arithmetic and copies ran while one was open for 1% of the time, Pallas kernels for 8%

profile of v5, /device:TPU:1, one launch (start us, length us, event | category | flops | bytes accessed | tf_op | source)
XLA Modules:
  0.0 262.9 jit_solution(2226389971146520243)
XLA Ops:
  3.8 17.5 %all_to_all.40.shares_ref = bf16[8,8,32,256]{3,2,1,0:T(8,128)(2,1)S(1)} all-to-all(bf16[8,8,32,256]{3,2,1,0:T(8,128)(2,1)S(1)} %shard_map.65), channel_id=1, replica_groups={{0,16,32,48,64,80,96,112},{8,24,40,56,72,88,104,120},{128,144,160,176,1..., dimensions={0} | all-to-all | bytes 2097152 | tf_op jit(solution)/shard_map/all_to_all | solution.py:270
  22.7 8.7 %all-to-all-start.1 = ((bf16[16,12,16,256]{3,2,1,0:T(8,128)(2,1)}), bf16[16,12,16,256]{3,2,1,0:T(8,128)(2,1)}, u32[]{:S(2)}, u32[]{:S(2)}) async-start(bf16[16,12,16,256]{3,2,1,0:T(8,128)(2,1)} %copy.11), calls=%async_computation.1 | async-start | bytes 3145728 | tf_op jit(solution)/shard_map/all_to_all | solution.py:270
  31.5 4.0 %collective-permute-start = (bf16[8,32,256]{2,1,0:T(8,128)(2,1)S(1)}, bf16[8,32,256]{2,1,0:T(8,128)(2,1)S(1)}, u32[]{:S(2)}, u32[]{:S(2)}) collective-permute-start(bf16[8,32,256]{2,1,0:T(8,128)(2,1)S(1)} %shard_map.66), channel_id=1, source_target_pairs={{0,1},{1,0},{2,3},{3,2},{4,5},{5,4},{6,7},{7,6},{8,9},{9,8},{10,11... | collective-permute-start | bytes 393224 | tf_op jit(solution)/shard_map/ppermute | solution.py:285
  40.3 3.9 %collective-permute-done.1 = bf16[8,32,256]{2,1,0:T(8,128)(2,1)S(1)} collective-permute-done((bf16[8,32,256]{2,1,0:T(8,128)(2,1)S(1)}, bf16[8,32,256]{2,1,0:T(8,128)(2,1)S(1)}, u32[]{:S(2)}, u32[]{:S(2)}) %collective-permute-start.1) | collective-permute-done | bytes 131104 | tf_op jit(solution)/shard_map/ppermute | solution.py:285
  44.2 4.8 %collective-permute-start.2 = (bf16[8,32,256]{2,1,0:T(8,128)(2,1)S(1)}, bf16[8,32,256]{2,1,0:T(8,128)(2,1)S(1)}, u32[]{:S(2)}, u32[]{:S(2)}) collective-permute-start(bf16[8,32,256]{2,1,0:T(8,128)(2,1)S(1)} %broadcast_select_fusion.1), channel_id=1, source_target_pairs={{0,4},{1,5},{2,6},{3,7},{4,0},{5,1},{6,2},{7,3},{8,12},{9,13},{10,... | collective-permute-start | bytes 393224 | tf_op jit(solution)/shard_map/ppermute | solution.py:285
  52.1 13.4 %collective-permute-start.3 = (bf16[2,32,256]{2,1,0:T(8,128)(2,1)S(1)}, bf16[2,32,256]{2,1,0:T(8,128)(2,1)S(1)}, u32[]{:S(2)}, u32[]{:S(2)}) collective-permute-start(bf16[2,32,256]{2,1,0:T(8,128)(2,1)S(1)} %pad_maximum_fusion.5), channel_id=1, source_target_pairs={{0,8},{8,0},{16,24},{24,16},{32,40},{40,32},{48,56},{56,48},{1,9},... | collective-permute-start | bytes 98312 | tf_op jit(solution)/shard_map/ppermute | solution.py:285
  67.4 7.5 %all-to-all-start.2 = ((bf16[8,384,256]{2,1,0:T(8,128)(2,1)}), bf16[8,384,256]{2,1,0:T(8,128)(2,1)S(1)}, u32[]{:S(2)}, u32[]{:S(2)}) async-start(bf16[8,384,256]{2,1,0:T(8,128)(2,1)} %bitcast.6), calls=%async_computation.2 | async-start | bytes 3145728 | tf_op jit(solution)/shard_map/all_to_all | solution.py:281
  80.0 4.7 %collective-permute-start.5 = (bf16[2,2,32,256]{3,2,1,0:T(8,128)(2,1)S(1)}, bf16[2,2,32,256]{3,2,1,0:T(8,128)(2,1)S(1)}, u32[]{:S(2)}, u32[]{:S(2)}) collective-permute-start(bf16[2,2,32,256]{3,2,1,0:T(8,128)(2,1)S(1)} %pad_maximum_fusion.3), channel_id=1, source_target_pairs={{0,32},{8,40},{16,48},{24,56},{32,0},{40,8},{48,16},{56,24},{1,33}... | collective-permute-start | bytes 196616 | tf_op jit(solution)/shard_map/ppermute | solution.py:285
  96.9 4.6 %all-to-all-start.3 = ((bf16[8,384,256]{2,1,0:T(8,128)(2,1)}), bf16[8,384,256]{2,1,0:T(8,128)(2,1)S(1)}, u32[]{:S(2)}, u32[]{:S(2)}) async-start(bf16[8,384,256]{2,1,0:T(8,128)(2,1)} %broadcast_in_dim.31), calls=%async_computation.3 | async-start | bytes 3145728 | tf_op jit(solution)/shard_map/all_to_all | solution.py:281
  101.5 9.4 %shard_map.67 = bf16[256,256]{1,0:T(8,128)(2,1)S(1)} custom-call(s32[3]{0:T(128)S(1)} %pad_add_fusion.meta_ref, f32[6,256]{1,0:T(8,128)S(1)} %copy-done.7, bf16[8,2,32,256]{3,2,1,0:T(8,128)(2,1)S(1)} %pad_maximum_fusion.gathered_ref), custom_call_target="tpu_custom_call" | custom-call | flops 536870912 | bytes 4194304 | tf_op jit(solution)/shard_map/pallas_call | solution.py:196
  111.0 4.6 %collective-permute-start.7 = (bf16[256,256]{1,0:T(8,128)(2,1)S(1)}, bf16[256,256]{1,0:T(8,128)(2,1)S(1)}, u32[]{:S(2)}, u32[]{:S(2)}) collective-permute-start(bf16[256,256]{1,0:T(8,128)(2,1)S(1)} %shard_map.67), channel_id=1, source_target_pairs={{0,128},{64,192},{128,0},{192,64},{256,384},{320,448},{384,256},{4... | collective-permute-start | bytes 393224 | tf_op jit(solution)/shard_map/ppermute | solution.py:285
  118.5 3.8 %collective-permute-done.7 = bf16[256,256]{1,0:T(8,128)(2,1)S(1)} collective-permute-done((bf16[256,256]{1,0:T(8,128)(2,1)S(1)}, bf16[256,256]{1,0:T(8,128)(2,1)S(1)}, u32[]{:S(2)}, u32[]{:S(2)}) %collective-permute-start.7) | collective-permute-done | bytes 131104 | tf_op jit(solution)/shard_map/ppermute | solution.py:285
  122.3 4.7 %shard_map.68 = (bf16[2,64,16,256]{3,2,1,0:T(8,128)(2,1)}, bf16[8,16,256]{2,1,0:T(8,128)(2,1)S(1)}) custom-call(s32[3]{0:T(128)S(1)} %pad_add_fusion.meta_ref, s32[6,8]{1,0:T(8,128)S(1)} %copy-done.1, s32[192]{0:T(256)S(1)} %shard_map.64.place_ref, bf16[192,16,256]{2,1,0:T(8,128)(2,1)} %bitcast.9.chunks_ref, bf16[192,16,256]{2,1,0:T(8,128)(2,1)S(1)} %bitcast.31, ...), custom_call_target="tpu_custom_call" | custom-call | flops 536870912 | bytes 8388608 | tf_op jit(solution)/shard_map/pallas_call | solution.py:363
  127.0 14.0 %all-to-all-start.4 = ((bf16[2,1024,256]{2,1,0:T(8,128)(2,1)}), bf16[2,1024,256]{2,1,0:T(8,128)(2,1)S(1)}, u32[]{:S(2)}, u32[]{:S(2)}) async-start(bf16[2,1024,256]{2,1,0:T(8,128)(2,1)} %bitcast.16), calls=%async_computation.4 | async-start | bytes 2097152 | tf_op jit(solution)/shard_map/all_to_all | solution.py:376
  149.7 4.9 %collective-permute-start.10 = (bf16[8,16,256]{2,1,0:T(8,128)(2,1)S(1)}, bf16[8,16,256]{2,1,0:T(8,128)(2,1)S(1)}, u32[]{:S(2)}, u32[]{:S(2)}) collective-permute-start(bf16[8,16,256]{2,1,0:T(8,128)(2,1)S(1)} %broadcast_select_fusion.4), channel_id=1, source_target_pairs={{0,4},{1,5},{2,6},{3,7},{4,0},{5,1},{6,2},{7,3},{8,12},{9,13},{10,... | collective-permute-start | bytes 196616 | tf_op jit(solution)/shard_map/ppermute | solution.py:285
  156.6 12.6 %collective-permute-start.11 = (bf16[2,16,256]{2,1,0:T(8,128)(2,1)S(1)}, bf16[2,16,256]{2,1,0:T(8,128)(2,1)S(1)}, u32[]{:S(2)}, u32[]{:S(2)}) collective-permute-start(bf16[2,16,256]{2,1,0:T(8,128)(2,1)S(1)} %pad_maximum_fusion.7), channel_id=1, source_target_pairs={{0,8},{8,0},{16,24},{24,16},{32,40},{40,32},{48,56},{56,48},{1,9},... | collective-permute-start | bytes 49160 | tf_op jit(solution)/shard_map/ppermute | solution.py:285
  170.9 16.2 %collective-permute-done.11 = bf16[2,16,256]{2,1,0:T(8,128)(2,1)S(1)} collective-permute-done((bf16[2,16,256]{2,1,0:T(8,128)(2,1)S(1)}, bf16[2,16,256]{2,1,0:T(8,128)(2,1)S(1)}, u32[]{:S(2)}, u32[]{:S(2)}) %collective-permute-start.11) | collective-permute-done | bytes 16416 | tf_op jit(solution)/shard_map/ppermute | solution.py:285
  191.6 5.1 %collective-permute-start.13 = (bf16[2,2,16,256]{3,2,1,0:T(8,128)(2,1)S(1)}, bf16[2,2,16,256]{3,2,1,0:T(8,128)(2,1)S(1)}, u32[]{:S(2)}, u32[]{:S(2)}) collective-permute-start(bf16[2,2,16,256]{3,2,1,0:T(8,128)(2,1)S(1)} %pad_maximum_fusion.6), channel_id=1, source_target_pairs={{0,32},{8,40},{16,48},{24,56},{32,0},{40,8},{48,16},{56,24},{1,33}... | collective-permute-start | bytes 98312 | tf_op jit(solution)/shard_map/ppermute | solution.py:285
  196.7 10.0 %all-to-all-start.5 = ((bf16[8,128,256]{2,1,0:T(8,128)(2,1)}), bf16[8,128,256]{2,1,0:T(8,128)(2,1)S(1)}, u32[]{:S(2)}, u32[]{:S(2)}) async-start(bf16[8,128,256]{2,1,0:T(8,128)(2,1)} %bitcast.19), calls=%async_computation.5 | async-start | bytes 1048576 | tf_op jit(solution)/shard_map/all_to_all | solution.py:281
  206.8 9.5 %collective-permute-start.14 = (bf16[4,2,16,256]{3,2,1,0:T(8,128)(2,1)S(1)}, bf16[4,2,16,256]{3,2,1,0:T(8,128)(2,1)S(1)}, u32[]{:S(2)}, u32[]{:S(2)}) collective-permute-start(bf16[4,2,16,256]{3,2,1,0:T(8,128)(2,1)S(1)} %pad_maximum_fusion.4), channel_id=1, source_target_pairs={{0,64},{64,0},{128,192},{192,128},{256,320},{320,256},{384,448},{4... | collective-permute-start | bytes 196616 | tf_op jit(solution)/shard_map/ppermute | solution.py:285
  220.5 8.1 %collective-permute-done.15 = bf16[8,2,16,256]{3,2,1,0:T(8,128)(2,1)S(1)} collective-permute-done((bf16[8,2,16,256]{3,2,1,0:T(8,128)(2,1)S(1)}, bf16[8,2,16,256]{3,2,1,0:T(8,128)(2,1)S(1)}, u32[]{:S(2)}, u32[]{:S(2)}) %collective-permute-start.15) | collective-permute-done | bytes 131104 | tf_op jit(solution)/shard_map/ppermute | solution.py:285
  229.5 5.7 %all-to-all-start.6 = ((bf16[8,128,256]{2,1,0:T(8,128)(2,1)}), bf16[8,128,256]{2,1,0:T(8,128)(2,1)S(1)}, u32[]{:S(2)}, u32[]{:S(2)}) async-start(bf16[8,128,256]{2,1,0:T(8,128)(2,1)} %broadcast_in_dim.33), calls=%async_computation.6 | async-start | bytes 1048576 | tf_op jit(solution)/shard_map/all_to_all | solution.py:281
  235.3 9.4 %shard_map.69.solved_ref = bf16[256,256]{1,0:T(8,128)(2,1)S(1)} custom-call(s32[3]{0:T(128)S(1)} %pad_add_fusion.meta_ref, f32[6,256]{1,0:T(8,128)S(1)} %copy-done.7, bf16[16,2,16,256]{3,2,1,0:T(8,128)(2,1)S(1)} %constant_dynamic-update-slice_fusion.gathered_ref), custom_call_target="tpu_custom_call" | custom-call | flops 536870912 | bytes 4194304 | tf_op jit(solution)/shard_map/pallas_call | solution.py:196
  245.7 16.4 %all_to_all.41 = bf16[16,4,16,256]{3,2,1,0:T(8,128)(2,1)S(1)} all-to-all(bf16[16,4,16,256]{3,2,1,0:T(8,128)(2,1)S(1)} %shard_map.70), channel_id=1, replica_groups={{0,16,32,48,64,80,96,112,128,144,160,176,192,208,224,240},{8,24,40,56,7..., dimensions={0} | all-to-all | bytes 1048576 | tf_op jit(solution)/shard_map/all_to_all | solution.py:270
  (80 shorter events, 50.0 us)
Async XLA Ops:
  22.7 44.7 %all-to-all-start.1 = ((bf16[16,12,16,256]{3,2,1,0:T(8,128)(2,1)}), bf16[16,12,16,256]{3,2,1,0:T(8,128)(2,1)}, u32[]{:S(2)}, u32[]{:S(2)}) async-start(bf16[16,12,16,256]{3,2,1,0:T(8,128)(2,1)} %copy.11), calls=%async_computation.1 | async-start | bytes 3145728 | tf_op jit(solution)/shard_map/all_to_all | solution.py:270
  31.5 5.5 %collective-permute-start = (bf16[8,32,256]{2,1,0:T(8,128)(2,1)S(1)}, bf16[8,32,256]{2,1,0:T(8,128)(2,1)S(1)}, u32[]{:S(2)}, u32[]{:S(2)}) collective-permute-start(bf16[8,32,256]{2,1,0:T(8,128)(2,1)S(1)} %shard_map.66), channel_id=1, source_target_pairs={{0,1},{1,0},{2,3},{3,2},{4,5},{5,4},{6,7},{7,6},{8,9},{9,8},{10,11... | collective-permute-start | bytes 393224 | tf_op jit(solution)/shard_map/ppermute | solution.py:285
  37.0 7.1 %collective-permute-start.1 = (bf16[8,32,256]{2,1,0:T(8,128)(2,1)S(1)}, bf16[8,32,256]{2,1,0:T(8,128)(2,1)S(1)}, u32[]{:S(2)}, u32[]{:S(2)}) collective-permute-start(bf16[8,32,256]{2,1,0:T(8,128)(2,1)S(1)} %broadcast_select_fusion), channel_id=1, source_target_pairs={{0,2},{1,3},{2,0},{3,1},{4,6},{5,7},{6,4},{7,5},{8,10},{9,11},{10,... | collective-permute-start | bytes 393224 | tf_op jit(solution)/shard_map/ppermute | solution.py:285
  44.2 7.9 %collective-permute-start.2 = (bf16[8,32,256]{2,1,0:T(8,128)(2,1)S(1)}, bf16[8,32,256]{2,1,0:T(8,128)(2,1)S(1)}, u32[]{:S(2)}, u32[]{:S(2)}) collective-permute-start(bf16[8,32,256]{2,1,0:T(8,128)(2,1)S(1)} %broadcast_select_fusion.1), channel_id=1, source_target_pairs={{0,4},{1,5},{2,6},{3,7},{4,0},{5,1},{6,2},{7,3},{8,12},{9,13},{10,... | collective-permute-start | bytes 393224 | tf_op jit(solution)/shard_map/ppermute | solution.py:285
  52.1 15.3 %collective-permute-start.3 = (bf16[2,32,256]{2,1,0:T(8,128)(2,1)S(1)}, bf16[2,32,256]{2,1,0:T(8,128)(2,1)S(1)}, u32[]{:S(2)}, u32[]{:S(2)}) collective-permute-start(bf16[2,32,256]{2,1,0:T(8,128)(2,1)S(1)} %pad_maximum_fusion.5), channel_id=1, source_target_pairs={{0,8},{8,0},{16,24},{24,16},{32,40},{40,32},{48,56},{56,48},{1,9},... | collective-permute-start | bytes 98312 | tf_op jit(solution)/shard_map/ppermute | solution.py:285
  67.4 28.2 %all-to-all-start.2 = ((bf16[8,384,256]{2,1,0:T(8,128)(2,1)}), bf16[8,384,256]{2,1,0:T(8,128)(2,1)S(1)}, u32[]{:S(2)}, u32[]{:S(2)}) async-start(bf16[8,384,256]{2,1,0:T(8,128)(2,1)} %bitcast.6), calls=%async_computation.2 | async-start | bytes 3145728 | tf_op jit(solution)/shard_map/all_to_all | solution.py:281
  74.9 5.0 %collective-permute-start.4 = (bf16[1,2,32,256]{3,2,1,0:T(8,128)(2,1)S(1)}, bf16[1,2,32,256]{3,2,1,0:T(8,128)(2,1)S(1)}, u32[]{:S(2)}, u32[]{:S(2)}) collective-permute-start(bf16[1,2,32,256]{3,2,1,0:T(8,128)(2,1)S(1)} %bitcast.35), channel_id=1, source_target_pairs={{0,16},{8,24},{16,0},{24,8},{32,48},{40,56},{48,32},{56,40},{1,17}... | collective-permute-start | bytes 98312 | tf_op jit(solution)/shard_map/ppermute | solution.py:285
  80.0 6.5 %collective-permute-start.5 = (bf16[2,2,32,256]{3,2,1,0:T(8,128)(2,1)S(1)}, bf16[2,2,32,256]{3,2,1,0:T(8,128)(2,1)S(1)}, u32[]{:S(2)}, u32[]{:S(2)}) collective-permute-start(bf16[2,2,32,256]{3,2,1,0:T(8,128)(2,1)S(1)} %pad_maximum_fusion.3), channel_id=1, source_target_pairs={{0,32},{8,40},{16,48},{24,56},{32,0},{40,8},{48,16},{56,24},{1,33}... | collective-permute-start | bytes 196616 | tf_op jit(solution)/shard_map/ppermute | solution.py:285
  86.5 6.0 %collective-permute-start.6 = (bf16[4,2,32,256]{3,2,1,0:T(8,128)(2,1)S(1)}, bf16[4,2,32,256]{3,2,1,0:T(8,128)(2,1)S(1)}, u32[]{:S(2)}, u32[]{:S(2)}) collective-permute-start(bf16[4,2,32,256]{3,2,1,0:T(8,128)(2,1)S(1)} %pad_maximum_fusion.1), channel_id=1, source_target_pairs={{0,64},{64,0},{128,192},{192,128},{256,320},{320,256},{384,448},{4... | collective-permute-start | bytes 393224 | tf_op jit(solution)/shard_map/ppermute | solution.py:285
  96.9 25.4 %all-to-all-start.3 = ((bf16[8,384,256]{2,1,0:T(8,128)(2,1)}), bf16[8,384,256]{2,1,0:T(8,128)(2,1)S(1)}, u32[]{:S(2)}, u32[]{:S(2)}) async-start(bf16[8,384,256]{2,1,0:T(8,128)(2,1)} %broadcast_in_dim.31), calls=%async_computation.3 | async-start | bytes 3145728 | tf_op jit(solution)/shard_map/all_to_all | solution.py:281
  101.5 14.1 %copy-start.5 = (s32[8]{0:T(128)S(1)}, s32[8]{0:T(128)}, u32[]{:S(2)}) copy-start(s32[8]{0:T(128)} %tiles_ref.3) | copy-start | bytes 100
  101.5 14.1 %copy-start.6 = (s32[4,128]{1,0:T(4,128)S(1)}, s32[4,128]{1,0:T(4,128)}, u32[]{:S(2)}) copy-start(s32[4,128]{1,0:T(4,128)} %upper_maps_ref.1) | copy-start | bytes 6148
  111.0 11.3 %collective-permute-start.7 = (bf16[256,256]{1,0:T(8,128)(2,1)S(1)}, bf16[256,256]{1,0:T(8,128)(2,1)S(1)}, u32[]{:S(2)}, u32[]{:S(2)}) collective-permute-start(bf16[256,256]{1,0:T(8,128)(2,1)S(1)} %shard_map.67), channel_id=1, source_target_pairs={{0,128},{64,192},{128,0},{192,64},{256,384},{320,448},{384,256},{4... | collective-permute-start | bytes 393224 | tf_op jit(solution)/shard_map/ppermute | solution.py:285
  127.0 60.1 %all-to-all-start.4 = ((bf16[2,1024,256]{2,1,0:T(8,128)(2,1)}), bf16[2,1024,256]{2,1,0:T(8,128)(2,1)S(1)}, u32[]{:S(2)}, u32[]{:S(2)}) async-start(bf16[2,1024,256]{2,1,0:T(8,128)(2,1)} %bitcast.16), calls=%async_computation.4 | async-start | bytes 2097152 | tf_op jit(solution)/shard_map/all_to_all | solution.py:376
  141.0 3.7 %collective-permute-start.8 = (bf16[8,16,256]{2,1,0:T(8,128)(2,1)S(1)}, bf16[8,16,256]{2,1,0:T(8,128)(2,1)S(1)}, u32[]{:S(2)}, u32[]{:S(2)}) collective-permute-start(bf16[8,16,256]{2,1,0:T(8,128)(2,1)S(1)} %get-tuple-element.24), channel_id=1, source_target_pairs={{0,1},{1,0},{2,3},{3,2},{4,5},{5,4},{6,7},{7,6},{8,9},{9,8},{10,11... | collective-permute-start | bytes 196616 | tf_op jit(solution)/shard_map/ppermute | solution.py:285
  144.7 5.0 %collective-permute-start.9 = (bf16[8,16,256]{2,1,0:T(8,128)(2,1)S(1)}, bf16[8,16,256]{2,1,0:T(8,128)(2,1)S(1)}, u32[]{:S(2)}, u32[]{:S(2)}) collective-permute-start(bf16[8,16,256]{2,1,0:T(8,128)(2,1)S(1)} %broadcast_select_fusion.3), channel_id=1, source_target_pairs={{0,2},{1,3},{2,0},{3,1},{4,6},{5,7},{6,4},{7,5},{8,10},{9,11},{10,... | collective-permute-start | bytes 196616 | tf_op jit(solution)/shard_map/ppermute | solution.py:285
  149.7 6.8 %collective-permute-start.10 = (bf16[8,16,256]{2,1,0:T(8,128)(2,1)S(1)}, bf16[8,16,256]{2,1,0:T(8,128)(2,1)S(1)}, u32[]{:S(2)}, u32[]{:S(2)}) collective-permute-start(bf16[8,16,256]{2,1,0:T(8,128)(2,1)S(1)} %broadcast_select_fusion.4), channel_id=1, source_target_pairs={{0,4},{1,5},{2,6},{3,7},{4,0},{5,1},{6,2},{7,3},{8,12},{9,13},{10,... | collective-permute-start | bytes 196616 | tf_op jit(solution)/shard_map/ppermute | solution.py:285
  156.6 30.5 %collective-permute-start.11 = (bf16[2,16,256]{2,1,0:T(8,128)(2,1)S(1)}, bf16[2,16,256]{2,1,0:T(8,128)(2,1)S(1)}, u32[]{:S(2)}, u32[]{:S(2)}) collective-permute-start(bf16[2,16,256]{2,1,0:T(8,128)(2,1)S(1)} %pad_maximum_fusion.7), channel_id=1, source_target_pairs={{0,8},{8,0},{16,24},{24,16},{32,40},{40,32},{48,56},{56,48},{1,9},... | collective-permute-start | bytes 49160 | tf_op jit(solution)/shard_map/ppermute | solution.py:285
  187.1 4.5 %collective-permute-start.12 = (bf16[1,2,16,256]{3,2,1,0:T(8,128)(2,1)S(1)}, bf16[1,2,16,256]{3,2,1,0:T(8,128)(2,1)S(1)}, u32[]{:S(2)}, u32[]{:S(2)}) collective-permute-start(bf16[1,2,16,256]{3,2,1,0:T(8,128)(2,1)S(1)} %bitcast.39), channel_id=1, source_target_pairs={{0,16},{8,24},{16,0},{24,8},{32,48},{40,56},{48,32},{56,40},{1,17}... | collective-permute-start | bytes 49160 | tf_op jit(solution)/shard_map/ppermute | solution.py:285
  191.6 15.2 %collective-permute-start.13 = (bf16[2,2,16,256]{3,2,1,0:T(8,128)(2,1)S(1)}, bf16[2,2,16,256]{3,2,1,0:T(8,128)(2,1)S(1)}, u32[]{:S(2)}, u32[]{:S(2)}) collective-permute-start(bf16[2,2,16,256]{3,2,1,0:T(8,128)(2,1)S(1)} %pad_maximum_fusion.6), channel_id=1, source_target_pairs={{0,32},{8,40},{16,48},{24,56},{32,0},{40,8},{48,16},{56,24},{1,33}... | collective-permute-start | bytes 98312 | tf_op jit(solution)/shard_map/ppermute | solution.py:285
  196.7 31.9 %all-to-all-start.5 = ((bf16[8,128,256]{2,1,0:T(8,128)(2,1)}), bf16[8,128,256]{2,1,0:T(8,128)(2,1)S(1)}, u32[]{:S(2)}, u32[]{:S(2)}) async-start(bf16[8,128,256]{2,1,0:T(8,128)(2,1)} %bitcast.19), calls=%async_computation.5 | async-start | bytes 1048576 | tf_op jit(solution)/shard_map/all_to_all | solution.py:281
  206.8 11.8 %collective-permute-start.14 = (bf16[4,2,16,256]{3,2,1,0:T(8,128)(2,1)S(1)}, bf16[4,2,16,256]{3,2,1,0:T(8,128)(2,1)S(1)}, u32[]{:S(2)}, u32[]{:S(2)}) collective-permute-start(bf16[4,2,16,256]{3,2,1,0:T(8,128)(2,1)S(1)} %pad_maximum_fusion.4), channel_id=1, source_target_pairs={{0,64},{64,0},{128,192},{192,128},{256,320},{320,256},{384,448},{4... | collective-permute-start | bytes 196616 | tf_op jit(solution)/shard_map/ppermute | solution.py:285
  218.6 10.1 %collective-permute-start.15 = (bf16[8,2,16,256]{3,2,1,0:T(8,128)(2,1)S(1)}, bf16[8,2,16,256]{3,2,1,0:T(8,128)(2,1)S(1)}, u32[]{:S(2)}, u32[]{:S(2)}) collective-permute-start(bf16[8,2,16,256]{3,2,1,0:T(8,128)(2,1)S(1)} %pad_maximum_fusion.2), channel_id=1, source_target_pairs={{0,128},{64,192},{128,0},{192,64},{256,384},{320,448},{384,256},{4... | collective-permute-start | bytes 393224 | tf_op jit(solution)/shard_map/ppermute | solution.py:285
  229.5 15.2 %all-to-all-start.6 = ((bf16[8,128,256]{2,1,0:T(8,128)(2,1)}), bf16[8,128,256]{2,1,0:T(8,128)(2,1)S(1)}, u32[]{:S(2)}, u32[]{:S(2)}) async-start(bf16[8,128,256]{2,1,0:T(8,128)(2,1)} %broadcast_in_dim.33), calls=%async_computation.6 | async-start | bytes 1048576 | tf_op jit(solution)/shard_map/all_to_all | solution.py:281
  (6 other events, 34.4 us)

commit v6 on v3

--- a/solution.py
+++ b/solution.py
@@ -294,8 +294,8 @@
     return lax.ppermute(value, axis, [(index, index ^ mask) for index in range(8)])
 
 
-def tied(first, second):
-    return lax.optimization_barrier((first, second))
+def tied(*values):
+    return lax.optimization_barrier(values)
 
 
 def picked(pieces, slot):
@@ -375,7 +375,10 @@
         moved=2**23,
     )(meta, front_slots, place, chunks.reshape(192, sixteenth, tile), pivot_columns, solved)
 
-    spread = picked(over_columns(spread), picked(slots, 4 + level // 4)).astype(F32)
+    sent = swapped(send, "row", 1)
+    spread = picked(over_columns(spread), picked(slots, 4 + level // 4))
+    spread, sent = tied(spread, sent)
+    spread = spread.astype(F32)
     passed = swapped(spread[8 * sixteenth :].astype(BF16), "row", 1).astype(F32)
     piece = (spread[: 8 * sixteenth] + passed[: 8 * sixteenth]).astype(BF16)
     parts = (spread[16 * sixteenth :] + passed[8 * sixteenth :]).astype(BF16)
@@ -383,7 +386,6 @@
     piece, gathered = tied(piece, gathered)
     pivot_columns = over_columns(repeated(piece, 8)).reshape(-1, tile)
     solved = solve(upper_front, no_place, meta, pivot_diag, gathered)
-    sent = swapped(send, "row", 1)
     finished = call(
         upper_kernel,
         jax.ShapeDtypeStruct((16, 4, sixteenth, tile), BF16),

time: 261 us -> 262 us (level)
  the two profiles are of different devices: /device:TPU:128 before, /device:TPU:1 now
where the time goes in v6:
time: 262 us; the launch traced here: 260 us
  starting transfers between devices  114 us (44%)
  waiting for transfers between devices  66.1 us (25%)
  blocking collectives  33.8 us (13%)
  Pallas kernels  28.4 us (11%)
  local copies, waits for them, and re-layouts  9.92 us (4%)
  between operations  6.77 us (3%)
    ppermute x10, starting transfers between devices, swapped(): lax.ppermute(value, axis, [(index, index ^ mask) for index in range(8)])  67.5 us
    ppermute x10, waiting for transfers between devices, swapped(): lax.ppermute(value, axis, [(index, index ^ mask) for index in range(8)])  53.9 us
    all_to_all x2, blocking collectives, exchange(): lax.all_to_all(value, ('level', 'row'), split_axis=0, concat_axis=0, axis...  33.8 us
    all_to_all x4, starting transfers between devices, over_columns(): return lax.all_to_all(value, 'col', split_axis=0, concat_axis=0, tiled=True)  29 us
    pallas_call x2, Pallas kernels, solve(): call(functools.partial(solve_kernel, front_of, place_of), jax.ShapeDtypeS...  18.7 us
    all_to_all x2, starting transfers between devices, exchange(): lax.all_to_all(value, ('level', 'row'), split_axis=0, concat_axis=0, axis...  17.5 us
    all_to_all x2, waiting for transfers between devices, exchange(): lax.all_to_all(value, ('level', 'row'), split_axis=0, concat_axis=0, axis...  8.81 us
  transfers between devices with their start and end apart: 16, of which 13 were waited for; matrix products, arithmetic and copies ran while one was open for 1% of the time, Pallas kernels for 8%

profile of v6, /device:TPU:1, one launch (start us, length us, event | category | flops | bytes accessed | tf_op | source)
XLA Modules:
  0.0 259.6 jit_solution(16667311143180620946)
XLA Ops:
  3.8 17.5 %all_to_all.40.shares_ref = bf16[8,8,32,256]{3,2,1,0:T(8,128)(2,1)S(1)} all-to-all(bf16[8,8,32,256]{3,2,1,0:T(8,128)(2,1)S(1)} %shard_map.65), channel_id=1, replica_groups={{0,16,32,48,64,80,96,112},{8,24,40,56,72,88,104,120},{128,144,160,176,1..., dimensions={0} | all-to-all | bytes 2097152 | tf_op jit(solution)/shard_map/all_to_all | solution.py:279
  22.7 8.7 %all-to-all-start.1 = ((bf16[16,12,16,256]{3,2,1,0:T(8,128)(2,1)}), bf16[16,12,16,256]{3,2,1,0:T(8,128)(2,1)}, u32[]{:S(2)}, u32[]{:S(2)}) async-start(bf16[16,12,16,256]{3,2,1,0:T(8,128)(2,1)} %copy.11), calls=%async_computation.1 | async-start | bytes 3145728 | tf_op jit(solution)/shard_map/all_to_all | solution.py:279
  31.5 4.0 %collective-permute-start = (bf16[8,32,256]{2,1,0:T(8,128)(2,1)S(1)}, bf16[8,32,256]{2,1,0:T(8,128)(2,1)S(1)}, u32[]{:S(2)}, u32[]{:S(2)}) collective-permute-start(bf16[8,32,256]{2,1,0:T(8,128)(2,1)S(1)} %shard_map.66), channel_id=1, source_target_pairs={{0,1},{1,0},{2,3},{3,2},{4,5},{5,4},{6,7},{7,6},{8,9},{9,8},{10,11... | collective-permute-start | bytes 393224 | tf_op jit(solution)/shard_map/ppermute | solution.py:294
  40.4 3.9 %collective-permute-done.1 = bf16[8,32,256]{2,1,0:T(8,128)(2,1)S(1)} collective-permute-done((bf16[8,32,256]{2,1,0:T(8,128)(2,1)S(1)}, bf16[8,32,256]{2,1,0:T(8,128)(2,1)S(1)}, u32[]{:S(2)}, u32[]{:S(2)}) %collective-permute-start.1) | collective-permute-done | bytes 131104 | tf_op jit(solution)/shard_map/ppermute | solution.py:294
  44.3 4.8 %collective-permute-start.2 = (bf16[8,32,256]{2,1,0:T(8,128)(2,1)S(1)}, bf16[8,32,256]{2,1,0:T(8,128)(2,1)S(1)}, u32[]{:S(2)}, u32[]{:S(2)}) collective-permute-start(bf16[8,32,256]{2,1,0:T(8,128)(2,1)S(1)} %broadcast_select_fusion.1), channel_id=1, source_target_pairs={{0,4},{1,5},{2,6},{3,7},{4,0},{5,1},{6,2},{7,3},{8,12},{9,13},{10,... | collective-permute-start | bytes 393224 | tf_op jit(solution)/shard_map/ppermute | solution.py:294
  52.2 13.4 %collective-permute-start.3 = (bf16[2,32,256]{2,1,0:T(8,128)(2,1)S(1)}, bf16[2,32,256]{2,1,0:T(8,128)(2,1)S(1)}, u32[]{:S(2)}, u32[]{:S(2)}) collective-permute-start(bf16[2,32,256]{2,1,0:T(8,128)(2,1)S(1)} %pad_maximum_fusion.3), channel_id=1, source_target_pairs={{0,8},{8,0},{16,24},{24,16},{32,40},{40,32},{48,56},{56,48},{1,9},... | collective-permute-start | bytes 98312 | tf_op jit(solution)/shard_map/ppermute | solution.py:294
  67.6 7.3 %all-to-all-start.2 = ((bf16[8,384,256]{2,1,0:T(8,128)(2,1)}), bf16[8,384,256]{2,1,0:T(8,128)(2,1)S(1)}, u32[]{:S(2)}, u32[]{:S(2)}) async-start(bf16[8,384,256]{2,1,0:T(8,128)(2,1)} %bitcast.6), calls=%async_computation.2 | async-start | bytes 3145728 | tf_op jit(solution)/shard_map/all_to_all | solution.py:290
  74.9 3.4 %collective-permute-start.4 = (bf16[1,2,32,256]{3,2,1,0:T(8,128)(2,1)S(1)}, bf16[1,2,32,256]{3,2,1,0:T(8,128)(2,1)S(1)}, u32[]{:S(2)}, u32[]{:S(2)}) collective-permute-start(bf16[1,2,32,256]{3,2,1,0:T(8,128)(2,1)S(1)} %bitcast.35), channel_id=1, source_target_pairs={{0,16},{8,24},{16,0},{24,8},{32,48},{40,56},{48,32},{56,40},{1,17}... | collective-permute-start | bytes 98312 | tf_op jit(solution)/shard_map/ppermute | solution.py:294
  79.9 4.7 %collective-permute-start.5 = (bf16[2,2,32,256]{3,2,1,0:T(8,128)(2,1)S(1)}, bf16[2,2,32,256]{3,2,1,0:T(8,128)(2,1)S(1)}, u32[]{:S(2)}, u32[]{:S(2)}) collective-permute-start(bf16[2,2,32,256]{3,2,1,0:T(8,128)(2,1)S(1)} %pad_maximum_fusion.2), channel_id=1, source_target_pairs={{0,32},{8,40},{16,48},{24,56},{32,0},{40,8},{48,16},{56,24},{1,33}... | collective-permute-start | bytes 196616 | tf_op jit(solution)/shard_map/ppermute | solution.py:294
  96.9 4.6 %all-to-all-start.3 = ((bf16[8,384,256]{2,1,0:T(8,128)(2,1)}), bf16[8,384,256]{2,1,0:T(8,128)(2,1)S(1)}, u32[]{:S(2)}, u32[]{:S(2)}) async-start(bf16[8,384,256]{2,1,0:T(8,128)(2,1)} %broadcast_in_dim.35), calls=%async_computation.3 | async-start | bytes 3145728 | tf_op jit(solution)/shard_map/all_to_all | solution.py:290
  101.5 9.4 %shard_map.67 = bf16[256,256]{1,0:T(8,128)(2,1)S(1)} custom-call(s32[3]{0:T(128)S(1)} %pad_add_fusion.meta_ref, f32[6,256]{1,0:T(8,128)S(1)} %copy-done.7, bf16[8,2,32,256]{3,2,1,0:T(8,128)(2,1)S(1)} %pad_maximum_fusion.gathered_ref), custom_call_target="tpu_custom_call" | custom-call | flops 536870912 | bytes 4194304 | tf_op jit(solution)/shard_map/pallas_call | solution.py:196
  111.0 4.8 %collective-permute-start.7 = (bf16[256,256]{1,0:T(8,128)(2,1)S(1)}, bf16[256,256]{1,0:T(8,128)(2,1)S(1)}, u32[]{:S(2)}, u32[]{:S(2)}) collective-permute-start(bf16[256,256]{1,0:T(8,128)(2,1)S(1)} %shard_map.67), channel_id=1, source_target_pairs={{0,128},{64,192},{128,0},{192,64},{256,384},{320,448},{384,256},{4... | collective-permute-start | bytes 393224 | tf_op jit(solution)/shard_map/ppermute | solution.py:294
  118.6 3.7 %collective-permute-done.7 = bf16[256,256]{1,0:T(8,128)(2,1)S(1)} collective-permute-done((bf16[256,256]{1,0:T(8,128)(2,1)S(1)}, bf16[256,256]{1,0:T(8,128)(2,1)S(1)}, u32[]{:S(2)}, u32[]{:S(2)}) %collective-permute-start.7) | collective-permute-done | bytes 131104 | tf_op jit(solution)/shard_map/ppermute | solution.py:294
  122.4 4.9 %shard_map.68 = (f32[64,16,256]{2,1,0:T(8,128)S(1)}, bf16[64,16,256]{2,1,0:T(8,128)(2,1)S(1)}, bf16[8,288,256]{2,1,0:T(8,128)(2,1)}) custom-call(s32[3]{0:T(128)S(1)} %pad_add_fusion.meta_ref, s32[6,8]{1,0:T(8,128)S(1)} %copy-done.1, s32[192]{0:T(256)S(1)} %shard_map.64.place_ref, bf16[192,16,256]{2,1,0:T(8,128)(2,1)} %bitcast.9.chunks_ref, ...), custom_call_target="tpu_custom_call" | custom-call | flops 536870912 | bytes 8388608 | tf_op jit(solution)/shard_map/pallas_call | solution.py:364
  127.3 5.0 %all-to-all-start.4 = ((bf16[8,288,256]{2,1,0:T(8,128)(2,1)}), bf16[8,288,256]{2,1,0:T(8,128)(2,1)}, u32[]{:S(2)}, u32[]{:S(2)}) async-start(bf16[8,288,256]{2,1,0:T(8,128)(2,1)} %get-tuple-element.25), calls=%async_computation.4 | async-start | bytes 2359296 | tf_op jit(solution)/shard_map/all_to_all | solution.py:290
  132.3 14.5 %collective-permute-start.8 = (bf16[64,16,256]{2,1,0:T(8,128)(2,1)S(1)}, bf16[64,16,256]{2,1,0:T(8,128)(2,1)S(1)}, u32[]{:S(2)}, u32[]{:S(2)}) collective-permute-start(bf16[64,16,256]{2,1,0:T(8,128)(2,1)S(1)} %get-tuple-element.26), channel_id=1, source_target_pairs={{0,8},{8,0},{16,24},{24,16},{32,40},{40,32},{48,56},{56,48},{1,9},... | collective-permute-start | bytes 1572872 | tf_op jit(solution)/shard_map/ppermute | solution.py:294
  149.9 12.4 %collective-permute-done.8 = bf16[64,16,256]{2,1,0:T(8,128)(2,1)S(1)} collective-permute-done((bf16[64,16,256]{2,1,0:T(8,128)(2,1)S(1)}, bf16[64,16,256]{2,1,0:T(8,128)(2,1)S(1)}, u32[]{:S(2)}, u32[]{:S(2)}) %collective-permute-start.8) | collective-permute-done | bytes 524320 | tf_op jit(solution)/shard_map/ppermute | solution.py:294
  162.3 12.1 %collective-permute-start.9 = (bf16[160,256]{1,0:T(8,128)(2,1)S(1)}, bf16[160,256]{1,0:T(8,128)(2,1)S(1)}, u32[]{:S(2)}, u32[]{:S(2)}) collective-permute-start(bf16[160,256]{1,0:T(8,128)(2,1)S(1)} %slice.21), channel_id=1, source_target_pairs={{0,8},{8,0},{16,24},{24,16},{32,40},{40,32},{48,56},{56,48},{1,9},... | collective-permute-start | bytes 245768 | tf_op jit(solution)/shard_map/ppermute | solution.py:294
  174.4 26.4 %collective-permute-done.9 = bf16[160,256]{1,0:T(8,128)(2,1)S(1)} collective-permute-done((bf16[160,256]{1,0:T(8,128)(2,1)S(1)}, bf16[160,256]{1,0:T(8,128)(2,1)S(1)}, u32[]{:S(2)}, u32[]{:S(2)}) %collective-permute-start.9) | collective-permute-done | bytes 81952 | tf_op jit(solution)/shard_map/ppermute | solution.py:294
  201.6 8.8 %all-to-all-start.5 = ((bf16[16,2,16,256]{3,2,1,0:T(8,128)(2,1)}), bf16[16,2,16,256]{3,2,1,0:T(8,128)(2,1)S(1)}, u32[]{:S(2)}, u32[]{:S(2)}) async-start(bf16[16,2,16,256]{3,2,1,0:T(8,128)(2,1)} %broadcast_in_dim.37), calls=%async_computation.5 | async-start | bytes 524288 | tf_op jit(solution)/shard_map/all_to_all | solution.py:279
  210.4 8.8 %all-to-all-done.5.gathered_ref = bf16[16,2,16,256]{3,2,1,0:T(8,128)(2,1)S(1)} async-done(((bf16[16,2,16,256]{3,2,1,0:T(8,128)(2,1)}), bf16[16,2,16,256]{3,2,1,0:T(8,128)(2,1)S(1)}, u32[]{:S(2)}, u32[]{:S(2)}) %all-to-all-start.5) | async-done | bytes 262176 | tf_op jit(solution)/shard_map/all_to_all | solution.py:279
  220.1 12.0 %all-to-all-start.6 = ((bf16[8,128,256]{2,1,0:T(8,128)(2,1)}), bf16[8,128,256]{2,1,0:T(8,128)(2,1)S(1)}, u32[]{:S(2)}, u32[]{:S(2)}) async-start(bf16[8,128,256]{2,1,0:T(8,128)(2,1)} %broadcast_in_dim.38), calls=%async_computation.6 | async-start | bytes 1048576 | tf_op jit(solution)/shard_map/all_to_all | solution.py:290
  232.1 9.3 %shard_map.69.solved_ref = bf16[256,256]{1,0:T(8,128)(2,1)S(1)} custom-call(s32[3]{0:T(128)S(1)} %pad_add_fusion.meta_ref, f32[6,256]{1,0:T(8,128)S(1)} %copy-done.7, bf16[16,2,16,256]{3,2,1,0:T(8,128)(2,1)S(1)} %all-to-all-done.5.gathered_ref), custom_call_target="tpu_custom_call" | custom-call | flops 536870912 | bytes 4194304 | tf_op jit(solution)/shard_map/pallas_call | solution.py:196
  242.5 16.3 %all_to_all.41 = bf16[16,4,16,256]{3,2,1,0:T(8,128)(2,1)S(1)} all-to-all(bf16[16,4,16,256]{3,2,1,0:T(8,128)(2,1)S(1)} %shard_map.70), channel_id=1, replica_groups={{0,16,32,48,64,80,96,112,128,144,160,176,192,208,224,240},{8,24,40,56,7..., dimensions={0} | all-to-all | bytes 1048576 | tf_op jit(solution)/shard_map/all_to_all | solution.py:279
  (59 shorter events, 32.0 us)
Async XLA Ops:
  0.1 1.4 copy-start
  1.5 0.7 copy-start.2
  2.2 0.7 copy-start.4
  22.6 13.0 %copy-start.1 = (s32[6,8]{1,0:T(8,128)S(1)}, s32[6,8]{1,0:T(8,128)}, u32[]{:S(2)}) copy-start(s32[6,8]{1,0:T(8,128)} %slots_ref.3) | copy-start | bytes 580
  22.7 44.9 %all-to-all-start.1 = ((bf16[16,12,16,256]{3,2,1,0:T(8,128)(2,1)}), bf16[16,12,16,256]{3,2,1,0:T(8,128)(2,1)}, u32[]{:S(2)}, u32[]{:S(2)}) async-start(bf16[16,12,16,256]{3,2,1,0:T(8,128)(2,1)} %copy.11), calls=%async_computation.1 | async-start | bytes 3145728 | tf_op jit(solution)/shard_map/all_to_all | solution.py:279
  31.5 5.6 %collective-permute-start = (bf16[8,32,256]{2,1,0:T(8,128)(2,1)S(1)}, bf16[8,32,256]{2,1,0:T(8,128)(2,1)S(1)}, u32[]{:S(2)}, u32[]{:S(2)}) collective-permute-start(bf16[8,32,256]{2,1,0:T(8,128)(2,1)S(1)} %shard_map.66), channel_id=1, source_target_pairs={{0,1},{1,0},{2,3},{3,2},{4,5},{5,4},{6,7},{7,6},{8,9},{9,8},{10,11... | collective-permute-start | bytes 393224 | tf_op jit(solution)/shard_map/ppermute | solution.py:294
  37.1 7.1 %collective-permute-start.1 = (bf16[8,32,256]{2,1,0:T(8,128)(2,1)S(1)}, bf16[8,32,256]{2,1,0:T(8,128)(2,1)S(1)}, u32[]{:S(2)}, u32[]{:S(2)}) collective-permute-start(bf16[8,32,256]{2,1,0:T(8,128)(2,1)S(1)} %broadcast_select_fusion), channel_id=1, source_target_pairs={{0,2},{1,3},{2,0},{3,1},{4,6},{5,7},{6,4},{7,5},{8,10},{9,11},{10,... | collective-permute-start | bytes 393224 | tf_op jit(solution)/shard_map/ppermute | solution.py:294
  44.3 7.9 %collective-permute-start.2 = (bf16[8,32,256]{2,1,0:T(8,128)(2,1)S(1)}, bf16[8,32,256]{2,1,0:T(8,128)(2,1)S(1)}, u32[]{:S(2)}, u32[]{:S(2)}) collective-permute-start(bf16[8,32,256]{2,1,0:T(8,128)(2,1)S(1)} %broadcast_select_fusion.1), channel_id=1, source_target_pairs={{0,4},{1,5},{2,6},{3,7},{4,0},{5,1},{6,2},{7,3},{8,12},{9,13},{10,... | collective-permute-start | bytes 393224 | tf_op jit(solution)/shard_map/ppermute | solution.py:294
  52.2 15.4 %collective-permute-start.3 = (bf16[2,32,256]{2,1,0:T(8,128)(2,1)S(1)}, bf16[2,32,256]{2,1,0:T(8,128)(2,1)S(1)}, u32[]{:S(2)}, u32[]{:S(2)}) collective-permute-start(bf16[2,32,256]{2,1,0:T(8,128)(2,1)S(1)} %pad_maximum_fusion.3), channel_id=1, source_target_pairs={{0,8},{8,0},{16,24},{24,16},{32,40},{40,32},{48,56},{56,48},{1,9},... | collective-permute-start | bytes 98312 | tf_op jit(solution)/shard_map/ppermute | solution.py:294
  67.6 28.1 %all-to-all-start.2 = ((bf16[8,384,256]{2,1,0:T(8,128)(2,1)}), bf16[8,384,256]{2,1,0:T(8,128)(2,1)S(1)}, u32[]{:S(2)}, u32[]{:S(2)}) async-start(bf16[8,384,256]{2,1,0:T(8,128)(2,1)} %bitcast.6), calls=%async_computation.2 | async-start | bytes 3145728 | tf_op jit(solution)/shard_map/all_to_all | solution.py:290
  74.9 5.0 %collective-permute-start.4 = (bf16[1,2,32,256]{3,2,1,0:T(8,128)(2,1)S(1)}, bf16[1,2,32,256]{3,2,1,0:T(8,128)(2,1)S(1)}, u32[]{:S(2)}, u32[]{:S(2)}) collective-permute-start(bf16[1,2,32,256]{3,2,1,0:T(8,128)(2,1)S(1)} %bitcast.35), channel_id=1, source_target_pairs={{0,16},{8,24},{16,0},{24,8},{32,48},{40,56},{48,32},{56,40},{1,17}... | collective-permute-start | bytes 98312 | tf_op jit(solution)/shard_map/ppermute | solution.py:294
  79.9 6.5 %collective-permute-start.5 = (bf16[2,2,32,256]{3,2,1,0:T(8,128)(2,1)S(1)}, bf16[2,2,32,256]{3,2,1,0:T(8,128)(2,1)S(1)}, u32[]{:S(2)}, u32[]{:S(2)}) collective-permute-start(bf16[2,2,32,256]{3,2,1,0:T(8,128)(2,1)S(1)} %pad_maximum_fusion.2), channel_id=1, source_target_pairs={{0,32},{8,40},{16,48},{24,56},{32,0},{40,8},{48,16},{56,24},{1,33}... | collective-permute-start | bytes 196616 | tf_op jit(solution)/shard_map/ppermute | solution.py:294
  86.5 6.0 %collective-permute-start.6 = (bf16[4,2,32,256]{3,2,1,0:T(8,128)(2,1)S(1)}, bf16[4,2,32,256]{3,2,1,0:T(8,128)(2,1)S(1)}, u32[]{:S(2)}, u32[]{:S(2)}) collective-permute-start(bf16[4,2,32,256]{3,2,1,0:T(8,128)(2,1)S(1)} %pad_maximum_fusion.1), channel_id=1, source_target_pairs={{0,64},{64,0},{128,192},{192,128},{256,320},{320,256},{384,448},{4... | collective-permute-start | bytes 393224 | tf_op jit(solution)/shard_map/ppermute | solution.py:294
  96.9 4.6 %copy-start.7 = (f32[6,256]{1,0:T(8,128)S(1)}, f32[6,256]{1,0:T(8,128)}, u32[]{:S(2)}) copy-start(f32[6,256]{1,0:T(8,128)} %diag_ref.3) | copy-start | bytes 18436
  96.9 25.5 %all-to-all-start.3 = ((bf16[8,384,256]{2,1,0:T(8,128)(2,1)}), bf16[8,384,256]{2,1,0:T(8,128)(2,1)S(1)}, u32[]{:S(2)}, u32[]{:S(2)}) async-start(bf16[8,384,256]{2,1,0:T(8,128)(2,1)} %broadcast_in_dim.35), calls=%async_computation.3 | async-start | bytes 3145728 | tf_op jit(solution)/shard_map/all_to_all | solution.py:290
  101.5 14.2 %copy-start.3 = (s32[8,96]{1,0:T(8,128)S(1)}, s32[8,96]{1,0:T(8,128)}, u32[]{:S(2)}) copy-start(s32[8,96]{1,0:T(8,128)} %leaf_maps_ref.3) | copy-start | bytes 9220
  101.5 14.2 %copy-start.5 = (s32[8]{0:T(128)S(1)}, s32[8]{0:T(128)}, u32[]{:S(2)}) copy-start(s32[8]{0:T(128)} %tiles_ref.3) | copy-start | bytes 100
  101.5 14.2 %copy-start.6 = (s32[4,128]{1,0:T(4,128)S(1)}, s32[4,128]{1,0:T(4,128)}, u32[]{:S(2)}) copy-start(s32[4,128]{1,0:T(4,128)} %upper_maps_ref.1) | copy-start | bytes 6148
  111.0 11.4 %collective-permute-start.7 = (bf16[256,256]{1,0:T(8,128)(2,1)S(1)}, bf16[256,256]{1,0:T(8,128)(2,1)S(1)}, u32[]{:S(2)}, u32[]{:S(2)}) collective-permute-start(bf16[256,256]{1,0:T(8,128)(2,1)S(1)} %shard_map.67), channel_id=1, source_target_pairs={{0,128},{64,192},{128,0},{192,64},{256,384},{320,448},{384,256},{4... | collective-permute-start | bytes 393224 | tf_op jit(solution)/shard_map/ppermute | solution.py:294
  127.3 21.6 %all-to-all-start.4 = ((bf16[8,288,256]{2,1,0:T(8,128)(2,1)}), bf16[8,288,256]{2,1,0:T(8,128)(2,1)}, u32[]{:S(2)}, u32[]{:S(2)}) async-start(bf16[8,288,256]{2,1,0:T(8,128)(2,1)} %get-tuple-element.25), calls=%async_computation.4 | async-start | bytes 2359296 | tf_op jit(solution)/shard_map/all_to_all | solution.py:290
  132.3 29.9 %collective-permute-start.8 = (bf16[64,16,256]{2,1,0:T(8,128)(2,1)S(1)}, bf16[64,16,256]{2,1,0:T(8,128)(2,1)S(1)}, u32[]{:S(2)}, u32[]{:S(2)}) collective-permute-start(bf16[64,16,256]{2,1,0:T(8,128)(2,1)S(1)} %get-tuple-element.26), channel_id=1, source_target_pairs={{0,8},{8,0},{16,24},{24,16},{32,40},{40,32},{48,56},{56,48},{1,9},... | collective-permute-start | bytes 1572872 | tf_op jit(solution)/shard_map/ppermute | solution.py:294
  162.3 38.5 %collective-permute-start.9 = (bf16[160,256]{1,0:T(8,128)(2,1)S(1)}, bf16[160,256]{1,0:T(8,128)(2,1)S(1)}, u32[]{:S(2)}, u32[]{:S(2)}) collective-permute-start(bf16[160,256]{1,0:T(8,128)(2,1)S(1)} %slice.21), channel_id=1, source_target_pairs={{0,8},{8,0},{16,24},{24,16},{32,40},{40,32},{48,56},{56,48},{1,9},... | collective-permute-start | bytes 245768 | tf_op jit(solution)/shard_map/ppermute | solution.py:294
  201.6 17.7 %all-to-all-start.5 = ((bf16[16,2,16,256]{3,2,1,0:T(8,128)(2,1)}), bf16[16,2,16,256]{3,2,1,0:T(8,128)(2,1)S(1)}, u32[]{:S(2)}, u32[]{:S(2)}) async-start(bf16[16,2,16,256]{3,2,1,0:T(8,128)(2,1)} %broadcast_in_dim.37), calls=%async_computation.5 | async-start | bytes 524288 | tf_op jit(solution)/shard_map/all_to_all | solution.py:279
  220.1 21.5 %all-to-all-start.6 = ((bf16[8,128,256]{2,1,0:T(8,128)(2,1)}), bf16[8,128,256]{2,1,0:T(8,128)(2,1)S(1)}, u32[]{:S(2)}, u32[]{:S(2)}) async-start(bf16[8,128,256]{2,1,0:T(8,128)(2,1)} %broadcast_in_dim.38), calls=%async_computation.6 | async-start | bytes 1048576 | tf_op jit(solution)/shard_map/all_to_all | solution.py:290

commit v7 on v6

--- a/solution.py
+++ b/solution.py
@@ -212,7 +212,7 @@
 
 
 def lower_kernel(
-    meta_ref, slots_ref, place_ref, chunks_ref, pivot_ref, solved_ref, keep_ref, send_ref, spread_ref, total_ref, update_ref
+    meta_ref, slots_ref, place_ref, chunks_ref, pivot_ref, solved_ref, keep_ref, send_ref, spread_ref, stay_ref, total_ref, update_ref
 ):
     level, row, col = meta_ref[0], meta_ref[1], meta_ref[2]
     total_ref[...] = jnp.zeros_like(total_ref)
@@ -237,14 +237,12 @@
     first = row % 2 * 64
     length, tile = total_ref.shape[1], total_ref.shape[2]
     for column in range(8):
-        for part in range(2):
+        for part, ref in enumerate((stay_ref, spread_ref)):
             value = total_ref[part * 64 + column * 8 : part * 64 + column * 8 + 8]
-            spread_ref[column, part * 8 * length : (part + 1) * 8 * length] = value.astype(
-                BF16
-            ).reshape(8 * length, tile)
+            ref[column, : 8 * length] = value.astype(BF16).reshape(8 * length, tile)
         panel_tile = first + 8 * slots_ref[4 + level // 4, column]
-        spread_ref[column, 16 * length : 17 * length] = total_ref[first].astype(BF16)
-        spread_ref[column, 17 * length : 18 * length] = total_ref[panel_tile].astype(BF16)
+        spread_ref[column, 8 * length : 9 * length] = total_ref[first].astype(BF16)
+        spread_ref[column, 9 * length : 10 * length] = total_ref[panel_tile].astype(BF16)
 
 
 def upper_kernel(meta_ref, slots_ref, keep_ref, sent_ref, pivot_ref, solved_ref, out_ref):
@@ -361,12 +359,13 @@
     other = swapped(solved, "level", 2)
     first_child = level // 2 % 2 == 0
     solved = jnp.where(first_child, jnp.stack([solved, other]), jnp.stack([other, solved]))
-    keep, send, spread = call(
+    keep, send, spread, stay = call(
         lower_kernel,
         (
             jax.ShapeDtypeStruct((64, sixteenth, tile), F32),
             jax.ShapeDtypeStruct((64, sixteenth, tile), BF16),
-            jax.ShapeDtypeStruct((8, 18 * sixteenth, tile), BF16),
+            jax.ShapeDtypeStruct((8, 10 * sixteenth, tile), BF16),
+            jax.ShapeDtypeStruct((8, 8 * sixteenth, tile), BF16),
         ),
         [SMEM, SMEM, SMEM, VMEM, VMEM, VMEM],
         None,
@@ -375,14 +374,15 @@
         moved=2**23,
     )(meta, front_slots, place, chunks.reshape(192, sixteenth, tile), pivot_columns, solved)
 
+    upper_slot = picked(slots, 4 + level // 4)
+    spread, stay = tied(picked(over_columns(spread), upper_slot), stay)
+    passed = swapped(spread, "row", 1).astype(F32)
+    stay = picked(over_columns(stay), upper_slot)
+    piece = (stay.astype(F32) + passed[: 8 * sixteenth]).astype(BF16)
+    parts = (spread[8 * sixteenth :].astype(F32) + passed[8 * sixteenth :]).astype(BF16)
+    piece, parts = tied(piece, parts)
+    gathered = exchange(repeated(parts.reshape(2, sixteenth, tile), 16), 4)
     sent = swapped(send, "row", 1)
-    spread = picked(over_columns(spread), picked(slots, 4 + level // 4))
-    spread, sent = tied(spread, sent)
-    spread = spread.astype(F32)
-    passed = swapped(spread[8 * sixteenth :].astype(BF16), "row", 1).astype(F32)
-    piece = (spread[: 8 * sixteenth] + passed[: 8 * sixteenth]).astype(BF16)
-    parts = (spread[16 * sixteenth :] + passed[8 * sixteenth :]).astype(BF16)
-    gathered = exchange(repeated(parts.reshape(2, sixteenth, tile), 16), 4)
     piece, gathered = tied(piece, gathered)
     pivot_columns = over_columns(repeated(piece, 8)).reshape(-1, tile)
     solved = solve(upper_front, no_place, meta, pivot_diag, gathered)

time: 262 us -> 261 us (level)
  the two profiles are of different devices: /device:TPU:1 before, /device:TPU:128 now
where the time goes in v7:
time: 261 us; the launch traced here: 260 us
  starting transfers between devices  91.7 us (35%)
  blocking collectives  62.3 us (24%)
  waiting for transfers between devices  61.2 us (23%)
  Pallas kernels  28.3 us (11%)
  local copies, waits for them, and re-layouts  9.04 us (3%)
  between operations  6.98 us (3%)
    all_to_all x2, blocking collectives, exchange(): lax.all_to_all(value, ('level', 'row'), split_axis=0, concat_axis=0, axis...  62.3 us
    ppermute x10, starting transfers between devices, swapped(): lax.ppermute(value, axis, [(index, index ^ mask) for index in range(8)])  58.7 us
    ppermute x10, waiting for transfers between devices, swapped(): lax.ppermute(value, axis, [(index, index ^ mask) for index in range(8)])  38.5 us
    all_to_all x5, starting transfers between devices, over_columns(): return lax.all_to_all(value, 'col', split_axis=0, concat_axis=0, tiled=True)  21.9 us
    pallas_call x2, Pallas kernels, solve(): call(functools.partial(solve_kernel, front_of, place_of), jax.ShapeDtypeS...  18.7 us
    all_to_all x2, waiting for transfers between devices, exchange(): lax.all_to_all(value, ('level', 'row'), split_axis=0, concat_axis=0, axis...  13 us
    all_to_all x2, starting transfers between devices, exchange(): lax.all_to_all(value, ('level', 'row'), split_axis=0, concat_axis=0, axis...  11.1 us
    all_to_all x5, waiting for transfers between devices, over_columns(): return lax.all_to_all(value, 'col', split_axis=0, concat_axis=0, tiled=True)  9.69 us
  transfers between devices with their start and end apart: 17, of which 11 were waited for; matrix products, arithmetic and copies ran while one was open for 1% of the time, Pallas kernels for 8%

profile of v7, /device:TPU:128, one launch (start us, length us, event | category | flops | bytes accessed | tf_op | source)
XLA Modules:
  0.0 259.9 jit_solution(10738062687541140396)
XLA Ops:
  3.8 21.2 %all_to_all.45.shares_ref = bf16[8,8,32,256]{3,2,1,0:T(8,128)(2,1)S(1)} all-to-all(bf16[8,8,32,256]{3,2,1,0:T(8,128)(2,1)S(1)} %shard_map.65), channel_id=1, replica_groups={{0,16,32,48,64,80,96,112},{8,24,40,56,72,88,104,120},{128,144,160,176,1..., dimensions={0} | all-to-all | bytes 2097152 | tf_op jit(solution)/shard_map/all_to_all | solution.py:277
  26.3 5.6 %all-to-all-start.1 = ((bf16[16,12,16,256]{3,2,1,0:T(8,128)(2,1)}), bf16[16,12,16,256]{3,2,1,0:T(8,128)(2,1)}, u32[]{:S(2)}, u32[]{:S(2)}) async-start(bf16[16,12,16,256]{3,2,1,0:T(8,128)(2,1)} %copy.11), calls=%async_computation.1 | async-start | bytes 3145728 | tf_op jit(solution)/shard_map/all_to_all | solution.py:277
  39.1 4.3 %collective-permute-done.1 = bf16[8,32,256]{2,1,0:T(8,128)(2,1)S(1)} collective-permute-done((bf16[8,32,256]{2,1,0:T(8,128)(2,1)S(1)}, bf16[8,32,256]{2,1,0:T(8,128)(2,1)S(1)}, u32[]{:S(2)}, u32[]{:S(2)}) %collective-permute-start.1) | collective-permute-done | bytes 131104 | tf_op jit(solution)/shard_map/ppermute | solution.py:292
  43.4 5.1 %collective-permute-start.2 = (bf16[8,32,256]{2,1,0:T(8,128)(2,1)S(1)}, bf16[8,32,256]{2,1,0:T(8,128)(2,1)S(1)}, u32[]{:S(2)}, u32[]{:S(2)}) collective-permute-start(bf16[8,32,256]{2,1,0:T(8,128)(2,1)S(1)} %broadcast_select_fusion.1), channel_id=1, source_target_pairs={{0,4},{1,5},{2,6},{3,7},{4,0},{5,1},{6,2},{7,3},{8,12},{9,13},{10,... | collective-permute-start | bytes 393224 | tf_op jit(solution)/shard_map/ppermute | solution.py:292
  52.1 8.9 %collective-permute-start.3 = (bf16[2,32,256]{2,1,0:T(8,128)(2,1)S(1)}, bf16[2,32,256]{2,1,0:T(8,128)(2,1)S(1)}, u32[]{:S(2)}, u32[]{:S(2)}) collective-permute-start(bf16[2,32,256]{2,1,0:T(8,128)(2,1)S(1)} %pad_maximum_fusion.3), channel_id=1, source_target_pairs={{0,8},{8,0},{16,24},{24,16},{32,40},{40,32},{48,56},{56,48},{1,9},... | collective-permute-start | bytes 98312 | tf_op jit(solution)/shard_map/ppermute | solution.py:292
  61.0 5.7 %collective-permute-done.3 = bf16[2,32,256]{2,1,0:T(8,128)(2,1)S(1)} collective-permute-done((bf16[2,32,256]{2,1,0:T(8,128)(2,1)S(1)}, bf16[2,32,256]{2,1,0:T(8,128)(2,1)S(1)}, u32[]{:S(2)}, u32[]{:S(2)}) %collective-permute-start.3) | collective-permute-done | bytes 32800 | tf_op jit(solution)/shard_map/ppermute | solution.py:292
  66.7 4.5 %all-to-all-start.2 = ((bf16[8,384,256]{2,1,0:T(8,128)(2,1)}), bf16[8,384,256]{2,1,0:T(8,128)(2,1)S(1)}, u32[]{:S(2)}, u32[]{:S(2)}) async-start(bf16[8,384,256]{2,1,0:T(8,128)(2,1)} %bitcast.6), calls=%async_computation.2 | async-start | bytes 3145728 | tf_op jit(solution)/shard_map/all_to_all | solution.py:288
  77.4 5.3 %collective-permute-start.5 = (bf16[2,2,32,256]{3,2,1,0:T(8,128)(2,1)S(1)}, bf16[2,2,32,256]{3,2,1,0:T(8,128)(2,1)S(1)}, u32[]{:S(2)}, u32[]{:S(2)}) collective-permute-start(bf16[2,2,32,256]{3,2,1,0:T(8,128)(2,1)S(1)} %pad_maximum_fusion.2), channel_id=1, source_target_pairs={{0,32},{8,40},{16,48},{24,56},{32,0},{40,8},{48,16},{56,24},{1,33}... | collective-permute-start | bytes 196616 | tf_op jit(solution)/shard_map/ppermute | solution.py:292
  85.1 6.5 %collective-permute-start.6 = (bf16[4,2,32,256]{3,2,1,0:T(8,128)(2,1)S(1)}, bf16[4,2,32,256]{3,2,1,0:T(8,128)(2,1)S(1)}, u32[]{:S(2)}, u32[]{:S(2)}) collective-permute-start(bf16[4,2,32,256]{3,2,1,0:T(8,128)(2,1)S(1)} %pad_maximum_fusion.1), channel_id=1, source_target_pairs={{0,64},{64,0},{128,192},{192,128},{256,320},{320,256},{384,448},{4... | collective-permute-start | bytes 393224 | tf_op jit(solution)/shard_map/ppermute | solution.py:292
  95.9 4.9 %all-to-all-start.3 = ((bf16[8,384,256]{2,1,0:T(8,128)(2,1)}), bf16[8,384,256]{2,1,0:T(8,128)(2,1)S(1)}, u32[]{:S(2)}, u32[]{:S(2)}) async-start(bf16[8,384,256]{2,1,0:T(8,128)(2,1)} %broadcast_in_dim.35), calls=%async_computation.3 | async-start | bytes 3145728 | tf_op jit(solution)/shard_map/all_to_all | solution.py:288
  100.8 9.4 %shard_map.67 = bf16[256,256]{1,0:T(8,128)(2,1)S(1)} custom-call(s32[3]{0:T(128)S(1)} %pad_add_fusion.meta_ref, f32[6,256]{1,0:T(8,128)S(1)} %copy-done.7, bf16[8,2,32,256]{3,2,1,0:T(8,128)(2,1)S(1)} %pad_maximum_fusion.gathered_ref), custom_call_target="tpu_custom_call" | custom-call | flops 536870912 | bytes 4194304 | tf_op jit(solution)/shard_map/pallas_call | solution.py:196
  110.2 5.7 %collective-permute-start.7 = (bf16[256,256]{1,0:T(8,128)(2,1)S(1)}, bf16[256,256]{1,0:T(8,128)(2,1)S(1)}, u32[]{:S(2)}, u32[]{:S(2)}) collective-permute-start(bf16[256,256]{1,0:T(8,128)(2,1)S(1)} %shard_map.67), channel_id=1, source_target_pairs={{0,128},{64,192},{128,0},{192,64},{256,384},{320,448},{384,256},{4... | collective-permute-start | bytes 393224 | tf_op jit(solution)/shard_map/ppermute | solution.py:292
  122.9 4.8 %shard_map.68 = (f32[64,16,256]{2,1,0:T(8,128)S(1)}, bf16[64,16,256]{2,1,0:T(8,128)(2,1)S(1)}, bf16[8,160,256]{2,1,0:T(8,128)(2,1)}, bf16[8,128,256]{2,1,0:T(8,128)(2,1)}) custom-call(s32[3]{0:T(128)S(1)} %pad_add_fusion.meta_ref, s32[6,8]{1,0:T(8,128)S(1)} %copy-done.1, s32[192]{0:T(256)S(1)} %shard_map.64.place_ref, ...), custom_call_target="tpu_custom_call" | custom-call | flops 536870912 | bytes 8388608 | tf_op jit(solution)/shard_map/pallas_call | solution.py:362
  127.8 4.7 %all-to-all-start.4 = ((bf16[8,160,256]{2,1,0:T(8,128)(2,1)}), bf16[8,160,256]{2,1,0:T(8,128)(2,1)S(1)}, u32[]{:S(2)}, u32[]{:S(2)}) async-start(bf16[8,160,256]{2,1,0:T(8,128)(2,1)} %get-tuple-element.29), calls=%async_computation.4 | async-start | bytes 1310720 | tf_op jit(solution)/shard_map/all_to_all | solution.py:288
  134.5 9.7 %all-to-all-done.4 = bf16[8,160,256]{2,1,0:T(8,128)(2,1)S(1)} async-done(((bf16[8,160,256]{2,1,0:T(8,128)(2,1)}), bf16[8,160,256]{2,1,0:T(8,128)(2,1)S(1)}, u32[]{:S(2)}, u32[]{:S(2)}) %all-to-all-start.4) | async-done | bytes 655392 | tf_op jit(solution)/shard_map/all_to_all | solution.py:288
  147.7 8.5 %collective-permute-start.9 = (bf16[160,256]{1,0:T(8,128)(2,1)S(1)}, bf16[160,256]{1,0:T(8,128)(2,1)S(1)}, u32[]{:S(2)}, u32[]{:S(2)}) collective-permute-start(bf16[160,256]{1,0:T(8,128)(2,1)S(1)} %dynamic-slice_bitcast_fusion.1), channel_id=1, source_target_pairs={{0,8},{8,0},{16,24},{24,16},{32,40},{40,32},{48,56},{56,48},{1,9},... | collective-permute-start | bytes 245768 | tf_op jit(solution)/shard_map/ppermute | solution.py:292
  156.2 9.4 %collective-permute-done.9 = bf16[160,256]{1,0:T(8,128)(2,1)S(1)} collective-permute-done((bf16[160,256]{1,0:T(8,128)(2,1)S(1)}, bf16[160,256]{1,0:T(8,128)(2,1)S(1)}, u32[]{:S(2)}, u32[]{:S(2)}) %collective-permute-start.9) | collective-permute-done | bytes 81952 | tf_op jit(solution)/shard_map/ppermute | solution.py:292
  166.4 5.4 %all-to-all-start.6 = ((bf16[16,2,16,256]{3,2,1,0:T(8,128)(2,1)}), bf16[16,2,16,256]{3,2,1,0:T(8,128)(2,1)S(1)}, u32[]{:S(2)}, u32[]{:S(2)}) async-start(bf16[16,2,16,256]{3,2,1,0:T(8,128)(2,1)} %broadcast_in_dim.37), calls=%async_computation.6 | async-start | bytes 524288 | tf_op jit(solution)/shard_map/all_to_all | solution.py:277
  171.8 9.1 %collective-permute-start.8 = (bf16[64,16,256]{2,1,0:T(8,128)(2,1)S(1)}, bf16[64,16,256]{2,1,0:T(8,128)(2,1)S(1)}, u32[]{:S(2)}, u32[]{:S(2)}) collective-permute-start(bf16[64,16,256]{2,1,0:T(8,128)(2,1)S(1)} %get-tuple-element.28), channel_id=1, source_target_pairs={{0,8},{8,0},{16,24},{24,16},{32,40},{40,32},{48,56},{56,48},{1,9},... | collective-permute-start | bytes 1572872 | tf_op jit(solution)/shard_map/ppermute | solution.py:292
  180.9 13.0 %all-to-all-done.6.gathered_ref = bf16[16,2,16,256]{3,2,1,0:T(8,128)(2,1)S(1)} async-done(((bf16[16,2,16,256]{3,2,1,0:T(8,128)(2,1)}), bf16[16,2,16,256]{3,2,1,0:T(8,128)(2,1)S(1)}, u32[]{:S(2)}, u32[]{:S(2)}) %all-to-all-start.6) | async-done | bytes 262176 | tf_op jit(solution)/shard_map/all_to_all | solution.py:277
  194.7 4.4 %all-to-all-start.7 = ((bf16[8,128,256]{2,1,0:T(8,128)(2,1)}), bf16[8,128,256]{2,1,0:T(8,128)(2,1)S(1)}, u32[]{:S(2)}, u32[]{:S(2)}) async-start(bf16[8,128,256]{2,1,0:T(8,128)(2,1)} %broadcast_in_dim.38), calls=%async_computation.7 | async-start | bytes 1048576 | tf_op jit(solution)/shard_map/all_to_all | solution.py:288
  199.1 9.3 %shard_map.69.solved_ref = bf16[256,256]{1,0:T(8,128)(2,1)S(1)} custom-call(s32[3]{0:T(128)S(1)} %pad_add_fusion.meta_ref, f32[6,256]{1,0:T(8,128)S(1)} %copy-done.7, bf16[16,2,16,256]{3,2,1,0:T(8,128)(2,1)S(1)} %all-to-all-done.6.gathered_ref), custom_call_target="tpu_custom_call" | custom-call | flops 536870912 | bytes 4194304 | tf_op jit(solution)/shard_map/pallas_call | solution.py:196
  208.4 8.7 %collective-permute-done.8 = bf16[64,16,256]{2,1,0:T(8,128)(2,1)S(1)} collective-permute-done((bf16[64,16,256]{2,1,0:T(8,128)(2,1)S(1)}, bf16[64,16,256]{2,1,0:T(8,128)(2,1)S(1)}, u32[]{:S(2)}, u32[]{:S(2)}) %collective-permute-start.8) | collective-permute-done | bytes 524320 | tf_op jit(solution)/shard_map/ppermute | solution.py:292
  218.0 41.0 %all_to_all.46 = bf16[16,4,16,256]{3,2,1,0:T(8,128)(2,1)S(1)} all-to-all(bf16[16,4,16,256]{3,2,1,0:T(8,128)(2,1)S(1)} %shard_map.70), channel_id=1, replica_groups={{0,16,32,48,64,80,96,112,128,144,160,176,192,208,224,240},{8,24,40,56,7..., dimensions={0} | all-to-all | bytes 1048576 | tf_op jit(solution)/shard_map/all_to_all | solution.py:277
  (59 shorter events, 37.7 us)
Async XLA Ops:
  0.1 1.4 copy-start
  1.5 0.7 copy-start.2
  26.3 7.8 %copy-start.1 = (s32[6,8]{1,0:T(8,128)S(1)}, s32[6,8]{1,0:T(8,128)}, u32[]{:S(2)}) copy-start(s32[6,8]{1,0:T(8,128)} %slots_ref.3) | copy-start | bytes 580
  26.3 40.4 %all-to-all-start.1 = ((bf16[16,12,16,256]{3,2,1,0:T(8,128)(2,1)}), bf16[16,12,16,256]{3,2,1,0:T(8,128)(2,1)}, u32[]{:S(2)}, u32[]{:S(2)}) async-start(bf16[16,12,16,256]{3,2,1,0:T(8,128)(2,1)} %copy.11), calls=%async_computation.1 | async-start | bytes 3145728 | tf_op jit(solution)/shard_map/all_to_all | solution.py:277
  32.1 3.4 %collective-permute-start = (bf16[8,32,256]{2,1,0:T(8,128)(2,1)S(1)}, bf16[8,32,256]{2,1,0:T(8,128)(2,1)S(1)}, u32[]{:S(2)}, u32[]{:S(2)}) collective-permute-start(bf16[8,32,256]{2,1,0:T(8,128)(2,1)S(1)} %shard_map.66), channel_id=1, source_target_pairs={{0,1},{1,0},{2,3},{3,2},{4,5},{5,4},{6,7},{7,6},{8,9},{9,8},{10,11... | collective-permute-start | bytes 393224 | tf_op jit(solution)/shard_map/ppermute | solution.py:292
  35.6 7.8 %collective-permute-start.1 = (bf16[8,32,256]{2,1,0:T(8,128)(2,1)S(1)}, bf16[8,32,256]{2,1,0:T(8,128)(2,1)S(1)}, u32[]{:S(2)}, u32[]{:S(2)}) collective-permute-start(bf16[8,32,256]{2,1,0:T(8,128)(2,1)S(1)} %broadcast_select_fusion), channel_id=1, source_target_pairs={{0,2},{1,3},{2,0},{3,1},{4,6},{5,7},{6,4},{7,5},{8,10},{9,11},{10,... | collective-permute-start | bytes 393224 | tf_op jit(solution)/shard_map/ppermute | solution.py:292
  43.4 8.6 %collective-permute-start.2 = (bf16[8,32,256]{2,1,0:T(8,128)(2,1)S(1)}, bf16[8,32,256]{2,1,0:T(8,128)(2,1)S(1)}, u32[]{:S(2)}, u32[]{:S(2)}) collective-permute-start(bf16[8,32,256]{2,1,0:T(8,128)(2,1)S(1)} %broadcast_select_fusion.1), channel_id=1, source_target_pairs={{0,4},{1,5},{2,6},{3,7},{4,0},{5,1},{6,2},{7,3},{8,12},{9,13},{10,... | collective-permute-start | bytes 393224 | tf_op jit(solution)/shard_map/ppermute | solution.py:292
  52.1 14.6 %collective-permute-start.3 = (bf16[2,32,256]{2,1,0:T(8,128)(2,1)S(1)}, bf16[2,32,256]{2,1,0:T(8,128)(2,1)S(1)}, u32[]{:S(2)}, u32[]{:S(2)}) collective-permute-start(bf16[2,32,256]{2,1,0:T(8,128)(2,1)S(1)} %pad_maximum_fusion.3), channel_id=1, source_target_pairs={{0,8},{8,0},{16,24},{24,16},{32,40},{40,32},{48,56},{56,48},{1,9},... | collective-permute-start | bytes 98312 | tf_op jit(solution)/shard_map/ppermute | solution.py:292
  66.7 27.9 %all-to-all-start.2 = ((bf16[8,384,256]{2,1,0:T(8,128)(2,1)}), bf16[8,384,256]{2,1,0:T(8,128)(2,1)S(1)}, u32[]{:S(2)}, u32[]{:S(2)}) async-start(bf16[8,384,256]{2,1,0:T(8,128)(2,1)} %bitcast.6), calls=%async_computation.2 | async-start | bytes 3145728 | tf_op jit(solution)/shard_map/all_to_all | solution.py:288
  71.2 6.2 %collective-permute-start.4 = (bf16[1,2,32,256]{3,2,1,0:T(8,128)(2,1)S(1)}, bf16[1,2,32,256]{3,2,1,0:T(8,128)(2,1)S(1)}, u32[]{:S(2)}, u32[]{:S(2)}) collective-permute-start(bf16[1,2,32,256]{3,2,1,0:T(8,128)(2,1)S(1)} %bitcast.38), channel_id=1, source_target_pairs={{0,16},{8,24},{16,0},{24,8},{32,48},{40,56},{48,32},{56,40},{1,17}... | collective-permute-start | bytes 98312 | tf_op jit(solution)/shard_map/ppermute | solution.py:292
  77.4 7.7 %collective-permute-start.5 = (bf16[2,2,32,256]{3,2,1,0:T(8,128)(2,1)S(1)}, bf16[2,2,32,256]{3,2,1,0:T(8,128)(2,1)S(1)}, u32[]{:S(2)}, u32[]{:S(2)}) collective-permute-start(bf16[2,2,32,256]{3,2,1,0:T(8,128)(2,1)S(1)} %pad_maximum_fusion.2), channel_id=1, source_target_pairs={{0,32},{8,40},{16,48},{24,56},{32,0},{40,8},{48,16},{56,24},{1,33}... | collective-permute-start | bytes 196616 | tf_op jit(solution)/shard_map/ppermute | solution.py:292
  85.1 9.4 %collective-permute-start.6 = (bf16[4,2,32,256]{3,2,1,0:T(8,128)(2,1)S(1)}, bf16[4,2,32,256]{3,2,1,0:T(8,128)(2,1)S(1)}, u32[]{:S(2)}, u32[]{:S(2)}) collective-permute-start(bf16[4,2,32,256]{3,2,1,0:T(8,128)(2,1)S(1)} %pad_maximum_fusion.1), channel_id=1, source_target_pairs={{0,64},{64,0},{128,192},{192,128},{256,320},{320,256},{384,448},{4... | collective-permute-start | bytes 393224 | tf_op jit(solution)/shard_map/ppermute | solution.py:292
  95.9 4.9 %copy-start.7 = (f32[6,256]{1,0:T(8,128)S(1)}, f32[6,256]{1,0:T(8,128)}, u32[]{:S(2)}) copy-start(f32[6,256]{1,0:T(8,128)} %diag_ref.3) | copy-start | bytes 18436
  95.9 27.1 %all-to-all-start.3 = ((bf16[8,384,256]{2,1,0:T(8,128)(2,1)}), bf16[8,384,256]{2,1,0:T(8,128)(2,1)S(1)}, u32[]{:S(2)}, u32[]{:S(2)}) async-start(bf16[8,384,256]{2,1,0:T(8,128)(2,1)} %broadcast_in_dim.35), calls=%async_computation.3 | async-start | bytes 3145728 | tf_op jit(solution)/shard_map/all_to_all | solution.py:288
  100.8 15.2 %copy-start.3 = (s32[8,96]{1,0:T(8,128)S(1)}, s32[8,96]{1,0:T(8,128)}, u32[]{:S(2)}) copy-start(s32[8,96]{1,0:T(8,128)} %leaf_maps_ref.3) | copy-start | bytes 9220
  100.8 15.2 %copy-start.5 = (s32[8]{0:T(128)S(1)}, s32[8]{0:T(128)}, u32[]{:S(2)}) copy-start(s32[8]{0:T(128)} %tiles_ref.3) | copy-start | bytes 100
  100.8 15.2 %copy-start.6 = (s32[4,128]{1,0:T(4,128)S(1)}, s32[4,128]{1,0:T(4,128)}, u32[]{:S(2)}) copy-start(s32[4,128]{1,0:T(4,128)} %upper_maps_ref.1) | copy-start | bytes 6148
  110.2 12.6 %collective-permute-start.7 = (bf16[256,256]{1,0:T(8,128)(2,1)S(1)}, bf16[256,256]{1,0:T(8,128)(2,1)S(1)}, u32[]{:S(2)}, u32[]{:S(2)}) collective-permute-start(bf16[256,256]{1,0:T(8,128)(2,1)S(1)} %shard_map.67), channel_id=1, source_target_pairs={{0,128},{64,192},{128,0},{192,64},{256,384},{320,448},{384,256},{4... | collective-permute-start | bytes 393224 | tf_op jit(solution)/shard_map/ppermute | solution.py:292
  127.8 16.4 %all-to-all-start.4 = ((bf16[8,160,256]{2,1,0:T(8,128)(2,1)}), bf16[8,160,256]{2,1,0:T(8,128)(2,1)S(1)}, u32[]{:S(2)}, u32[]{:S(2)}) async-start(bf16[8,160,256]{2,1,0:T(8,128)(2,1)} %get-tuple-element.29), calls=%async_computation.4 | async-start | bytes 1310720 | tf_op jit(solution)/shard_map/all_to_all | solution.py:288
  144.2 21.4 %all-to-all-start.5 = ((bf16[8,128,256]{2,1,0:T(8,128)(2,1)}), bf16[8,128,256]{2,1,0:T(8,128)(2,1)S(1)}, u32[]{:S(2)}, u32[]{:S(2)}) async-start(bf16[8,128,256]{2,1,0:T(8,128)(2,1)} %get-tuple-element.31), calls=%async_computation.5 | async-start | bytes 1048576 | tf_op jit(solution)/shard_map/all_to_all | solution.py:288
  147.7 17.9 %collective-permute-start.9 = (bf16[160,256]{1,0:T(8,128)(2,1)S(1)}, bf16[160,256]{1,0:T(8,128)(2,1)S(1)}, u32[]{:S(2)}, u32[]{:S(2)}) collective-permute-start(bf16[160,256]{1,0:T(8,128)(2,1)S(1)} %dynamic-slice_bitcast_fusion.1), channel_id=1, source_target_pairs={{0,8},{8,0},{16,24},{24,16},{32,40},{40,32},{48,56},{56,48},{1,9},... | collective-permute-start | bytes 245768 | tf_op jit(solution)/shard_map/ppermute | solution.py:292
  166.4 27.5 %all-to-all-start.6 = ((bf16[16,2,16,256]{3,2,1,0:T(8,128)(2,1)}), bf16[16,2,16,256]{3,2,1,0:T(8,128)(2,1)S(1)}, u32[]{:S(2)}, u32[]{:S(2)}) async-start(bf16[16,2,16,256]{3,2,1,0:T(8,128)(2,1)} %broadcast_in_dim.37), calls=%async_computation.6 | async-start | bytes 524288 | tf_op jit(solution)/shard_map/all_to_all | solution.py:277
  171.8 45.3 %collective-permute-start.8 = (bf16[64,16,256]{2,1,0:T(8,128)(2,1)S(1)}, bf16[64,16,256]{2,1,0:T(8,128)(2,1)S(1)}, u32[]{:S(2)}, u32[]{:S(2)}) collective-permute-start(bf16[64,16,256]{2,1,0:T(8,128)(2,1)S(1)} %get-tuple-element.28), channel_id=1, source_target_pairs={{0,8},{8,0},{16,24},{24,16},{32,40},{40,32},{48,56},{56,48},{1,9},... | collective-permute-start | bytes 1572872 | tf_op jit(solution)/shard_map/ppermute | solution.py:292
  194.7 22.3 %all-to-all-start.7 = ((bf16[8,128,256]{2,1,0:T(8,128)(2,1)}), bf16[8,128,256]{2,1,0:T(8,128)(2,1)S(1)}, u32[]{:S(2)}, u32[]{:S(2)}) async-start(bf16[8,128,256]{2,1,0:T(8,128)(2,1)} %broadcast_in_dim.38), calls=%async_computation.7 | async-start | bytes 1048576 | tf_op jit(solution)/shard_map/all_to_all | solution.py:288
  (1 other events, 0.7 us)

commit v8 on v6

--- a/solution.py
+++ b/solution.py
@@ -237,28 +237,33 @@
     first = row % 2 * 64
     length, tile = total_ref.shape[1], total_ref.shape[2]
     for column in range(8):
+        local, side = column // 2, column % 2 * (length // 2)
         for part in range(2):
-            value = total_ref[part * 64 + column * 8 : part * 64 + column * 8 + 8]
-            spread_ref[column, part * 8 * length : (part + 1) * 8 * length] = value.astype(
-                BF16
-            ).reshape(8 * length, tile)
+            value = jnp.concatenate(
+                [
+                    total_ref[part * 64 + home * 4 + local, side : side + length // 2]
+                    for home in range(16)
+                ],
+                axis=0,
+            )
+            spread_ref[column, part * 8 * length : (part + 1) * 8 * length] = value.astype(BF16)
         panel_tile = first + 8 * slots_ref[4 + level // 4, column]
         spread_ref[column, 16 * length : 17 * length] = total_ref[first].astype(BF16)
         spread_ref[column, 17 * length : 18 * length] = total_ref[panel_tile].astype(BF16)
 
 
-def upper_kernel(meta_ref, slots_ref, keep_ref, sent_ref, pivot_ref, solved_ref, out_ref):
+def upper_kernel(meta_ref, slots_ref, front_ref, pivot_ref, solved_ref, out_ref):
     level, row, col = meta_ref[0], meta_ref[1], meta_ref[2]
-    tile = keep_ref.shape[1]
+    tile = solved_ref.shape[0]
+    length = tile // 16
     dropped = pivot_slot_of(slots_ref, 4 + level // 4) == col
-    update = jnp.dot(pivot_ref[...], solved_ref[...], preferred_element_type=F32)
-    front = keep_ref[...] + sent_ref[...].astype(F32)
-    result = jnp.where(dropped, 0.0, front - update)
-    top = jnp.logical_and(
-        lax.broadcasted_iota(jnp.int32, result.shape, 0) < tile // 16, row % 2 == 0
-    )
-    result = jnp.where(top, 0.0, result).astype(BF16)
-    out_ref[...] = result.reshape(out_ref.shape)
+    corner = jnp.logical_and(level % 4 == 0, row == 0)
+    for index in range(4):
+        rows = slice(index * tile, (index + 1) * tile)
+        front = front_ref[:, index * length : (index + 1) * length].reshape(tile, tile)
+        update = jnp.dot(pivot_ref[rows], solved_ref[...], preferred_element_type=F32)
+        gone = jnp.logical_or(dropped, corner) if index == 0 else dropped
+        out_ref[rows] = jnp.where(gone, 0.0, front.astype(F32) - update).astype(BF16)
 
 
 def lane_groups(levels):
@@ -378,31 +383,29 @@
     sent = swapped(send, "row", 1)
     spread = picked(over_columns(spread), picked(slots, 4 + level // 4))
     spread, sent = tied(spread, sent)
+    front = (keep + sent.astype(F32)).astype(BF16)
+    front = exchange(front.reshape(16, 4 * sixteenth, tile), 4)
     spread = spread.astype(F32)
     passed = swapped(spread[8 * sixteenth :].astype(BF16), "row", 1).astype(F32)
     piece = (spread[: 8 * sixteenth] + passed[: 8 * sixteenth]).astype(BF16)
     parts = (spread[16 * sixteenth :] + passed[8 * sixteenth :]).astype(BF16)
-    gathered = exchange(repeated(parts.reshape(2, sixteenth, tile), 16), 4)
-    piece, gathered = tied(piece, gathered)
-    pivot_columns = over_columns(repeated(piece, 8)).reshape(-1, tile)
+    piece = jnp.concatenate([piece.reshape(16, -1, tile), repeated(parts, 16)], axis=1)
+    piece, front = tied(piece, front)
+    piece = exchange(piece, 4)
+    half = sixteenth // 2
+    gathered = piece[:, half:].reshape(16, 2, sixteenth, tile)
+    pivot_columns = over_columns(repeated(piece[:, :half], 8)).reshape(4, 2, 16, half, tile)
+    pivot_columns = jnp.swapaxes(pivot_columns, 1, 2).reshape(-1, tile)
     solved = solve(upper_front, no_place, meta, pivot_diag, gathered)
-    finished = call(
+    result = call(
         upper_kernel,
-        jax.ShapeDtypeStruct((16, 4, sixteenth, tile), BF16),
-        [SMEM, SMEM, VMEM, VMEM, VMEM, VMEM],
+        jax.ShapeDtypeStruct((4 * tile, tile), BF16),
+        [SMEM, SMEM, VMEM, VMEM, VMEM],
         VMEM,
         flops=2**28,
         moved=2**22,
-    )(
-        meta,
-        front_slots,
-        keep.reshape(-1, tile),
-        sent.reshape(-1, tile),
-        pivot_columns,
-        solved,
-    )
-    result = exchange(finished, 4)
-    return jnp.swapaxes(result, 0, 1).reshape(1, -1, tile)
+    )(meta, front_slots, front, pivot_columns, solved)
+    return result[None]
 
 
 def solution(mesh):

time: 262 us -> 258 us (0.985)
  waiting for transfers between devices: 66.1 us -> 38.7 us
  starting transfers between devices: 114 us -> 139 us
    all_to_all x2, starting transfers between devices: 17.5 us -> 40.9 us  [exchange(): lax.all_to_all(value, ('level', 'row'), split_axis=0, concat_axis=0, axis...]
    ppermute x10, waiting for transfers between devices: 53.9 us -> 35.3 us  [swapped(): lax.ppermute(value, axis, [(index, index ^ mask) for index in range(8)])]
    all_to_all x2, waiting for transfers between devices: 8.81 us -> 0.01 us  [exchange(): lax.all_to_all(value, ('level', 'row'), split_axis=0, concat_axis=0, axis...]
  transfers between devices with their start and end apart: 16 -> 16, of which waited for: 13 -> 12; matrix products, arithmetic and copies ran while one was open for 1% -> 1% of each run, Pallas kernels for 8% -> 8%
where the time goes in v8:
time: 258 us; the launch traced here: 257 us
  starting transfers between devices  139 us (54%)
  waiting for transfers between devices  38.7 us (15%)
  blocking collectives  33.6 us (13%)
  Pallas kernels  29.2 us (11%)
  local copies, waits for them, and re-layouts  7.53 us (3%)
  between operations  6.81 us (3%)
    ppermute x10, starting transfers between devices, swapped(): lax.ppermute(value, axis, [(index, index ^ mask) for index in range(8)])  67.5 us
    all_to_all x2, starting transfers between devices, exchange(): lax.all_to_all(value, ('level', 'row'), split_axis=0, concat_axis=0, axis...  40.9 us
    ppermute x10, waiting for transfers between devices, swapped(): lax.ppermute(value, axis, [(index, index ^ mask) for index in range(8)])  35.3 us
    all_to_all x2, blocking collectives, exchange(): lax.all_to_all(value, ('level', 'row'), split_axis=0, concat_axis=0, axis...  33.6 us
    all_to_all x4, starting transfers between devices, over_columns(): return lax.all_to_all(value, 'col', split_axis=0, concat_axis=0, tiled=True)  30.3 us
    pallas_call x2, Pallas kernels, solve(): call(functools.partial(solve_kernel, front_of, place_of), jax.ShapeDtypeS...  18.7 us
  transfers between devices with their start and end apart: 16, of which 12 were waited for; matrix products, arithmetic and copies ran while one was open for 1% of the time, Pallas kernels for 8%

profile of v8, /device:TPU:1, one launch (start us, length us, event | category | flops | bytes accessed | tf_op | source)
XLA Modules:
  0.0 256.9 jit_solution(16919065834198279662)
XLA Ops:
  3.8 17.5 %all_to_all.40.shares_ref = bf16[8,8,32,256]{3,2,1,0:T(8,128)(2,1)S(1)} all-to-all(bf16[8,8,32,256]{3,2,1,0:T(8,128)(2,1)S(1)} %shard_map.65), channel_id=1, replica_groups={{0,16,32,48,64,80,96,112},{8,24,40,56,72,88,104,120},{128,144,160,176,1..., dimensions={0} | all-to-all | bytes 2097152 | tf_op jit(solution)/shard_map/all_to_all | solution.py:284
  22.6 8.7 %all-to-all-start.1 = ((bf16[16,12,16,256]{3,2,1,0:T(8,128)(2,1)}), bf16[16,12,16,256]{3,2,1,0:T(8,128)(2,1)}, u32[]{:S(2)}, u32[]{:S(2)}) async-start(bf16[16,12,16,256]{3,2,1,0:T(8,128)(2,1)} %copy.11), calls=%async_computation.1 | async-start | bytes 3145728 | tf_op jit(solution)/shard_map/all_to_all | solution.py:284
  31.5 4.0 %collective-permute-start = (bf16[8,32,256]{2,1,0:T(8,128)(2,1)S(1)}, bf16[8,32,256]{2,1,0:T(8,128)(2,1)S(1)}, u32[]{:S(2)}, u32[]{:S(2)}) collective-permute-start(bf16[8,32,256]{2,1,0:T(8,128)(2,1)S(1)} %shard_map.66), channel_id=1, source_target_pairs={{0,1},{1,0},{2,3},{3,2},{4,5},{5,4},{6,7},{7,6},{8,9},{9,8},{10,11... | collective-permute-start | bytes 393224 | tf_op jit(solution)/shard_map/ppermute | solution.py:299
  37.1 3.2 %collective-permute-start.1 = (bf16[8,32,256]{2,1,0:T(8,128)(2,1)S(1)}, bf16[8,32,256]{2,1,0:T(8,128)(2,1)S(1)}, u32[]{:S(2)}, u32[]{:S(2)}) collective-permute-start(bf16[8,32,256]{2,1,0:T(8,128)(2,1)S(1)} %broadcast_select_fusion), channel_id=1, source_target_pairs={{0,2},{1,3},{2,0},{3,1},{4,6},{5,7},{6,4},{7,5},{8,10},{9,11},{10,... | collective-permute-start | bytes 393224 | tf_op jit(solution)/shard_map/ppermute | solution.py:299
  40.3 3.9 %collective-permute-done.1 = bf16[8,32,256]{2,1,0:T(8,128)(2,1)S(1)} collective-permute-done((bf16[8,32,256]{2,1,0:T(8,128)(2,1)S(1)}, bf16[8,32,256]{2,1,0:T(8,128)(2,1)S(1)}, u32[]{:S(2)}, u32[]{:S(2)}) %collective-permute-start.1) | collective-permute-done | bytes 131104 | tf_op jit(solution)/shard_map/ppermute | solution.py:299
  44.3 4.8 %collective-permute-start.2 = (bf16[8,32,256]{2,1,0:T(8,128)(2,1)S(1)}, bf16[8,32,256]{2,1,0:T(8,128)(2,1)S(1)}, u32[]{:S(2)}, u32[]{:S(2)}) collective-permute-start(bf16[8,32,256]{2,1,0:T(8,128)(2,1)S(1)} %broadcast_select_fusion.1), channel_id=1, source_target_pairs={{0,4},{1,5},{2,6},{3,7},{4,0},{5,1},{6,2},{7,3},{8,12},{9,13},{10,... | collective-permute-start | bytes 393224 | tf_op jit(solution)/shard_map/ppermute | solution.py:299
  52.2 13.4 %collective-permute-start.3 = (bf16[2,32,256]{2,1,0:T(8,128)(2,1)S(1)}, bf16[2,32,256]{2,1,0:T(8,128)(2,1)S(1)}, u32[]{:S(2)}, u32[]{:S(2)}) collective-permute-start(bf16[2,32,256]{2,1,0:T(8,128)(2,1)S(1)} %pad_maximum_fusion.4), channel_id=1, source_target_pairs={{0,8},{8,0},{16,24},{24,16},{32,40},{40,32},{48,56},{56,48},{1,9},... | collective-permute-start | bytes 98312 | tf_op jit(solution)/shard_map/ppermute | solution.py:299
  67.6 7.3 %all-to-all-start.2 = ((bf16[8,384,256]{2,1,0:T(8,128)(2,1)}), bf16[8,384,256]{2,1,0:T(8,128)(2,1)S(1)}, u32[]{:S(2)}, u32[]{:S(2)}) async-start(bf16[8,384,256]{2,1,0:T(8,128)(2,1)} %bitcast.6), calls=%async_computation.2 | async-start | bytes 3145728 | tf_op jit(solution)/shard_map/all_to_all | solution.py:295
  74.9 3.4 %collective-permute-start.4 = (bf16[1,2,32,256]{3,2,1,0:T(8,128)(2,1)S(1)}, bf16[1,2,32,256]{3,2,1,0:T(8,128)(2,1)S(1)}, u32[]{:S(2)}, u32[]{:S(2)}) collective-permute-start(bf16[1,2,32,256]{3,2,1,0:T(8,128)(2,1)S(1)} %bitcast.37), channel_id=1, source_target_pairs={{0,16},{8,24},{16,0},{24,8},{32,48},{40,56},{48,32},{56,40},{1,17}... | collective-permute-start | bytes 98312 | tf_op jit(solution)/shard_map/ppermute | solution.py:299
  79.9 4.7 %collective-permute-start.5 = (bf16[2,2,32,256]{3,2,1,0:T(8,128)(2,1)S(1)}, bf16[2,2,32,256]{3,2,1,0:T(8,128)(2,1)S(1)}, u32[]{:S(2)}, u32[]{:S(2)}) collective-permute-start(bf16[2,2,32,256]{3,2,1,0:T(8,128)(2,1)S(1)} %pad_maximum_fusion.3), channel_id=1, source_target_pairs={{0,32},{8,40},{16,48},{24,56},{32,0},{40,8},{48,16},{56,24},{1,33}... | collective-permute-start | bytes 196616 | tf_op jit(solution)/shard_map/ppermute | solution.py:299
  96.9 4.6 %all-to-all-start.3 = ((bf16[8,384,256]{2,1,0:T(8,128)(2,1)}), bf16[8,384,256]{2,1,0:T(8,128)(2,1)S(1)}, u32[]{:S(2)}, u32[]{:S(2)}) async-start(bf16[8,384,256]{2,1,0:T(8,128)(2,1)} %broadcast_in_dim.22), calls=%async_computation.3 | async-start | bytes 3145728 | tf_op jit(solution)/shard_map/all_to_all | solution.py:295
  101.6 9.4 %shard_map.67 = bf16[256,256]{1,0:T(8,128)(2,1)S(1)} custom-call(s32[3]{0:T(128)S(1)} %pad_add_fusion.meta_ref, f32[6,256]{1,0:T(8,128)S(1)} %copy-done.7, bf16[8,2,32,256]{3,2,1,0:T(8,128)(2,1)S(1)} %pad_maximum_fusion.1.gathered_ref), custom_call_target="tpu_custom_call" | custom-call | flops 536870912 | bytes 4194304 | tf_op jit(solution)/shard_map/pallas_call | solution.py:196
  111.0 4.7 %collective-permute-start.7 = (bf16[256,256]{1,0:T(8,128)(2,1)S(1)}, bf16[256,256]{1,0:T(8,128)(2,1)S(1)}, u32[]{:S(2)}, u32[]{:S(2)}) collective-permute-start(bf16[256,256]{1,0:T(8,128)(2,1)S(1)} %shard_map.67), channel_id=1, source_target_pairs={{0,128},{64,192},{128,0},{192,64},{256,384},{320,448},{384,256},{4... | collective-permute-start | bytes 393224 | tf_op jit(solution)/shard_map/ppermute | solution.py:299
  118.6 3.7 %collective-permute-done.7 = bf16[256,256]{1,0:T(8,128)(2,1)S(1)} collective-permute-done((bf16[256,256]{1,0:T(8,128)(2,1)S(1)}, bf16[256,256]{1,0:T(8,128)(2,1)S(1)}, u32[]{:S(2)}, u32[]{:S(2)}) %collective-permute-start.7) | collective-permute-done | bytes 131104 | tf_op jit(solution)/shard_map/ppermute | solution.py:299
  122.4 4.9 %shard_map.68 = (f32[64,16,256]{2,1,0:T(8,128)S(1)}, bf16[64,16,256]{2,1,0:T(8,128)(2,1)S(1)}, bf16[8,288,256]{2,1,0:T(8,128)(2,1)}) custom-call(s32[3]{0:T(128)S(1)} %pad_add_fusion.meta_ref, s32[6,8]{1,0:T(8,128)S(1)} %copy-done.1, s32[192]{0:T(256)S(1)} %shard_map.64.place_ref, bf16[192,16,256]{2,1,0:T(8,128)(2,1)} %bitcast.9.chunks_ref, ...), custom_call_target="tpu_custom_call" | custom-call | flops 536870912 | bytes 8388608 | tf_op jit(solution)/shard_map/pallas_call | solution.py:369
  127.3 5.0 %all-to-all-start.4 = ((bf16[8,288,256]{2,1,0:T(8,128)(2,1)}), bf16[8,288,256]{2,1,0:T(8,128)(2,1)S(1)}, u32[]{:S(2)}, u32[]{:S(2)}) async-start(bf16[8,288,256]{2,1,0:T(8,128)(2,1)} %get-tuple-element.24), calls=%async_computation.4 | async-start | bytes 2359296 | tf_op jit(solution)/shard_map/all_to_all | solution.py:295
  132.3 14.5 %collective-permute-start.8 = (bf16[64,16,256]{2,1,0:T(8,128)(2,1)S(1)}, bf16[64,16,256]{2,1,0:T(8,128)(2,1)}, u32[]{:S(2)}, u32[]{:S(2)}) collective-permute-start(bf16[64,16,256]{2,1,0:T(8,128)(2,1)S(1)} %get-tuple-element.25), channel_id=1, source_target_pairs={{0,8},{8,0},{16,24},{24,16},{32,40},{40,32},{48,56},{56,48},{1,9},... | collective-permute-start | bytes 1572872 | tf_op jit(solution)/shard_map/ppermute | solution.py:299
  148.9 13.6 %collective-permute-done.8 = bf16[64,16,256]{2,1,0:T(8,128)(2,1)} collective-permute-done((bf16[64,16,256]{2,1,0:T(8,128)(2,1)S(1)}, bf16[64,16,256]{2,1,0:T(8,128)(2,1)}, u32[]{:S(2)}, u32[]{:S(2)}) %collective-permute-start.8) | collective-permute-done | bytes 524320 | tf_op jit(solution)/shard_map/ppermute | solution.py:299
  164.6 32.2 %all-to-all-start.5 = ((bf16[16,64,256]{2,1,0:T(8,128)(2,1)}), bf16[16,64,256]{2,1,0:T(8,128)(2,1)S(1)}, u32[]{:S(2)}, u32[]{:S(2)}) async-start(bf16[16,64,256]{2,1,0:T(8,128)(2,1)} %bitcast.19), calls=%async_computation.5 | async-start | bytes 1048576 | tf_op jit(solution)/shard_map/all_to_all | solution.py:284
  196.8 12.1 %collective-permute-start.9 = (bf16[160,256]{1,0:T(8,128)(2,1)S(1)}, bf16[160,256]{1,0:T(8,128)(2,1)S(1)}, u32[]{:S(2)}, u32[]{:S(2)}) collective-permute-start(bf16[160,256]{1,0:T(8,128)(2,1)S(1)} %slice.27), channel_id=1, source_target_pairs={{0,8},{8,0},{16,24},{24,16},{32,40},{40,32},{48,56},{56,48},{1,9},... | collective-permute-start | bytes 245768 | tf_op jit(solution)/shard_map/ppermute | solution.py:299
  208.9 6.5 %collective-permute-done.9 = bf16[160,256]{1,0:T(8,128)(2,1)S(1)} collective-permute-done((bf16[160,256]{1,0:T(8,128)(2,1)S(1)}, bf16[160,256]{1,0:T(8,128)(2,1)S(1)}, u32[]{:S(2)}, u32[]{:S(2)}) %collective-permute-start.9) | collective-permute-done | bytes 81952 | tf_op jit(solution)/shard_map/ppermute | solution.py:299
  215.5 16.0 %all_to_all.41 = bf16[16,40,256]{2,1,0:T(8,128)(2,1)S(1)} all-to-all(bf16[16,40,256]{2,1,0:T(8,128)(2,1)S(1)} %pad_maximum_fusion), channel_id=1, replica_groups={{0,16,32,48,64,80,96,112,128,144,160,176,192,208,224,240},{8,24,40,56,7..., dimensions={0} | all-to-all | bytes 655360 | tf_op jit(solution)/shard_map/all_to_all | solution.py:284
  232.4 13.3 %all-to-all-start.7 = ((bf16[8,16,8,256]{3,2,1,0:T(8,128)(2,1)}), bf16[8,16,8,256]{3,2,1,0:T(8,128)(2,1)S(1)}, u32[]{:S(2)}, u32[]{:S(2)}) async-start(bf16[8,16,8,256]{3,2,1,0:T(8,128)(2,1)} %broadcast_in_dim.39), calls=%async_computation.7 | async-start | bytes 1048576 | tf_op jit(solution)/shard_map/all_to_all | solution.py:295
  245.7 9.3 %shard_map.69.solved_ref = bf16[256,256]{1,0:T(8,128)(2,1)S(1)} custom-call(s32[3]{0:T(128)S(1)} %pad_add_fusion.meta_ref, f32[6,256]{1,0:T(8,128)S(1)} %copy-done.7, bf16[16,2,16,256]{3,2,1,0:T(8,128)(2,1)S(1)} %bitcast.34), custom_call_target="tpu_custom_call" | custom-call | flops 536870912 | bytes 4194304 | tf_op jit(solution)/shard_map/pallas_call | solution.py:196
  (63 shorter events, 29.2 us)
Async XLA Ops:
  0.1 1.4 copy-start
  1.5 0.7 copy-start.2
  2.2 0.7 copy-start.4
  22.6 13.0 %copy-start.1 = (s32[6,8]{1,0:T(8,128)S(1)}, s32[6,8]{1,0:T(8,128)}, u32[]{:S(2)}) copy-start(s32[6,8]{1,0:T(8,128)} %slots_ref.3) | copy-start | bytes 580
  22.6 44.9 %all-to-all-start.1 = ((bf16[16,12,16,256]{3,2,1,0:T(8,128)(2,1)}), bf16[16,12,16,256]{3,2,1,0:T(8,128)(2,1)}, u32[]{:S(2)}, u32[]{:S(2)}) async-start(bf16[16,12,16,256]{3,2,1,0:T(8,128)(2,1)} %copy.11), calls=%async_computation.1 | async-start | bytes 3145728 | tf_op jit(solution)/shard_map/all_to_all | solution.py:284
  31.5 5.6 %collective-permute-start = (bf16[8,32,256]{2,1,0:T(8,128)(2,1)S(1)}, bf16[8,32,256]{2,1,0:T(8,128)(2,1)S(1)}, u32[]{:S(2)}, u32[]{:S(2)}) collective-permute-start(bf16[8,32,256]{2,1,0:T(8,128)(2,1)S(1)} %shard_map.66), channel_id=1, source_target_pairs={{0,1},{1,0},{2,3},{3,2},{4,5},{5,4},{6,7},{7,6},{8,9},{9,8},{10,11... | collective-permute-start | bytes 393224 | tf_op jit(solution)/shard_map/ppermute | solution.py:299
  37.1 7.1 %collective-permute-start.1 = (bf16[8,32,256]{2,1,0:T(8,128)(2,1)S(1)}, bf16[8,32,256]{2,1,0:T(8,128)(2,1)S(1)}, u32[]{:S(2)}, u32[]{:S(2)}) collective-permute-start(bf16[8,32,256]{2,1,0:T(8,128)(2,1)S(1)} %broadcast_select_fusion), channel_id=1, source_target_pairs={{0,2},{1,3},{2,0},{3,1},{4,6},{5,7},{6,4},{7,5},{8,10},{9,11},{10,... | collective-permute-start | bytes 393224 | tf_op jit(solution)/shard_map/ppermute | solution.py:299
  44.3 7.9 %collective-permute-start.2 = (bf16[8,32,256]{2,1,0:T(8,128)(2,1)S(1)}, bf16[8,32,256]{2,1,0:T(8,128)(2,1)S(1)}, u32[]{:S(2)}, u32[]{:S(2)}) collective-permute-start(bf16[8,32,256]{2,1,0:T(8,128)(2,1)S(1)} %broadcast_select_fusion.1), channel_id=1, source_target_pairs={{0,4},{1,5},{2,6},{3,7},{4,0},{5,1},{6,2},{7,3},{8,12},{9,13},{10,... | collective-permute-start | bytes 393224 | tf_op jit(solution)/shard_map/ppermute | solution.py:299
  52.2 15.4 %collective-permute-start.3 = (bf16[2,32,256]{2,1,0:T(8,128)(2,1)S(1)}, bf16[2,32,256]{2,1,0:T(8,128)(2,1)S(1)}, u32[]{:S(2)}, u32[]{:S(2)}) collective-permute-start(bf16[2,32,256]{2,1,0:T(8,128)(2,1)S(1)} %pad_maximum_fusion.4), channel_id=1, source_target_pairs={{0,8},{8,0},{16,24},{24,16},{32,40},{40,32},{48,56},{56,48},{1,9},... | collective-permute-start | bytes 98312 | tf_op jit(solution)/shard_map/ppermute | solution.py:299
  67.6 28.1 %all-to-all-start.2 = ((bf16[8,384,256]{2,1,0:T(8,128)(2,1)}), bf16[8,384,256]{2,1,0:T(8,128)(2,1)S(1)}, u32[]{:S(2)}, u32[]{:S(2)}) async-start(bf16[8,384,256]{2,1,0:T(8,128)(2,1)} %bitcast.6), calls=%async_computation.2 | async-start | bytes 3145728 | tf_op jit(solution)/shard_map/all_to_all | solution.py:295
  74.9 5.0 %collective-permute-start.4 = (bf16[1,2,32,256]{3,2,1,0:T(8,128)(2,1)S(1)}, bf16[1,2,32,256]{3,2,1,0:T(8,128)(2,1)S(1)}, u32[]{:S(2)}, u32[]{:S(2)}) collective-permute-start(bf16[1,2,32,256]{3,2,1,0:T(8,128)(2,1)S(1)} %bitcast.37), channel_id=1, source_target_pairs={{0,16},{8,24},{16,0},{24,8},{32,48},{40,56},{48,32},{56,40},{1,17}... | collective-permute-start | bytes 98312 | tf_op jit(solution)/shard_map/ppermute | solution.py:299
  79.9 6.5 %collective-permute-start.5 = (bf16[2,2,32,256]{3,2,1,0:T(8,128)(2,1)S(1)}, bf16[2,2,32,256]{3,2,1,0:T(8,128)(2,1)S(1)}, u32[]{:S(2)}, u32[]{:S(2)}) collective-permute-start(bf16[2,2,32,256]{3,2,1,0:T(8,128)(2,1)S(1)} %pad_maximum_fusion.3), channel_id=1, source_target_pairs={{0,32},{8,40},{16,48},{24,56},{32,0},{40,8},{48,16},{56,24},{1,33}... | collective-permute-start | bytes 196616 | tf_op jit(solution)/shard_map/ppermute | solution.py:299
  86.5 6.0 %collective-permute-start.6 = (bf16[4,2,32,256]{3,2,1,0:T(8,128)(2,1)S(1)}, bf16[4,2,32,256]{3,2,1,0:T(8,128)(2,1)S(1)}, u32[]{:S(2)}, u32[]{:S(2)}) collective-permute-start(bf16[4,2,32,256]{3,2,1,0:T(8,128)(2,1)S(1)} %pad_maximum_fusion.2), channel_id=1, source_target_pairs={{0,64},{64,0},{128,192},{192,128},{256,320},{320,256},{384,448},{4... | collective-permute-start | bytes 393224 | tf_op jit(solution)/shard_map/ppermute | solution.py:299
  96.9 4.6 %copy-start.7 = (f32[6,256]{1,0:T(8,128)S(1)}, f32[6,256]{1,0:T(8,128)}, u32[]{:S(2)}) copy-start(f32[6,256]{1,0:T(8,128)} %diag_ref.3) | copy-start | bytes 18436
  96.9 25.5 %all-to-all-start.3 = ((bf16[8,384,256]{2,1,0:T(8,128)(2,1)}), bf16[8,384,256]{2,1,0:T(8,128)(2,1)S(1)}, u32[]{:S(2)}, u32[]{:S(2)}) async-start(bf16[8,384,256]{2,1,0:T(8,128)(2,1)} %broadcast_in_dim.22), calls=%async_computation.3 | async-start | bytes 3145728 | tf_op jit(solution)/shard_map/all_to_all | solution.py:295
  101.5 14.2 %copy-start.3 = (s32[8,96]{1,0:T(8,128)S(1)}, s32[8,96]{1,0:T(8,128)}, u32[]{:S(2)}) copy-start(s32[8,96]{1,0:T(8,128)} %leaf_maps_ref.3) | copy-start | bytes 9220
  101.5 14.2 %copy-start.5 = (s32[8]{0:T(128)S(1)}, s32[8]{0:T(128)}, u32[]{:S(2)}) copy-start(s32[8]{0:T(128)} %tiles_ref.3) | copy-start | bytes 100
  101.5 14.2 %copy-start.6 = (s32[4,128]{1,0:T(4,128)S(1)}, s32[4,128]{1,0:T(4,128)}, u32[]{:S(2)}) copy-start(s32[4,128]{1,0:T(4,128)} %upper_maps_ref.1) | copy-start | bytes 6148
  111.0 11.4 %collective-permute-start.7 = (bf16[256,256]{1,0:T(8,128)(2,1)S(1)}, bf16[256,256]{1,0:T(8,128)(2,1)S(1)}, u32[]{:S(2)}, u32[]{:S(2)}) collective-permute-start(bf16[256,256]{1,0:T(8,128)(2,1)S(1)} %shard_map.67), channel_id=1, source_target_pairs={{0,128},{64,192},{128,0},{192,64},{256,384},{320,448},{384,256},{4... | collective-permute-start | bytes 393224 | tf_op jit(solution)/shard_map/ppermute | solution.py:299
  127.3 21.6 %all-to-all-start.4 = ((bf16[8,288,256]{2,1,0:T(8,128)(2,1)}), bf16[8,288,256]{2,1,0:T(8,128)(2,1)S(1)}, u32[]{:S(2)}, u32[]{:S(2)}) async-start(bf16[8,288,256]{2,1,0:T(8,128)(2,1)} %get-tuple-element.24), calls=%async_computation.4 | async-start | bytes 2359296 | tf_op jit(solution)/shard_map/all_to_all | solution.py:295
  132.3 30.3 %collective-permute-start.8 = (bf16[64,16,256]{2,1,0:T(8,128)(2,1)S(1)}, bf16[64,16,256]{2,1,0:T(8,128)(2,1)}, u32[]{:S(2)}, u32[]{:S(2)}) collective-permute-start(bf16[64,16,256]{2,1,0:T(8,128)(2,1)S(1)} %get-tuple-element.25), channel_id=1, source_target_pairs={{0,8},{8,0},{16,24},{24,16},{32,40},{40,32},{48,56},{56,48},{1,9},... | collective-permute-start | bytes 1572872 | tf_op jit(solution)/shard_map/ppermute | solution.py:299
  164.6 51.0 %all-to-all-start.5 = ((bf16[16,64,256]{2,1,0:T(8,128)(2,1)}), bf16[16,64,256]{2,1,0:T(8,128)(2,1)S(1)}, u32[]{:S(2)}, u32[]{:S(2)}) async-start(bf16[16,64,256]{2,1,0:T(8,128)(2,1)} %bitcast.19), calls=%async_computation.5 | async-start | bytes 1048576 | tf_op jit(solution)/shard_map/all_to_all | solution.py:284
  196.8 18.6 %collective-permute-start.9 = (bf16[160,256]{1,0:T(8,128)(2,1)S(1)}, bf16[160,256]{1,0:T(8,128)(2,1)S(1)}, u32[]{:S(2)}, u32[]{:S(2)}) collective-permute-start(bf16[160,256]{1,0:T(8,128)(2,1)S(1)} %slice.27), channel_id=1, source_target_pairs={{0,8},{8,0},{16,24},{24,16},{32,40},{40,32},{48,56},{56,48},{1,9},... | collective-permute-start | bytes 245768 | tf_op jit(solution)/shard_map/ppermute | solution.py:299
  232.4 22.8 %all-to-all-start.7 = ((bf16[8,16,8,256]{3,2,1,0:T(8,128)(2,1)}), bf16[8,16,8,256]{3,2,1,0:T(8,128)(2,1)S(1)}, u32[]{:S(2)}, u32[]{:S(2)}) async-start(bf16[8,16,8,256]{3,2,1,0:T(8,128)(2,1)} %broadcast_in_dim.39), calls=%async_computation.7 | async-start | bytes 1048576 | tf_op jit(solution)/shard_map/all_to_all | solution.py:295

commit v9 on v8

--- a/solution.py
+++ b/solution.py
@@ -71,13 +71,6 @@
         return carry
 
     lax.fori_loop(0, 12, look, 0)
-
-
-def combine_kernel(shares_ref, out_ref):
-    total = shares_ref[0].astype(F32)
-    for source in range(1, shares_ref.shape[0]):
-        total = total + shares_ref[source].astype(F32)
-    out_ref[...] = total.astype(BF16)
 
 
 def split(value):
@@ -161,9 +154,8 @@
 def solve_kernel(front_of, place_of, meta_ref, diag_ref, gathered_ref, out_ref, work_ref, chosen_ref):
     tile = out_ref.shape[0]
     count, length = gathered_ref.shape[0], gathered_ref.shape[2]
-    place = place_of(meta_ref)
     for piece in range(count):
-        rows = pl.ds(pl.multiple_of((place ^ piece) * length, length), length)
+        rows = pl.ds(pl.multiple_of(place_of(meta_ref, piece) * length, length), length)
         work_ref[rows, :] = gathered_ref[piece, 0].astype(F32)
         chosen_ref[rows, :] = gathered_ref[piece, 1].astype(F32)
     pivot = work_ref[...]
@@ -183,12 +175,12 @@
     return 4 + level // 4
 
 
-def pair_place(meta_ref):
-    return (meta_ref[0] & 1) * 4 + (meta_ref[1] >> 1)
-
-
-def no_place(meta_ref):
-    return jnp.int32(0)
+def across_place(meta_ref, piece):
+    return ((meta_ref[1] >> 1) - piece) & 3
+
+
+def same_place(meta_ref, piece):
+    return jnp.int32(piece)
 
 
 def solve(front_of, place_of, meta, diagonals, gathered):
@@ -299,6 +291,11 @@
     return lax.ppermute(value, axis, [(index, index ^ mask) for index in range(8)])
 
 
+def turned(value, axis, step):
+    pairs = [(index, ((index >> 1) + step) % 4 * 2 + (index & 1)) for index in range(8)]
+    return lax.ppermute(value, axis, pairs)
+
+
 def tied(*values):
     return lax.optimization_barrier(values)
 
@@ -322,16 +319,15 @@
     eighth, sixteenth = tile // 8, tile // 16
     own = leaf_blocks.reshape(12, tile, tile)
 
+    quarter = tile // 4
     shares = call(
         share_kernel,
-        jax.ShapeDtypeStruct((8, 8, eighth, tile), BF16),
+        jax.ShapeDtypeStruct((4, 8, quarter, tile), BF16),
         [SMEM] * 3 + [VMEM],
         VMEM,
         moved=2**21,
     )(meta, leaf_tiles, leaf_maps, own)
-    shares = exchange(shares, 2)
     chunks = jnp.swapaxes(own.reshape(12, 16, sixteenth, tile), 0, 1)
-    chunks, shares = tied(chunks, shares)
     chunks = exchange(chunks, 4).reshape(8, -1, tile)
     place = call(
         plan_kernel,
@@ -340,29 +336,28 @@
         SMEM,
     )(meta, leaf_tiles, leaf_maps, upper_maps)
 
-    shares = call(
-        combine_kernel,
-        jax.ShapeDtypeStruct((8, eighth, tile), BF16),
-        [VMEM],
-        VMEM,
-        moved=2**21,
-    )(shares)
-    away = col ^ picked(slots, level // 2)
-    for mask in (1, 2, 4):
-        shares = jnp.where(away & mask == 0, shares, swapped(shares, "col", mask))
+    across = row // 2
+    arrived = [turned(picked(shares, (across + step) % 4), "row", step) for step in (1, 2, 3)]
+    shares = picked(shares, across)
+    for value in arrived:
+        shares = shares + value
+    pivot_slot = picked(slots, level // 2)
+    shares = jnp.where((col ^ pivot_slot) & 1 == 0, shares, swapped(shares, "col", 1))
+    away = (col // 2 - pivot_slot // 2) % 4
+    arrived = [turned(shares, "col", step) for step in (1, 2, 3)]
+    for step, value in enumerate(arrived):
+        shares = jnp.where(away == step + 1, value, shares)
     my_tile = lax.dynamic_slice(front_slots, (level // 2, col), (1, 1))[0, 0]
     parts = jnp.stack([shares[0], picked(shares, my_tile)])
-    parts = (parts.astype(F32) + swapped(parts, "row", 1).astype(F32)).astype(BF16)
-
     chunks, parts = tied(chunks, parts)
     pieces = over_columns(chunks)
-    gathered = parts[None]
-    for axis, mask in (("row", 2), ("row", 4), ("level", 1)):
-        gathered = jnp.concatenate([gathered, swapped(gathered, axis, mask)], axis=0)
+    parts = (parts.astype(F32) + swapped(parts, "row", 1).astype(F32)).astype(BF16)
+    parts = (parts.astype(F32) + swapped(parts, "level", 1).astype(F32)).astype(BF16)
+    gathered = jnp.stack([parts] + [turned(parts, "row", step) for step in (1, 2, 3)])
     piece = picked(pieces, picked(slots, level // 4 * 2 + col // 4))
     piece, gathered = tied(piece, gathered)
     pivot_columns = over_columns(repeated(piece, 8)).reshape(192, sixteenth, tile)
-    solved = solve(lower_front, pair_place, meta, pivot_diag, gathered)
+    solved = solve(lower_front, across_place, meta, pivot_diag, gathered)
     other = swapped(solved, "level", 2)
     first_child = level // 2 % 2 == 0
     solved = jnp.where(first_child, jnp.stack([solved, other]), jnp.stack([other, solved]))
@@ -396,7 +391,7 @@
     gathered = piece[:, half:].reshape(16, 2, sixteenth, tile)
     pivot_columns = over_columns(repeated(piece[:, :half], 8)).reshape(4, 2, 16, half, tile)
     pivot_columns = jnp.swapaxes(pivot_columns, 1, 2).reshape(-1, tile)
-    solved = solve(upper_front, no_place, meta, pivot_diag, gathered)
+    solved = solve(upper_front, same_place, meta, pivot_diag, gathered)
     result = call(
         upper_kernel,
         jax.ShapeDtypeStruct((4 * tile, tile), BF16),

time: 258 us -> 274 us (1.062)
  waiting for transfers between devices: 38.7 us -> 68.4 us
  blocking collectives: 33.6 us -> 16.6 us
  between operations: 6.81 us -> 9.7 us
    ppermute x0 -> x9, starting transfers between devices: none -> 28.4 us  [turned(): return lax.ppermute(value, axis, pairs)]
    ppermute x0 -> x9, waiting for transfers between devices: none -> 21.3 us  [turned(): return lax.ppermute(value, axis, pairs)]
    ppermute x10 -> x6, starting transfers between devices: 67.5 us -> 48.3 us  [swapped(): lax.ppermute(value, axis, [(index, index ^ mask) for index in range(8)])]
    all_to_all x2 -> x1, blocking collectives: 33.6 us -> 16.6 us  [exchange(): lax.all_to_all(value, ('level', 'row'), split_axis=0, concat_axis=0, axis...]
    ppermute x10 -> x6, waiting for transfers between devices: 35.3 us -> 44.4 us  [swapped(): lax.ppermute(value, axis, [(index, index ^ mask) for index in range(8)])]
    all_to_all x2, starting transfers between devices: 40.9 us -> 34.2 us  [exchange(): lax.all_to_all(value, ('level', 'row'), split_axis=0, concat_axis=0, axis...]
    unnamed x16 -> x12, local copies, waits for them, and re-layouts: 2.77 us -> 0.02 us
  transfers between devices with their start and end apart: 16 -> 21, of which waited for: 12 -> 13; matrix products, arithmetic and copies ran while one was open for 1% -> 1% of each run, Pallas kernels for 8% -> 8%
where the time goes in v9:
time: 274 us; the launch traced here: 272 us
  starting transfers between devices  140 us (51%)
  waiting for transfers between devices  68.4 us (25%)
  Pallas kernels  29 us (11%)
  blocking collectives  16.6 us (6%)
  between operations  9.7 us (4%)
  local copies, waits for them, and re-layouts  6.31 us (2%)
    ppermute x6, starting transfers between devices, swapped(): lax.ppermute(value, axis, [(index, index ^ mask) for index in range(8)])  48.3 us
    ppermute x6, waiting for transfers between devices, swapped(): lax.ppermute(value, axis, [(index, index ^ mask) for index in range(8)])  44.4 us
    all_to_all x2, starting transfers between devices, exchange(): lax.all_to_all(value, ('level', 'row'), split_axis=0, concat_axis=0, axis...  34.2 us
    all_to_all x4, starting transfers between devices, over_columns(): return lax.all_to_all(value, 'col', split_axis=0, concat_axis=0, tiled=True)  28.7 us
    ppermute x9, starting transfers between devices, turned(): return lax.ppermute(value, axis, pairs)  28.4 us
    ppermute x9, waiting for transfers between devices, turned(): return lax.ppermute(value, axis, pairs)  21.3 us
    pallas_call x2, Pallas kernels, solve(): call(functools.partial(solve_kernel, front_of, place_of), jax.ShapeDtypeS...  18.6 us
    all_to_all x1, blocking collectives, exchange(): lax.all_to_all(value, ('level', 'row'), split_axis=0, concat_axis=0, axis...  16.6 us
  transfers between devices with their start and end apart: 21, of which 13 were waited for; matrix products, arithmetic and copies ran while one was open for 1% of the time, Pallas kernels for 8%

profile of v9, /device:TPU:1, one launch (start us, length us, event | category | flops | bytes accessed | tf_op | source)
XLA Modules:
  0.0 272.3 jit_solution(13520687517637386165)
XLA Ops:
  2.7 9.2 %all-to-all-start = ((bf16[16,12,16,256]{3,2,1,0:T(8,128)(2,1)}), bf16[16,12,16,256]{3,2,1,0:T(8,128)(2,1)}, u32[]{:S(2)}, u32[]{:S(2)}) async-start(bf16[16,12,16,256]{3,2,1,0:T(8,128)(2,1)} %copy.11), calls=%async_computation | async-start | bytes 3145728 | tf_op jit(solution)/shard_map/all_to_all | solution.py:276
  16.3 3.4 %collective-permute-start.2 = (bf16[8,64,256]{2,1,0:T(8,128)(2,1)S(1)}, bf16[8,64,256]{2,1,0:T(8,128)(2,1)S(1)}, u32[]{:S(2)}, u32[]{:S(2)}) collective-permute-start(bf16[8,64,256]{2,1,0:T(8,128)(2,1)S(1)} %get-tuple-element.28), channel_id=1, source_target_pairs={{0,48},{8,56},{16,0},{24,8},{32,16},{40,24},{48,32},{56,40},{1,49}... | collective-permute-start | bytes 786440 | tf_op jit(solution)/shard_map/ppermute | solution.py:296
  19.7 3.4 %collective-permute-start.1 = (bf16[8,64,256]{2,1,0:T(8,128)(2,1)S(1)}, bf16[8,64,256]{2,1,0:T(8,128)(2,1)S(1)}, u32[]{:S(2)}, u32[]{:S(2)}) collective-permute-start(bf16[8,64,256]{2,1,0:T(8,128)(2,1)S(1)} %get-tuple-element.29), channel_id=1, source_target_pairs={{0,32},{8,40},{16,48},{24,56},{32,0},{40,8},{48,16},{56,24},{1,33}... | collective-permute-start | bytes 786440 | tf_op jit(solution)/shard_map/ppermute | solution.py:296
  23.1 12.2 %collective-permute-done = bf16[8,64,256]{2,1,0:T(8,128)(2,1)S(1)} collective-permute-done((bf16[8,64,256]{2,1,0:T(8,128)(2,1)S(1)}, bf16[8,64,256]{2,1,0:T(8,128)(2,1)S(1)}, u32[]{:S(2)}, u32[]{:S(2)}) %collective-permute-start) | collective-permute-done | bytes 262176 | tf_op jit(solution)/shard_map/ppermute | solution.py:296
  35.3 3.7 %collective-permute-done.1 = bf16[8,64,256]{2,1,0:T(8,128)(2,1)S(1)} collective-permute-done((bf16[8,64,256]{2,1,0:T(8,128)(2,1)S(1)}, bf16[8,64,256]{2,1,0:T(8,128)(2,1)S(1)}, u32[]{:S(2)}, u32[]{:S(2)}) %collective-permute-start.1) | collective-permute-done | bytes 262176 | tf_op jit(solution)/shard_map/ppermute | solution.py:296
  39.1 4.1 %collective-permute-start.3 = (bf16[8,64,256]{2,1,0:T(8,128)(2,1)S(1)}, bf16[8,64,256]{2,1,0:T(8,128)(2,1)S(1)}, u32[]{:S(2)}, u32[]{:S(2)}) collective-permute-start(bf16[8,64,256]{2,1,0:T(8,128)(2,1)S(1)} %fusion.1), channel_id=1, source_target_pairs={{0,1},{1,0},{2,3},{3,2},{4,5},{5,4},{6,7},{7,6},{8,9},{9,8},{10,11... | collective-permute-start | bytes 786440 | tf_op jit(solution)/shard_map/ppermute | solution.py:291
  47.9 4.5 %collective-permute-start.5 = (bf16[8,64,256]{2,1,0:T(8,128)(2,1)S(1)}, bf16[8,64,256]{2,1,0:T(8,128)(2,1)S(1)}, u32[]{:S(2)}, u32[]{:S(2)}) collective-permute-start(bf16[8,64,256]{2,1,0:T(8,128)(2,1)S(1)} %broadcast_select_fusion), channel_id=1, source_target_pairs={{0,4},{1,5},{2,6},{3,7},{4,0},{5,1},{6,2},{7,3},{8,12},{9,13},{10,... | collective-permute-start | bytes 786440 | tf_op jit(solution)/shard_map/ppermute | solution.py:296
  63.8 5.4 %all-to-all-start.1 = ((bf16[8,384,256]{2,1,0:T(8,128)(2,1)}), bf16[8,384,256]{2,1,0:T(8,128)(2,1)S(1)}, u32[]{:S(2)}, u32[]{:S(2)}) async-start(bf16[8,384,256]{2,1,0:T(8,128)(2,1)} %bitcast.5), calls=%async_computation.1 | async-start | bytes 3145728 | tf_op jit(solution)/shard_map/all_to_all | solution.py:287
  69.2 12.7 %collective-permute-start.7 = (bf16[2,64,256]{2,1,0:T(8,128)(2,1)S(1)}, bf16[2,64,256]{2,1,0:T(8,128)(2,1)S(1)}, u32[]{:S(2)}, u32[]{:S(2)}) collective-permute-start(bf16[2,64,256]{2,1,0:T(8,128)(2,1)S(1)} %pad_maximum_fusion.2), channel_id=1, source_target_pairs={{0,8},{8,0},{16,24},{24,16},{32,40},{40,32},{48,56},{56,48},{1,9},... | collective-permute-start | bytes 196616 | tf_op jit(solution)/shard_map/ppermute | solution.py:291
  84.4 4.7 %collective-permute-start.8 = (bf16[2,64,256]{2,1,0:T(8,128)(2,1)S(1)}, bf16[2,64,256]{2,1,0:T(8,128)(2,1)S(1)}, u32[]{:S(2)}, u32[]{:S(2)}) collective-permute-start(bf16[2,64,256]{2,1,0:T(8,128)(2,1)S(1)} %add_convert_fusion.2), channel_id=1, source_target_pairs={{0,64},{64,0},{128,192},{192,128},{256,320},{320,256},{384,448},{4... | collective-permute-start | bytes 196616 | tf_op jit(solution)/shard_map/ppermute | solution.py:291
  92.4 3.3 %collective-permute-start.11 = (bf16[2,64,256]{2,1,0:T(8,128)(2,1)S(1)}, bf16[2,64,256]{2,1,0:T(8,128)(2,1)S(1)}, u32[]{:S(2)}, u32[]{:S(2)}) collective-permute-start(bf16[2,64,256]{2,1,0:T(8,128)(2,1)S(1)} %add_convert_fusion.1), channel_id=1, source_target_pairs={{0,48},{8,56},{16,0},{24,8},{32,16},{40,24},{48,32},{56,40},{1,49}... | collective-permute-start | bytes 196616 | tf_op jit(solution)/shard_map/ppermute | solution.py:296
  106.0 10.4 %all-to-all-start.2 = ((bf16[8,384,256]{2,1,0:T(8,128)(2,1)}), bf16[8,384,256]{2,1,0:T(8,128)(2,1)S(1)}, u32[]{:S(2)}, u32[]{:S(2)}) async-start(bf16[8,384,256]{2,1,0:T(8,128)(2,1)} %broadcast_in_dim.19), calls=%async_computation.2 | async-start | bytes 3145728 | tf_op jit(solution)/shard_map/all_to_all | solution.py:287
  116.4 9.3 %shard_map.66 = bf16[256,256]{1,0:T(8,128)(2,1)S(1)} custom-call(s32[3]{0:T(128)S(1)} %pad_add_fusion.meta_ref, f32[6,256]{1,0:T(8,128)S(1)} %copy-done.5, bf16[4,2,64,256]{3,2,1,0:T(8,128)(2,1)S(1)} %pad_maximum_fusion.1.gathered_ref), custom_call_target="tpu_custom_call" | custom-call | flops 536870912 | bytes 4194304 | tf_op jit(solution)/shard_map/pallas_call | solution.py:188
  130.6 5.7 %collective-permute-done.12 = bf16[256,256]{1,0:T(8,128)(2,1)S(1)} collective-permute-done((bf16[256,256]{1,0:T(8,128)(2,1)S(1)}, bf16[256,256]{1,0:T(8,128)(2,1)S(1)}, u32[]{:S(2)}, u32[]{:S(2)}) %collective-permute-start.12) | collective-permute-done | bytes 131104 | tf_op jit(solution)/shard_map/ppermute | solution.py:291
  137.1 4.9 %shard_map.67 = (f32[64,16,256]{2,1,0:T(8,128)S(1)}, bf16[64,16,256]{2,1,0:T(8,128)(2,1)S(1)}, bf16[8,288,256]{2,1,0:T(8,128)(2,1)}) custom-call(s32[3]{0:T(128)S(1)} %pad_add_fusion.meta_ref, s32[6,8]{1,0:T(8,128)S(1)} %copy-done.1, s32[192]{0:T(256)S(1)} %shard_map.64.place_ref, bf16[192,16,256]{2,1,0:T(8,128)(2,1)} %bitcast.13.chunks_ref, ...), custom_call_target="tpu_custom_call" | custom-call | flops 536870912 | bytes 8388608 | tf_op jit(solution)/shard_map/pallas_call | solution.py:364
  142.0 4.3 %all-to-all-start.3 = ((bf16[8,288,256]{2,1,0:T(8,128)(2,1)}), bf16[8,288,256]{2,1,0:T(8,128)(2,1)S(1)}, u32[]{:S(2)}, u32[]{:S(2)}) async-start(bf16[8,288,256]{2,1,0:T(8,128)(2,1)} %get-tuple-element.20), calls=%async_computation.3 | async-start | bytes 2359296 | tf_op jit(solution)/shard_map/all_to_all | solution.py:287
  146.3 13.0 %collective-permute-start.13 = (bf16[64,16,256]{2,1,0:T(8,128)(2,1)S(1)}, bf16[64,16,256]{2,1,0:T(8,128)(2,1)}, u32[]{:S(2)}, u32[]{:S(2)}) collective-permute-start(bf16[64,16,256]{2,1,0:T(8,128)(2,1)S(1)} %get-tuple-element.21), channel_id=1, source_target_pairs={{0,8},{8,0},{16,24},{24,16},{32,40},{40,32},{48,56},{56,48},{1,9},... | collective-permute-start | bytes 1572872 | tf_op jit(solution)/shard_map/ppermute | solution.py:291
  163.0 21.8 %collective-permute-done.13 = bf16[64,16,256]{2,1,0:T(8,128)(2,1)} collective-permute-done((bf16[64,16,256]{2,1,0:T(8,128)(2,1)S(1)}, bf16[64,16,256]{2,1,0:T(8,128)(2,1)}, u32[]{:S(2)}, u32[]{:S(2)}) %collective-permute-start.13) | collective-permute-done | bytes 524320 | tf_op jit(solution)/shard_map/ppermute | solution.py:291
  186.8 25.1 %all-to-all-start.4 = ((bf16[16,64,256]{2,1,0:T(8,128)(2,1)}), bf16[16,64,256]{2,1,0:T(8,128)(2,1)S(1)}, u32[]{:S(2)}, u32[]{:S(2)}) async-start(bf16[16,64,256]{2,1,0:T(8,128)(2,1)} %bitcast.26), calls=%async_computation.4 | async-start | bytes 1048576 | tf_op jit(solution)/shard_map/all_to_all | solution.py:276
  211.9 11.8 %collective-permute-start.14 = (bf16[160,256]{1,0:T(8,128)(2,1)S(1)}, bf16[160,256]{1,0:T(8,128)(2,1)S(1)}, u32[]{:S(2)}, u32[]{:S(2)}) collective-permute-start(bf16[160,256]{1,0:T(8,128)(2,1)S(1)} %slice.27), channel_id=1, source_target_pairs={{0,8},{8,0},{16,24},{24,16},{32,40},{40,32},{48,56},{56,48},{1,9},... | collective-permute-start | bytes 245768 | tf_op jit(solution)/shard_map/ppermute | solution.py:291
  223.7 11.2 %collective-permute-done.14 = bf16[160,256]{1,0:T(8,128)(2,1)S(1)} collective-permute-done((bf16[160,256]{1,0:T(8,128)(2,1)S(1)}, bf16[160,256]{1,0:T(8,128)(2,1)S(1)}, u32[]{:S(2)}, u32[]{:S(2)}) %collective-permute-start.14) | collective-permute-done | bytes 81952 | tf_op jit(solution)/shard_map/ppermute | solution.py:291
  235.1 16.6 %all_to_all.35 = bf16[16,40,256]{2,1,0:T(8,128)(2,1)S(1)} all-to-all(bf16[16,40,256]{2,1,0:T(8,128)(2,1)S(1)} %pad_maximum_fusion), channel_id=1, replica_groups={{0,16,32,48,64,80,96,112,128,144,160,176,192,208,224,240},{8,24,40,56,7..., dimensions={0} | all-to-all | bytes 655360 | tf_op jit(solution)/shard_map/all_to_all | solution.py:276
  252.5 8.5 %all-to-all-start.6 = ((bf16[8,16,8,256]{3,2,1,0:T(8,128)(2,1)}), bf16[8,16,8,256]{3,2,1,0:T(8,128)(2,1)S(1)}, u32[]{:S(2)}, u32[]{:S(2)}) async-start(bf16[8,16,8,256]{3,2,1,0:T(8,128)(2,1)} %broadcast_in_dim.21), calls=%async_computation.6 | async-start | bytes 1048576 | tf_op jit(solution)/shard_map/all_to_all | solution.py:287
  261.1 9.3 %shard_map.68.solved_ref = bf16[256,256]{1,0:T(8,128)(2,1)S(1)} custom-call(s32[3]{0:T(128)S(1)} %pad_add_fusion.meta_ref, f32[6,256]{1,0:T(8,128)S(1)} %copy-done.5, bf16[16,2,16,256]{3,2,1,0:T(8,128)(2,1)S(1)} %bitcast.49), custom_call_target="tpu_custom_call" | custom-call | flops 536870912 | bytes 4194304 | tf_op jit(solution)/shard_map/pallas_call | solution.py:188
  (67 shorter events, 43.9 us)
Async XLA Ops:
  2.7 61.0 %all-to-all-start = ((bf16[16,12,16,256]{3,2,1,0:T(8,128)(2,1)}), bf16[16,12,16,256]{3,2,1,0:T(8,128)(2,1)}, u32[]{:S(2)}, u32[]{:S(2)}) async-start(bf16[16,12,16,256]{3,2,1,0:T(8,128)(2,1)} %copy.11), calls=%async_computation | async-start | bytes 3145728 | tf_op jit(solution)/shard_map/all_to_all | solution.py:276
  13.1 30.2 %copy-start.1 = (s32[6,8]{1,0:T(8,128)S(1)}, s32[6,8]{1,0:T(8,128)}, u32[]{:S(2)}) copy-start(s32[6,8]{1,0:T(8,128)} %slots_ref.3) | copy-start | bytes 580
  13.2 22.2 %collective-permute-start = (bf16[8,64,256]{2,1,0:T(8,128)(2,1)S(1)}, bf16[8,64,256]{2,1,0:T(8,128)(2,1)S(1)}, u32[]{:S(2)}, u32[]{:S(2)}) collective-permute-start(bf16[8,64,256]{2,1,0:T(8,128)(2,1)S(1)} %get-tuple-element.27), channel_id=1, source_target_pairs={{0,16},{8,24},{16,32},{24,40},{32,48},{40,56},{48,0},{56,8},{1,17}... | collective-permute-start | bytes 786440 | tf_op jit(solution)/shard_map/ppermute | solution.py:296
  16.3 19.0 %collective-permute-start.2 = (bf16[8,64,256]{2,1,0:T(8,128)(2,1)S(1)}, bf16[8,64,256]{2,1,0:T(8,128)(2,1)S(1)}, u32[]{:S(2)}, u32[]{:S(2)}) collective-permute-start(bf16[8,64,256]{2,1,0:T(8,128)(2,1)S(1)} %get-tuple-element.28), channel_id=1, source_target_pairs={{0,48},{8,56},{16,0},{24,8},{32,16},{40,24},{48,32},{56,40},{1,49}... | collective-permute-start | bytes 786440 | tf_op jit(solution)/shard_map/ppermute | solution.py:296
  19.7 19.4 %collective-permute-start.1 = (bf16[8,64,256]{2,1,0:T(8,128)(2,1)S(1)}, bf16[8,64,256]{2,1,0:T(8,128)(2,1)S(1)}, u32[]{:S(2)}, u32[]{:S(2)}) collective-permute-start(bf16[8,64,256]{2,1,0:T(8,128)(2,1)S(1)} %get-tuple-element.29), channel_id=1, source_target_pairs={{0,32},{8,40},{16,48},{24,56},{32,0},{40,8},{48,16},{56,24},{1,33}... | collective-permute-start | bytes 786440 | tf_op jit(solution)/shard_map/ppermute | solution.py:296
  39.1 5.7 %collective-permute-start.3 = (bf16[8,64,256]{2,1,0:T(8,128)(2,1)S(1)}, bf16[8,64,256]{2,1,0:T(8,128)(2,1)S(1)}, u32[]{:S(2)}, u32[]{:S(2)}) collective-permute-start(bf16[8,64,256]{2,1,0:T(8,128)(2,1)S(1)} %fusion.1), channel_id=1, source_target_pairs={{0,1},{1,0},{2,3},{3,2},{4,5},{5,4},{6,7},{7,6},{8,9},{9,8},{10,11... | collective-permute-start | bytes 786440 | tf_op jit(solution)/shard_map/ppermute | solution.py:291
  44.9 15.9 %collective-permute-start.6 = (bf16[8,64,256]{2,1,0:T(8,128)(2,1)S(1)}, bf16[8,64,256]{2,1,0:T(8,128)(2,1)S(1)}, u32[]{:S(2)}, u32[]{:S(2)}) collective-permute-start(bf16[8,64,256]{2,1,0:T(8,128)(2,1)S(1)} %broadcast_select_fusion), channel_id=1, source_target_pairs={{0,2},{1,3},{2,4},{3,5},{4,6},{5,7},{6,0},{7,1},{8,10},{9,11},{10,... | collective-permute-start | bytes 786440 | tf_op jit(solution)/shard_map/ppermute | solution.py:296
  47.9 14.7 %collective-permute-start.5 = (bf16[8,64,256]{2,1,0:T(8,128)(2,1)S(1)}, bf16[8,64,256]{2,1,0:T(8,128)(2,1)S(1)}, u32[]{:S(2)}, u32[]{:S(2)}) collective-permute-start(bf16[8,64,256]{2,1,0:T(8,128)(2,1)S(1)} %broadcast_select_fusion), channel_id=1, source_target_pairs={{0,4},{1,5},{2,6},{3,7},{4,0},{5,1},{6,2},{7,3},{8,12},{9,13},{10,... | collective-permute-start | bytes 786440 | tf_op jit(solution)/shard_map/ppermute | solution.py:296
  52.4 11.3 %collective-permute-start.4 = (bf16[8,64,256]{2,1,0:T(8,128)(2,1)S(1)}, bf16[8,64,256]{2,1,0:T(8,128)(2,1)S(1)}, u32[]{:S(2)}, u32[]{:S(2)}) collective-permute-start(bf16[8,64,256]{2,1,0:T(8,128)(2,1)S(1)} %broadcast_select_fusion), channel_id=1, source_target_pairs={{0,6},{1,7},{2,0},{3,1},{4,2},{5,3},{6,4},{7,5},{8,14},{9,15},{10,... | collective-permute-start | bytes 786440 | tf_op jit(solution)/shard_map/ppermute | solution.py:296
  63.8 40.9 %all-to-all-start.1 = ((bf16[8,384,256]{2,1,0:T(8,128)(2,1)}), bf16[8,384,256]{2,1,0:T(8,128)(2,1)S(1)}, u32[]{:S(2)}, u32[]{:S(2)}) async-start(bf16[8,384,256]{2,1,0:T(8,128)(2,1)} %bitcast.5), calls=%async_computation.1 | async-start | bytes 3145728 | tf_op jit(solution)/shard_map/all_to_all | solution.py:287
  69.2 15.2 %collective-permute-start.7 = (bf16[2,64,256]{2,1,0:T(8,128)(2,1)S(1)}, bf16[2,64,256]{2,1,0:T(8,128)(2,1)S(1)}, u32[]{:S(2)}, u32[]{:S(2)}) collective-permute-start(bf16[2,64,256]{2,1,0:T(8,128)(2,1)S(1)} %pad_maximum_fusion.2), channel_id=1, source_target_pairs={{0,8},{8,0},{16,24},{24,16},{32,40},{40,32},{48,56},{56,48},{1,9},... | collective-permute-start | bytes 196616 | tf_op jit(solution)/shard_map/ppermute | solution.py:291
  84.4 7.9 %collective-permute-start.8 = (bf16[2,64,256]{2,1,0:T(8,128)(2,1)S(1)}, bf16[2,64,256]{2,1,0:T(8,128)(2,1)S(1)}, u32[]{:S(2)}, u32[]{:S(2)}) collective-permute-start(bf16[2,64,256]{2,1,0:T(8,128)(2,1)S(1)} %add_convert_fusion.2), channel_id=1, source_target_pairs={{0,64},{64,0},{128,192},{192,128},{256,320},{320,256},{384,448},{4... | collective-permute-start | bytes 196616 | tf_op jit(solution)/shard_map/ppermute | solution.py:291
  92.4 9.9 %collective-permute-start.11 = (bf16[2,64,256]{2,1,0:T(8,128)(2,1)S(1)}, bf16[2,64,256]{2,1,0:T(8,128)(2,1)S(1)}, u32[]{:S(2)}, u32[]{:S(2)}) collective-permute-start(bf16[2,64,256]{2,1,0:T(8,128)(2,1)S(1)} %add_convert_fusion.1), channel_id=1, source_target_pairs={{0,48},{8,56},{16,0},{24,8},{32,16},{40,24},{48,32},{56,40},{1,49}... | collective-permute-start | bytes 196616 | tf_op jit(solution)/shard_map/ppermute | solution.py:296
  95.7 6.6 %collective-permute-start.10 = (bf16[2,64,256]{2,1,0:T(8,128)(2,1)S(1)}, bf16[2,64,256]{2,1,0:T(8,128)(2,1)S(1)}, u32[]{:S(2)}, u32[]{:S(2)}) collective-permute-start(bf16[2,64,256]{2,1,0:T(8,128)(2,1)S(1)} %add_convert_fusion.1), channel_id=1, source_target_pairs={{0,32},{8,40},{16,48},{24,56},{32,0},{40,8},{48,16},{56,24},{1,33}... | collective-permute-start | bytes 196616 | tf_op jit(solution)/shard_map/ppermute | solution.py:296
  98.5 6.2 %collective-permute-start.9 = (bf16[2,64,256]{2,1,0:T(8,128)(2,1)S(1)}, bf16[2,64,256]{2,1,0:T(8,128)(2,1)S(1)}, u32[]{:S(2)}, u32[]{:S(2)}) collective-permute-start(bf16[2,64,256]{2,1,0:T(8,128)(2,1)S(1)} %add_convert_fusion.1), channel_id=1, source_target_pairs={{0,16},{8,24},{16,32},{24,40},{32,48},{40,56},{48,0},{56,8},{1,17}... | collective-permute-start | bytes 196616 | tf_op jit(solution)/shard_map/ppermute | solution.py:296
  106.0 10.4 %copy-start.5 = (f32[6,256]{1,0:T(8,128)S(1)}, f32[6,256]{1,0:T(8,128)}, u32[]{:S(2)}) copy-start(f32[6,256]{1,0:T(8,128)} %diag_ref.3) | copy-start | bytes 18436
  106.0 31.1 %all-to-all-start.2 = ((bf16[8,384,256]{2,1,0:T(8,128)(2,1)}), bf16[8,384,256]{2,1,0:T(8,128)(2,1)S(1)}, u32[]{:S(2)}, u32[]{:S(2)}) async-start(bf16[8,384,256]{2,1,0:T(8,128)(2,1)} %broadcast_in_dim.19), calls=%async_computation.2 | async-start | bytes 3145728 | tf_op jit(solution)/shard_map/all_to_all | solution.py:287
  116.4 11.3 %copy-start.4 = (s32[4,128]{1,0:T(4,128)S(1)}, s32[4,128]{1,0:T(4,128)}, u32[]{:S(2)}) copy-start(s32[4,128]{1,0:T(4,128)} %upper_maps_ref.1) | copy-start | bytes 6148
  125.8 10.5 %collective-permute-start.12 = (bf16[256,256]{1,0:T(8,128)(2,1)S(1)}, bf16[256,256]{1,0:T(8,128)(2,1)S(1)}, u32[]{:S(2)}, u32[]{:S(2)}) collective-permute-start(bf16[256,256]{1,0:T(8,128)(2,1)S(1)} %shard_map.66), channel_id=1, source_target_pairs={{0,128},{64,192},{128,0},{192,64},{256,384},{320,448},{384,256},{4... | collective-permute-start | bytes 393224 | tf_op jit(solution)/shard_map/ppermute | solution.py:291
  142.0 21.0 %all-to-all-start.3 = ((bf16[8,288,256]{2,1,0:T(8,128)(2,1)}), bf16[8,288,256]{2,1,0:T(8,128)(2,1)S(1)}, u32[]{:S(2)}, u32[]{:S(2)}) async-start(bf16[8,288,256]{2,1,0:T(8,128)(2,1)} %get-tuple-element.20), calls=%async_computation.3 | async-start | bytes 2359296 | tf_op jit(solution)/shard_map/all_to_all | solution.py:287
  146.3 38.5 %collective-permute-start.13 = (bf16[64,16,256]{2,1,0:T(8,128)(2,1)S(1)}, bf16[64,16,256]{2,1,0:T(8,128)(2,1)}, u32[]{:S(2)}, u32[]{:S(2)}) collective-permute-start(bf16[64,16,256]{2,1,0:T(8,128)(2,1)S(1)} %get-tuple-element.21), channel_id=1, source_target_pairs={{0,8},{8,0},{16,24},{24,16},{32,40},{40,32},{48,56},{56,48},{1,9},... | collective-permute-start | bytes 1572872 | tf_op jit(solution)/shard_map/ppermute | solution.py:291
  186.8 48.2 %all-to-all-start.4 = ((bf16[16,64,256]{2,1,0:T(8,128)(2,1)}), bf16[16,64,256]{2,1,0:T(8,128)(2,1)S(1)}, u32[]{:S(2)}, u32[]{:S(2)}) async-start(bf16[16,64,256]{2,1,0:T(8,128)(2,1)} %bitcast.26), calls=%async_computation.4 | async-start | bytes 1048576 | tf_op jit(solution)/shard_map/all_to_all | solution.py:276
  211.9 23.0 %collective-permute-start.14 = (bf16[160,256]{1,0:T(8,128)(2,1)S(1)}, bf16[160,256]{1,0:T(8,128)(2,1)S(1)}, u32[]{:S(2)}, u32[]{:S(2)}) collective-permute-start(bf16[160,256]{1,0:T(8,128)(2,1)S(1)} %slice.27), channel_id=1, source_target_pairs={{0,8},{8,0},{16,24},{24,16},{32,40},{40,32},{48,56},{56,48},{1,9},... | collective-permute-start | bytes 245768 | tf_op jit(solution)/shard_map/ppermute | solution.py:291
  252.5 18.0 %all-to-all-start.6 = ((bf16[8,16,8,256]{3,2,1,0:T(8,128)(2,1)}), bf16[8,16,8,256]{3,2,1,0:T(8,128)(2,1)S(1)}, u32[]{:S(2)}, u32[]{:S(2)}) async-start(bf16[8,16,8,256]{3,2,1,0:T(8,128)(2,1)} %broadcast_in_dim.21), calls=%async_computation.6 | async-start | bytes 1048576 | tf_op jit(solution)/shard_map/all_to_all | solution.py:287
  (3 other events, 28.1 us)

commit v10 on v8

--- a/solution.py
+++ b/solution.py
@@ -231,7 +231,7 @@
             total_ref[place] = total_ref[place] + value
             return carry
 
-        lax.fori_loop(0, half, one, 0, unroll=4)
+        lax.fori_loop(0, half, one, 0, unroll=8)
     keep_ref[...] = total_ref[:64]
     send_ref[...] = total_ref[64:128].astype(BF16)
     first = row % 2 * 64
@@ -352,10 +352,9 @@
         shares = jnp.where(away & mask == 0, shares, swapped(shares, "col", mask))
     my_tile = lax.dynamic_slice(front_slots, (level // 2, col), (1, 1))[0, 0]
     parts = jnp.stack([shares[0], picked(shares, my_tile)])
-    parts = (parts.astype(F32) + swapped(parts, "row", 1).astype(F32)).astype(BF16)
-
     chunks, parts = tied(chunks, parts)
     pieces = over_columns(chunks)
+    parts = (parts.astype(F32) + swapped(parts, "row", 1).astype(F32)).astype(BF16)
     gathered = parts[None]
     for axis, mask in (("row", 2), ("row", 4), ("level", 1)):
         gathered = jnp.concatenate([gathered, swapped(gathered, axis, mask)], axis=0)

time: 258 us -> 268 us (1.039)
  waiting for transfers between devices: 38.7 us -> 45 us
  starting transfers between devices: 139 us -> 142 us
    all_to_all x2, waiting for transfers between devices: 0.01 us -> 10.2 us  [exchange(): lax.all_to_all(value, ('level', 'row'), split_axis=0, concat_axis=0, axis...]
    all_to_all x4, starting transfers between devices: 30.3 us -> 33.8 us  [over_columns(): return lax.all_to_all(value, 'col', split_axis=0, concat_axis=0, tiled=True)]
where the time goes in v10:
time: 268 us; the launch traced here: 267 us
  starting transfers between devices  142 us (53%)
  waiting for transfers between devices  45 us (17%)
  blocking collectives  33.6 us (13%)
  Pallas kernels  29.3 us (11%)
  local copies, waits for them, and re-layouts  7.54 us (3%)
  between operations  6.81 us (3%)
    ppermute x10, starting transfers between devices, swapped(): lax.ppermute(value, axis, [(index, index ^ mask) for index in range(8)])  68 us
    all_to_all x2, starting transfers between devices, exchange(): lax.all_to_all(value, ('level', 'row'), split_axis=0, concat_axis=0, axis...  40.4 us
    all_to_all x4, starting transfers between devices, over_columns(): return lax.all_to_all(value, 'col', split_axis=0, concat_axis=0, tiled=True)  33.8 us
    all_to_all x2, blocking collectives, exchange(): lax.all_to_all(value, ('level', 'row'), split_axis=0, concat_axis=0, axis...  33.6 us
    ppermute x10, waiting for transfers between devices, swapped(): lax.ppermute(value, axis, [(index, index ^ mask) for index in range(8)])  32.7 us
    pallas_call x2, Pallas kernels, solve(): call(functools.partial(solve_kernel, front_of, place_of), jax.ShapeDtypeS...  18.7 us
    all_to_all x2, waiting for transfers between devices, exchange(): lax.all_to_all(value, ('level', 'row'), split_axis=0, concat_axis=0, axis...  10.2 us
  transfers between devices with their start and end apart: 16, of which 12 were waited for; matrix products, arithmetic and copies ran while one was open for 1% of the time, Pallas kernels for 8%

profile of v10, /device:TPU:1, one launch (start us, length us, event | category | flops | bytes accessed | tf_op | source)
XLA Modules:
  0.0 266.9 jit_solution(2777010794092927783)
XLA Ops:
  3.8 17.5 %all_to_all.40.shares_ref = bf16[8,8,32,256]{3,2,1,0:T(8,128)(2,1)S(1)} all-to-all(bf16[8,8,32,256]{3,2,1,0:T(8,128)(2,1)S(1)} %shard_map.65), channel_id=1, replica_groups={{0,16,32,48,64,80,96,112},{8,24,40,56,72,88,104,120},{128,144,160,176,1..., dimensions={0} | all-to-all | bytes 2097152 | tf_op jit(solution)/shard_map/all_to_all | solution.py:284
  22.7 8.7 %all-to-all-start.1 = ((bf16[16,12,16,256]{3,2,1,0:T(8,128)(2,1)}), bf16[16,12,16,256]{3,2,1,0:T(8,128)(2,1)}, u32[]{:S(2)}, u32[]{:S(2)}) async-start(bf16[16,12,16,256]{3,2,1,0:T(8,128)(2,1)} %copy.11), calls=%async_computation.1 | async-start | bytes 3145728 | tf_op jit(solution)/shard_map/all_to_all | solution.py:284
  31.5 4.0 %collective-permute-start = (bf16[8,32,256]{2,1,0:T(8,128)(2,1)S(1)}, bf16[8,32,256]{2,1,0:T(8,128)(2,1)S(1)}, u32[]{:S(2)}, u32[]{:S(2)}) collective-permute-start(bf16[8,32,256]{2,1,0:T(8,128)(2,1)S(1)} %shard_map.66), channel_id=1, source_target_pairs={{0,1},{1,0},{2,3},{3,2},{4,5},{5,4},{6,7},{7,6},{8,9},{9,8},{10,11... | collective-permute-start | bytes 393224 | tf_op jit(solution)/shard_map/ppermute | solution.py:299
  40.4 3.9 %collective-permute-done.1 = bf16[8,32,256]{2,1,0:T(8,128)(2,1)S(1)} collective-permute-done((bf16[8,32,256]{2,1,0:T(8,128)(2,1)S(1)}, bf16[8,32,256]{2,1,0:T(8,128)(2,1)S(1)}, u32[]{:S(2)}, u32[]{:S(2)}) %collective-permute-start.1) | collective-permute-done | bytes 131104 | tf_op jit(solution)/shard_map/ppermute | solution.py:299
  44.3 4.8 %collective-permute-start.2 = (bf16[8,32,256]{2,1,0:T(8,128)(2,1)S(1)}, bf16[8,32,256]{2,1,0:T(8,128)(2,1)S(1)}, u32[]{:S(2)}, u32[]{:S(2)}) collective-permute-start(bf16[8,32,256]{2,1,0:T(8,128)(2,1)S(1)} %broadcast_select_fusion.1), channel_id=1, source_target_pairs={{0,4},{1,5},{2,6},{3,7},{4,0},{5,1},{6,2},{7,3},{8,12},{9,13},{10,... | collective-permute-start | bytes 393224 | tf_op jit(solution)/shard_map/ppermute | solution.py:299
  52.2 10.2 %all-to-all-done.1 = bf16[16,12,16,256]{3,2,1,0:T(8,128)(2,1)} async-done(((bf16[16,12,16,256]{3,2,1,0:T(8,128)(2,1)}), bf16[16,12,16,256]{3,2,1,0:T(8,128)(2,1)}, u32[]{:S(2)}, u32[]{:S(2)}) %all-to-all-start.1) | async-done | bytes 1572896 | tf_op jit(solution)/shard_map/all_to_all | solution.py:284
  62.4 8.3 %all-to-all-start.2 = ((bf16[8,384,256]{2,1,0:T(8,128)(2,1)}), bf16[8,384,256]{2,1,0:T(8,128)(2,1)S(1)}, u32[]{:S(2)}, u32[]{:S(2)}) async-start(bf16[8,384,256]{2,1,0:T(8,128)(2,1)} %bitcast.6), calls=%async_computation.2 | async-start | bytes 3145728 | tf_op jit(solution)/shard_map/all_to_all | solution.py:295
  70.7 13.0 %collective-permute-start.3 = (bf16[2,32,256]{2,1,0:T(8,128)(2,1)S(1)}, bf16[2,32,256]{2,1,0:T(8,128)(2,1)S(1)}, u32[]{:S(2)}, u32[]{:S(2)}) collective-permute-start(bf16[2,32,256]{2,1,0:T(8,128)(2,1)S(1)} %pad_maximum_fusion.4), channel_id=1, source_target_pairs={{0,8},{8,0},{16,24},{24,16},{32,40},{40,32},{48,56},{56,48},{1,9},... | collective-permute-start | bytes 98312 | tf_op jit(solution)/shard_map/ppermute | solution.py:299
  90.5 5.2 %collective-permute-start.5 = (bf16[2,2,32,256]{3,2,1,0:T(8,128)(2,1)S(1)}, bf16[2,2,32,256]{3,2,1,0:T(8,128)(2,1)S(1)}, u32[]{:S(2)}, u32[]{:S(2)}) collective-permute-start(bf16[2,2,32,256]{3,2,1,0:T(8,128)(2,1)S(1)} %pad_maximum_fusion.3), channel_id=1, source_target_pairs={{0,32},{8,40},{16,48},{24,56},{32,0},{40,8},{48,16},{56,24},{1,33}... | collective-permute-start | bytes 196616 | tf_op jit(solution)/shard_map/ppermute | solution.py:299
  97.3 6.5 %collective-permute-start.6 = (bf16[4,2,32,256]{3,2,1,0:T(8,128)(2,1)S(1)}, bf16[4,2,32,256]{3,2,1,0:T(8,128)(2,1)S(1)}, u32[]{:S(2)}, u32[]{:S(2)}) collective-permute-start(bf16[4,2,32,256]{3,2,1,0:T(8,128)(2,1)S(1)} %pad_maximum_fusion.2), channel_id=1, source_target_pairs={{0,64},{64,0},{128,192},{192,128},{256,320},{320,256},{384,448},{4... | collective-permute-start | bytes 393224 | tf_op jit(solution)/shard_map/ppermute | solution.py:299
  107.5 7.9 %all-to-all-start.3 = ((bf16[8,384,256]{2,1,0:T(8,128)(2,1)}), bf16[8,384,256]{2,1,0:T(8,128)(2,1)S(1)}, u32[]{:S(2)}, u32[]{:S(2)}) async-start(bf16[8,384,256]{2,1,0:T(8,128)(2,1)} %broadcast_in_dim.22), calls=%async_computation.3 | async-start | bytes 3145728 | tf_op jit(solution)/shard_map/all_to_all | solution.py:295
  115.5 9.4 %shard_map.67 = bf16[256,256]{1,0:T(8,128)(2,1)S(1)} custom-call(s32[3]{0:T(128)S(1)} %pad_add_fusion.meta_ref, f32[6,256]{1,0:T(8,128)S(1)} %copy-done.7, bf16[8,2,32,256]{3,2,1,0:T(8,128)(2,1)S(1)} %pad_maximum_fusion.1.gathered_ref), custom_call_target="tpu_custom_call" | custom-call | flops 536870912 | bytes 4194304 | tf_op jit(solution)/shard_map/pallas_call | solution.py:196
  124.9 4.7 %collective-permute-start.7 = (bf16[256,256]{1,0:T(8,128)(2,1)S(1)}, bf16[256,256]{1,0:T(8,128)(2,1)S(1)}, u32[]{:S(2)}, u32[]{:S(2)}) collective-permute-start(bf16[256,256]{1,0:T(8,128)(2,1)S(1)} %shard_map.67), channel_id=1, source_target_pairs={{0,128},{64,192},{128,0},{192,64},{256,384},{320,448},{384,256},{4... | collective-permute-start | bytes 393224 | tf_op jit(solution)/shard_map/ppermute | solution.py:299
  132.5 3.7 %collective-permute-done.7 = bf16[256,256]{1,0:T(8,128)(2,1)S(1)} collective-permute-done((bf16[256,256]{1,0:T(8,128)(2,1)S(1)}, bf16[256,256]{1,0:T(8,128)(2,1)S(1)}, u32[]{:S(2)}, u32[]{:S(2)}) %collective-permute-start.7) | collective-permute-done | bytes 131104 | tf_op jit(solution)/shard_map/ppermute | solution.py:299
  136.2 4.9 %shard_map.68 = (f32[64,16,256]{2,1,0:T(8,128)S(1)}, bf16[64,16,256]{2,1,0:T(8,128)(2,1)S(1)}, bf16[8,288,256]{2,1,0:T(8,128)(2,1)}) custom-call(s32[3]{0:T(128)S(1)} %pad_add_fusion.meta_ref, s32[6,8]{1,0:T(8,128)S(1)} %copy-done.1, s32[192]{0:T(256)S(1)} %shard_map.64.place_ref, bf16[192,16,256]{2,1,0:T(8,128)(2,1)} %bitcast.9.chunks_ref, ...), custom_call_target="tpu_custom_call" | custom-call | flops 536870912 | bytes 8388608 | tf_op jit(solution)/shard_map/pallas_call | solution.py:368
  141.2 4.8 %all-to-all-start.4 = ((bf16[8,288,256]{2,1,0:T(8,128)(2,1)}), bf16[8,288,256]{2,1,0:T(8,128)(2,1)S(1)}, u32[]{:S(2)}, u32[]{:S(2)}) async-start(bf16[8,288,256]{2,1,0:T(8,128)(2,1)} %get-tuple-element.24), calls=%async_computation.4 | async-start | bytes 2359296 | tf_op jit(solution)/shard_map/all_to_all | solution.py:295
  146.0 12.5 %collective-permute-start.8 = (bf16[64,16,256]{2,1,0:T(8,128)(2,1)S(1)}, bf16[64,16,256]{2,1,0:T(8,128)(2,1)}, u32[]{:S(2)}, u32[]{:S(2)}) collective-permute-start(bf16[64,16,256]{2,1,0:T(8,128)(2,1)S(1)} %get-tuple-element.25), channel_id=1, source_target_pairs={{0,8},{8,0},{16,24},{24,16},{32,40},{40,32},{48,56},{56,48},{1,9},... | collective-permute-start | bytes 1572872 | tf_op jit(solution)/shard_map/ppermute | solution.py:299
  162.6 11.9 %collective-permute-done.8 = bf16[64,16,256]{2,1,0:T(8,128)(2,1)} collective-permute-done((bf16[64,16,256]{2,1,0:T(8,128)(2,1)S(1)}, bf16[64,16,256]{2,1,0:T(8,128)(2,1)}, u32[]{:S(2)}, u32[]{:S(2)}) %collective-permute-start.8) | collective-permute-done | bytes 524320 | tf_op jit(solution)/shard_map/ppermute | solution.py:299
  176.5 31.7 %all-to-all-start.5 = ((bf16[16,64,256]{2,1,0:T(8,128)(2,1)}), bf16[16,64,256]{2,1,0:T(8,128)(2,1)S(1)}, u32[]{:S(2)}, u32[]{:S(2)}) async-start(bf16[16,64,256]{2,1,0:T(8,128)(2,1)} %bitcast.19), calls=%async_computation.5 | async-start | bytes 1048576 | tf_op jit(solution)/shard_map/all_to_all | solution.py:284
  208.2 12.0 %collective-permute-start.9 = (bf16[160,256]{1,0:T(8,128)(2,1)S(1)}, bf16[160,256]{1,0:T(8,128)(2,1)S(1)}, u32[]{:S(2)}, u32[]{:S(2)}) collective-permute-start(bf16[160,256]{1,0:T(8,128)(2,1)S(1)} %slice.27), channel_id=1, source_target_pairs={{0,8},{8,0},{16,24},{24,16},{32,40},{40,32},{48,56},{56,48},{1,9},... | collective-permute-start | bytes 245768 | tf_op jit(solution)/shard_map/ppermute | solution.py:299
  220.3 5.6 %collective-permute-done.9 = bf16[160,256]{1,0:T(8,128)(2,1)S(1)} collective-permute-done((bf16[160,256]{1,0:T(8,128)(2,1)S(1)}, bf16[160,256]{1,0:T(8,128)(2,1)S(1)}, u32[]{:S(2)}, u32[]{:S(2)}) %collective-permute-start.9) | collective-permute-done | bytes 81952 | tf_op jit(solution)/shard_map/ppermute | solution.py:299
  226.0 16.1 %all_to_all.41 = bf16[16,40,256]{2,1,0:T(8,128)(2,1)S(1)} all-to-all(bf16[16,40,256]{2,1,0:T(8,128)(2,1)S(1)} %pad_maximum_fusion), channel_id=1, replica_groups={{0,16,32,48,64,80,96,112,128,144,160,176,192,208,224,240},{8,24,40,56,7..., dimensions={0} | all-to-all | bytes 655360 | tf_op jit(solution)/shard_map/all_to_all | solution.py:284
  242.9 12.8 %all-to-all-start.7 = ((bf16[8,16,8,256]{3,2,1,0:T(8,128)(2,1)}), bf16[8,16,8,256]{3,2,1,0:T(8,128)(2,1)S(1)}, u32[]{:S(2)}, u32[]{:S(2)}) async-start(bf16[8,16,8,256]{3,2,1,0:T(8,128)(2,1)} %broadcast_in_dim.39), calls=%async_computation.7 | async-start | bytes 1048576 | tf_op jit(solution)/shard_map/all_to_all | solution.py:295
  255.7 9.3 %shard_map.69.solved_ref = bf16[256,256]{1,0:T(8,128)(2,1)S(1)} custom-call(s32[3]{0:T(128)S(1)} %pad_add_fusion.meta_ref, f32[6,256]{1,0:T(8,128)S(1)} %copy-done.7, bf16[16,2,16,256]{3,2,1,0:T(8,128)(2,1)S(1)} %bitcast.35), custom_call_target="tpu_custom_call" | custom-call | flops 536870912 | bytes 4194304 | tf_op jit(solution)/shard_map/pallas_call | solution.py:196
  (63 shorter events, 30.5 us)
Async XLA Ops:
  0.1 1.4 copy-start
  1.5 0.7 copy-start.2
  2.2 0.7 copy-start.4
  22.7 13.0 %copy-start.1 = (s32[6,8]{1,0:T(8,128)S(1)}, s32[6,8]{1,0:T(8,128)}, u32[]{:S(2)}) copy-start(s32[6,8]{1,0:T(8,128)} %slots_ref.3) | copy-start | bytes 580
  22.7 39.7 %all-to-all-start.1 = ((bf16[16,12,16,256]{3,2,1,0:T(8,128)(2,1)}), bf16[16,12,16,256]{3,2,1,0:T(8,128)(2,1)}, u32[]{:S(2)}, u32[]{:S(2)}) async-start(bf16[16,12,16,256]{3,2,1,0:T(8,128)(2,1)} %copy.11), calls=%async_computation.1 | async-start | bytes 3145728 | tf_op jit(solution)/shard_map/all_to_all | solution.py:284
  31.5 5.6 %collective-permute-start = (bf16[8,32,256]{2,1,0:T(8,128)(2,1)S(1)}, bf16[8,32,256]{2,1,0:T(8,128)(2,1)S(1)}, u32[]{:S(2)}, u32[]{:S(2)}) collective-permute-start(bf16[8,32,256]{2,1,0:T(8,128)(2,1)S(1)} %shard_map.66), channel_id=1, source_target_pairs={{0,1},{1,0},{2,3},{3,2},{4,5},{5,4},{6,7},{7,6},{8,9},{9,8},{10,11... | collective-permute-start | bytes 393224 | tf_op jit(solution)/shard_map/ppermute | solution.py:299
  37.1 7.1 %collective-permute-start.1 = (bf16[8,32,256]{2,1,0:T(8,128)(2,1)S(1)}, bf16[8,32,256]{2,1,0:T(8,128)(2,1)S(1)}, u32[]{:S(2)}, u32[]{:S(2)}) collective-permute-start(bf16[8,32,256]{2,1,0:T(8,128)(2,1)S(1)} %broadcast_select_fusion), channel_id=1, source_target_pairs={{0,2},{1,3},{2,0},{3,1},{4,6},{5,7},{6,4},{7,5},{8,10},{9,11},{10,... | collective-permute-start | bytes 393224 | tf_op jit(solution)/shard_map/ppermute | solution.py:299
  44.3 7.9 %collective-permute-start.2 = (bf16[8,32,256]{2,1,0:T(8,128)(2,1)S(1)}, bf16[8,32,256]{2,1,0:T(8,128)(2,1)S(1)}, u32[]{:S(2)}, u32[]{:S(2)}) collective-permute-start(bf16[8,32,256]{2,1,0:T(8,128)(2,1)S(1)} %broadcast_select_fusion.1), channel_id=1, source_target_pairs={{0,4},{1,5},{2,6},{3,7},{4,0},{5,1},{6,2},{7,3},{8,12},{9,13},{10,... | collective-permute-start | bytes 393224 | tf_op jit(solution)/shard_map/ppermute | solution.py:299
  62.4 43.9 %all-to-all-start.2 = ((bf16[8,384,256]{2,1,0:T(8,128)(2,1)}), bf16[8,384,256]{2,1,0:T(8,128)(2,1)S(1)}, u32[]{:S(2)}, u32[]{:S(2)}) async-start(bf16[8,384,256]{2,1,0:T(8,128)(2,1)} %bitcast.6), calls=%async_computation.2 | async-start | bytes 3145728 | tf_op jit(solution)/shard_map/all_to_all | solution.py:295
  70.7 14.8 %collective-permute-start.3 = (bf16[2,32,256]{2,1,0:T(8,128)(2,1)S(1)}, bf16[2,32,256]{2,1,0:T(8,128)(2,1)S(1)}, u32[]{:S(2)}, u32[]{:S(2)}) collective-permute-start(bf16[2,32,256]{2,1,0:T(8,128)(2,1)S(1)} %pad_maximum_fusion.4), channel_id=1, source_target_pairs={{0,8},{8,0},{16,24},{24,16},{32,40},{40,32},{48,56},{56,48},{1,9},... | collective-permute-start | bytes 98312 | tf_op jit(solution)/shard_map/ppermute | solution.py:299
  85.5 5.0 %collective-permute-start.4 = (bf16[1,2,32,256]{3,2,1,0:T(8,128)(2,1)S(1)}, bf16[1,2,32,256]{3,2,1,0:T(8,128)(2,1)S(1)}, u32[]{:S(2)}, u32[]{:S(2)}) collective-permute-start(bf16[1,2,32,256]{3,2,1,0:T(8,128)(2,1)S(1)} %fusion.2), channel_id=1, source_target_pairs={{0,16},{8,24},{16,0},{24,8},{32,48},{40,56},{48,32},{56,40},{1,17}... | collective-permute-start | bytes 98312 | tf_op jit(solution)/shard_map/ppermute | solution.py:299
  90.5 6.8 %collective-permute-start.5 = (bf16[2,2,32,256]{3,2,1,0:T(8,128)(2,1)S(1)}, bf16[2,2,32,256]{3,2,1,0:T(8,128)(2,1)S(1)}, u32[]{:S(2)}, u32[]{:S(2)}) collective-permute-start(bf16[2,2,32,256]{3,2,1,0:T(8,128)(2,1)S(1)} %pad_maximum_fusion.3), channel_id=1, source_target_pairs={{0,32},{8,40},{16,48},{24,56},{32,0},{40,8},{48,16},{56,24},{1,33}... | collective-permute-start | bytes 196616 | tf_op jit(solution)/shard_map/ppermute | solution.py:299
  97.3 8.8 %collective-permute-start.6 = (bf16[4,2,32,256]{3,2,1,0:T(8,128)(2,1)S(1)}, bf16[4,2,32,256]{3,2,1,0:T(8,128)(2,1)S(1)}, u32[]{:S(2)}, u32[]{:S(2)}) collective-permute-start(bf16[4,2,32,256]{3,2,1,0:T(8,128)(2,1)S(1)} %pad_maximum_fusion.2), channel_id=1, source_target_pairs={{0,64},{64,0},{128,192},{192,128},{256,320},{320,256},{384,448},{4... | collective-permute-start | bytes 393224 | tf_op jit(solution)/shard_map/ppermute | solution.py:299
  107.5 7.9 %copy-start.7 = (f32[6,256]{1,0:T(8,128)S(1)}, f32[6,256]{1,0:T(8,128)}, u32[]{:S(2)}) copy-start(f32[6,256]{1,0:T(8,128)} %diag_ref.3) | copy-start | bytes 18436
  107.5 28.7 %all-to-all-start.3 = ((bf16[8,384,256]{2,1,0:T(8,128)(2,1)}), bf16[8,384,256]{2,1,0:T(8,128)(2,1)S(1)}, u32[]{:S(2)}, u32[]{:S(2)}) async-start(bf16[8,384,256]{2,1,0:T(8,128)(2,1)} %broadcast_in_dim.22), calls=%async_computation.3 | async-start | bytes 3145728 | tf_op jit(solution)/shard_map/all_to_all | solution.py:295
  115.4 14.1 %copy-start.3 = (s32[8,96]{1,0:T(8,128)S(1)}, s32[8,96]{1,0:T(8,128)}, u32[]{:S(2)}) copy-start(s32[8,96]{1,0:T(8,128)} %leaf_maps_ref.3) | copy-start | bytes 9220
  115.4 14.2 %copy-start.5 = (s32[8]{0:T(128)S(1)}, s32[8]{0:T(128)}, u32[]{:S(2)}) copy-start(s32[8]{0:T(128)} %tiles_ref.3) | copy-start | bytes 100
  115.4 14.2 %copy-start.6 = (s32[4,128]{1,0:T(4,128)S(1)}, s32[4,128]{1,0:T(4,128)}, u32[]{:S(2)}) copy-start(s32[4,128]{1,0:T(4,128)} %upper_maps_ref.1) | copy-start | bytes 6148
  124.9 11.3 %collective-permute-start.7 = (bf16[256,256]{1,0:T(8,128)(2,1)S(1)}, bf16[256,256]{1,0:T(8,128)(2,1)S(1)}, u32[]{:S(2)}, u32[]{:S(2)}) collective-permute-start(bf16[256,256]{1,0:T(8,128)(2,1)S(1)} %shard_map.67), channel_id=1, source_target_pairs={{0,128},{64,192},{128,0},{192,64},{256,384},{320,448},{384,256},{4... | collective-permute-start | bytes 393224 | tf_op jit(solution)/shard_map/ppermute | solution.py:299
  141.2 21.4 %all-to-all-start.4 = ((bf16[8,288,256]{2,1,0:T(8,128)(2,1)}), bf16[8,288,256]{2,1,0:T(8,128)(2,1)S(1)}, u32[]{:S(2)}, u32[]{:S(2)}) async-start(bf16[8,288,256]{2,1,0:T(8,128)(2,1)} %get-tuple-element.24), calls=%async_computation.4 | async-start | bytes 2359296 | tf_op jit(solution)/shard_map/all_to_all | solution.py:295
  146.0 28.5 %collective-permute-start.8 = (bf16[64,16,256]{2,1,0:T(8,128)(2,1)S(1)}, bf16[64,16,256]{2,1,0:T(8,128)(2,1)}, u32[]{:S(2)}, u32[]{:S(2)}) collective-permute-start(bf16[64,16,256]{2,1,0:T(8,128)(2,1)S(1)} %get-tuple-element.25), channel_id=1, source_target_pairs={{0,8},{8,0},{16,24},{24,16},{32,40},{40,32},{48,56},{56,48},{1,9},... | collective-permute-start | bytes 1572872 | tf_op jit(solution)/shard_map/ppermute | solution.py:299
  176.5 49.5 %all-to-all-start.5 = ((bf16[16,64,256]{2,1,0:T(8,128)(2,1)}), bf16[16,64,256]{2,1,0:T(8,128)(2,1)S(1)}, u32[]{:S(2)}, u32[]{:S(2)}) async-start(bf16[16,64,256]{2,1,0:T(8,128)(2,1)} %bitcast.19), calls=%async_computation.5 | async-start | bytes 1048576 | tf_op jit(solution)/shard_map/all_to_all | solution.py:284
  208.2 17.7 %collective-permute-start.9 = (bf16[160,256]{1,0:T(8,128)(2,1)S(1)}, bf16[160,256]{1,0:T(8,128)(2,1)S(1)}, u32[]{:S(2)}, u32[]{:S(2)}) collective-permute-start(bf16[160,256]{1,0:T(8,128)(2,1)S(1)} %slice.27), channel_id=1, source_target_pairs={{0,8},{8,0},{16,24},{24,16},{32,40},{40,32},{48,56},{56,48},{1,9},... | collective-permute-start | bytes 245768 | tf_op jit(solution)/shard_map/ppermute | solution.py:299
  242.9 22.3 %all-to-all-start.7 = ((bf16[8,16,8,256]{3,2,1,0:T(8,128)(2,1)}), bf16[8,16,8,256]{3,2,1,0:T(8,128)(2,1)S(1)}, u32[]{:S(2)}, u32[]{:S(2)}) async-start(bf16[8,16,8,256]{3,2,1,0:T(8,128)(2,1)} %broadcast_in_dim.39), calls=%async_computation.7 | async-start | bytes 1048576 | tf_op jit(solution)/shard_map/all_to_all | solution.py:295

commit v11 on v8

--- a/solution.py
+++ b/solution.py
@@ -384,17 +384,18 @@
     spread = picked(over_columns(spread), picked(slots, 4 + level // 4))
     spread, sent = tied(spread, sent)
     front = (keep + sent.astype(F32)).astype(BF16)
-    front = exchange(front.reshape(16, 4 * sixteenth, tile), 4)
     spread = spread.astype(F32)
     passed = swapped(spread[8 * sixteenth :].astype(BF16), "row", 1).astype(F32)
     piece = (spread[: 8 * sixteenth] + passed[: 8 * sixteenth]).astype(BF16)
     parts = (spread[16 * sixteenth :] + passed[8 * sixteenth :]).astype(BF16)
-    piece = jnp.concatenate([piece.reshape(16, -1, tile), repeated(parts, 16)], axis=1)
-    piece, front = tied(piece, front)
+    half, whole = sixteenth // 2, 4 * sixteenth
+    piece = jnp.concatenate(
+        [front.reshape(16, whole, tile), repeated(parts, 16), piece.reshape(16, half, tile)], axis=1
+    )
     piece = exchange(piece, 4)
-    half = sixteenth // 2
-    gathered = piece[:, half:].reshape(16, 2, sixteenth, tile)
-    pivot_columns = over_columns(repeated(piece[:, :half], 8)).reshape(4, 2, 16, half, tile)
+    front = piece[:, :whole]
+    gathered = piece[:, whole:-half].reshape(16, 2, sixteenth, tile)
+    pivot_columns = over_columns(repeated(piece[:, -half:], 8)).reshape(4, 2, 16, half, tile)
     pivot_columns = jnp.swapaxes(pivot_columns, 1, 2).reshape(-1, tile)
     solved = solve(upper_front, no_place, meta, pivot_diag, gathered)
     result = call(

time: 258 us -> 251 us (0.973)
  starting transfers between devices: 139 us -> 102 us
  waiting for transfers between devices: 38.7 us -> 58 us
  blocking collectives: 33.6 us -> 44.8 us
    all_to_all x2 -> x1, starting transfers between devices: 40.9 us -> 8.68 us  [exchange(): lax.all_to_all(value, ('level', 'row'), split_axis=0, concat_axis=0, axis...]
    ppermute x10, waiting for transfers between devices: 35.3 us -> 54.5 us  [swapped(): lax.ppermute(value, axis, [(index, index ^ mask) for index in range(8)])]
    all_to_all x2, blocking collectives: 33.6 us -> 44.8 us  [exchange(): lax.all_to_all(value, ('level', 'row'), split_axis=0, concat_axis=0, axis...]
    all_to_all x4, starting transfers between devices: 30.3 us -> 25.5 us  [over_columns(): return lax.all_to_all(value, 'col', split_axis=0, concat_axis=0, tiled=True)]
  transfers between devices with their start and end apart: 16 -> 15, of which waited for: 12 -> 12; matrix products, arithmetic and copies ran while one was open for 1% -> 1% of each run, Pallas kernels for 8% -> 9%
where the time goes in v11:
time: 251 us; the launch traced here: 250 us
  starting transfers between devices  102 us (41%)
  waiting for transfers between devices  58 us (23%)
  blocking collectives  44.8 us (18%)
  Pallas kernels  29.2 us (12%)
  local copies, waits for them, and re-layouts  7.59 us (3%)
  between operations  6.64 us (3%)
    ppermute x10, starting transfers between devices, swapped(): lax.ppermute(value, axis, [(index, index ^ mask) for index in range(8)])  67.5 us
    ppermute x10, waiting for transfers between devices, swapped(): lax.ppermute(value, axis, [(index, index ^ mask) for index in range(8)])  54.5 us
    all_to_all x2, blocking collectives, exchange(): lax.all_to_all(value, ('level', 'row'), split_axis=0, concat_axis=0, axis...  44.8 us
    all_to_all x4, starting transfers between devices, over_columns(): return lax.all_to_all(value, 'col', split_axis=0, concat_axis=0, tiled=True)  25.5 us
    pallas_call x2, Pallas kernels, solve(): call(functools.partial(solve_kernel, front_of, place_of), jax.ShapeDtypeS...  18.7 us
    all_to_all x1, starting transfers between devices, exchange(): lax.all_to_all(value, ('level', 'row'), split_axis=0, concat_axis=0, axis...  8.68 us
  transfers between devices with their start and end apart: 15, of which 12 were waited for; matrix products, arithmetic and copies ran while one was open for 1% of the time, Pallas kernels for 9%

profile of v11, /device:TPU:1, one launch (start us, length us, event | category | flops | bytes accessed | tf_op | source)
XLA Modules:
  0.0 249.7 jit_solution(13635012151501612455)
XLA Ops:
  3.8 17.5 %all_to_all.35.shares_ref = bf16[8,8,32,256]{3,2,1,0:T(8,128)(2,1)S(1)} all-to-all(bf16[8,8,32,256]{3,2,1,0:T(8,128)(2,1)S(1)} %shard_map.65), channel_id=1, replica_groups={{0,16,32,48,64,80,96,112},{8,24,40,56,72,88,104,120},{128,144,160,176,1..., dimensions={0} | all-to-all | bytes 2097152 | tf_op jit(solution)/shard_map/all_to_all | solution.py:284
  22.7 8.7 %all-to-all-start.1 = ((bf16[16,12,16,256]{3,2,1,0:T(8,128)(2,1)}), bf16[16,12,16,256]{3,2,1,0:T(8,128)(2,1)}, u32[]{:S(2)}, u32[]{:S(2)}) async-start(bf16[16,12,16,256]{3,2,1,0:T(8,128)(2,1)} %copy.11), calls=%async_computation.1 | async-start | bytes 3145728 | tf_op jit(solution)/shard_map/all_to_all | solution.py:284
  31.5 4.0 %collective-permute-start = (bf16[8,32,256]{2,1,0:T(8,128)(2,1)S(1)}, bf16[8,32,256]{2,1,0:T(8,128)(2,1)S(1)}, u32[]{:S(2)}, u32[]{:S(2)}) collective-permute-start(bf16[8,32,256]{2,1,0:T(8,128)(2,1)S(1)} %shard_map.66), channel_id=1, source_target_pairs={{0,1},{1,0},{2,3},{3,2},{4,5},{5,4},{6,7},{7,6},{8,9},{9,8},{10,11... | collective-permute-start | bytes 393224 | tf_op jit(solution)/shard_map/ppermute | solution.py:299
  37.1 3.2 %collective-permute-start.1 = (bf16[8,32,256]{2,1,0:T(8,128)(2,1)S(1)}, bf16[8,32,256]{2,1,0:T(8,128)(2,1)S(1)}, u32[]{:S(2)}, u32[]{:S(2)}) collective-permute-start(bf16[8,32,256]{2,1,0:T(8,128)(2,1)S(1)} %broadcast_select_fusion), channel_id=1, source_target_pairs={{0,2},{1,3},{2,0},{3,1},{4,6},{5,7},{6,4},{7,5},{8,10},{9,11},{10,... | collective-permute-start | bytes 393224 | tf_op jit(solution)/shard_map/ppermute | solution.py:299
  40.4 3.9 %collective-permute-done.1 = bf16[8,32,256]{2,1,0:T(8,128)(2,1)S(1)} collective-permute-done((bf16[8,32,256]{2,1,0:T(8,128)(2,1)S(1)}, bf16[8,32,256]{2,1,0:T(8,128)(2,1)S(1)}, u32[]{:S(2)}, u32[]{:S(2)}) %collective-permute-start.1) | collective-permute-done | bytes 131104 | tf_op jit(solution)/shard_map/ppermute | solution.py:299
  44.3 4.8 %collective-permute-start.2 = (bf16[8,32,256]{2,1,0:T(8,128)(2,1)S(1)}, bf16[8,32,256]{2,1,0:T(8,128)(2,1)S(1)}, u32[]{:S(2)}, u32[]{:S(2)}) collective-permute-start(bf16[8,32,256]{2,1,0:T(8,128)(2,1)S(1)} %broadcast_select_fusion.1), channel_id=1, source_target_pairs={{0,4},{1,5},{2,6},{3,7},{4,0},{5,1},{6,2},{7,3},{8,12},{9,13},{10,... | collective-permute-start | bytes 393224 | tf_op jit(solution)/shard_map/ppermute | solution.py:299
  52.2 13.5 %collective-permute-start.3 = (bf16[2,32,256]{2,1,0:T(8,128)(2,1)S(1)}, bf16[2,32,256]{2,1,0:T(8,128)(2,1)S(1)}, u32[]{:S(2)}, u32[]{:S(2)}) collective-permute-start(bf16[2,32,256]{2,1,0:T(8,128)(2,1)S(1)} %pad_maximum_fusion.4), channel_id=1, source_target_pairs={{0,8},{8,0},{16,24},{24,16},{32,40},{40,32},{48,56},{56,48},{1,9},... | collective-permute-start | bytes 98312 | tf_op jit(solution)/shard_map/ppermute | solution.py:299
  67.6 7.3 %all-to-all-start.2 = ((bf16[8,384,256]{2,1,0:T(8,128)(2,1)}), bf16[8,384,256]{2,1,0:T(8,128)(2,1)S(1)}, u32[]{:S(2)}, u32[]{:S(2)}) async-start(bf16[8,384,256]{2,1,0:T(8,128)(2,1)} %bitcast.6), calls=%async_computation.2 | async-start | bytes 3145728 | tf_op jit(solution)/shard_map/all_to_all | solution.py:295
  74.9 3.4 %collective-permute-start.4 = (bf16[1,2,32,256]{3,2,1,0:T(8,128)(2,1)S(1)}, bf16[1,2,32,256]{3,2,1,0:T(8,128)(2,1)S(1)}, u32[]{:S(2)}, u32[]{:S(2)}) collective-permute-start(bf16[1,2,32,256]{3,2,1,0:T(8,128)(2,1)S(1)} %bitcast.38), channel_id=1, source_target_pairs={{0,16},{8,24},{16,0},{24,8},{32,48},{40,56},{48,32},{56,40},{1,17}... | collective-permute-start | bytes 98312 | tf_op jit(solution)/shard_map/ppermute | solution.py:299
  80.0 4.7 %collective-permute-start.5 = (bf16[2,2,32,256]{3,2,1,0:T(8,128)(2,1)S(1)}, bf16[2,2,32,256]{3,2,1,0:T(8,128)(2,1)S(1)}, u32[]{:S(2)}, u32[]{:S(2)}) collective-permute-start(bf16[2,2,32,256]{3,2,1,0:T(8,128)(2,1)S(1)} %pad_maximum_fusion.3), channel_id=1, source_target_pairs={{0,32},{8,40},{16,48},{24,56},{32,0},{40,8},{48,16},{56,24},{1,33}... | collective-permute-start | bytes 196616 | tf_op jit(solution)/shard_map/ppermute | solution.py:299
  92.6 3.1 %all-to-all-done.2 = bf16[8,384,256]{2,1,0:T(8,128)(2,1)S(1)} async-done(((bf16[8,384,256]{2,1,0:T(8,128)(2,1)}), bf16[8,384,256]{2,1,0:T(8,128)(2,1)S(1)}, u32[]{:S(2)}, u32[]{:S(2)}) %all-to-all-start.2) | async-done | bytes 1572896 | tf_op jit(solution)/shard_map/all_to_all | solution.py:295
  96.9 4.6 %all-to-all-start.3 = ((bf16[8,384,256]{2,1,0:T(8,128)(2,1)}), bf16[8,384,256]{2,1,0:T(8,128)(2,1)S(1)}, u32[]{:S(2)}, u32[]{:S(2)}) async-start(bf16[8,384,256]{2,1,0:T(8,128)(2,1)} %broadcast_in_dim.22), calls=%async_computation.3 | async-start | bytes 3145728 | tf_op jit(solution)/shard_map/all_to_all | solution.py:295
  101.6 9.4 %shard_map.67 = bf16[256,256]{1,0:T(8,128)(2,1)S(1)} custom-call(s32[3]{0:T(128)S(1)} %pad_add_fusion.meta_ref, f32[6,256]{1,0:T(8,128)S(1)} %copy-done.7, bf16[8,2,32,256]{3,2,1,0:T(8,128)(2,1)S(1)} %pad_maximum_fusion.1.gathered_ref), custom_call_target="tpu_custom_call" | custom-call | flops 536870912 | bytes 4194304 | tf_op jit(solution)/shard_map/pallas_call | solution.py:196
  111.0 4.8 %collective-permute-start.7 = (bf16[256,256]{1,0:T(8,128)(2,1)S(1)}, bf16[256,256]{1,0:T(8,128)(2,1)S(1)}, u32[]{:S(2)}, u32[]{:S(2)}) collective-permute-start(bf16[256,256]{1,0:T(8,128)(2,1)S(1)} %shard_map.67), channel_id=1, source_target_pairs={{0,128},{64,192},{128,0},{192,64},{256,384},{320,448},{384,256},{4... | collective-permute-start | bytes 393224 | tf_op jit(solution)/shard_map/ppermute | solution.py:299
  118.7 3.7 %collective-permute-done.7 = bf16[256,256]{1,0:T(8,128)(2,1)S(1)} collective-permute-done((bf16[256,256]{1,0:T(8,128)(2,1)S(1)}, bf16[256,256]{1,0:T(8,128)(2,1)S(1)}, u32[]{:S(2)}, u32[]{:S(2)}) %collective-permute-start.7) | collective-permute-done | bytes 131104 | tf_op jit(solution)/shard_map/ppermute | solution.py:299
  122.4 4.9 %shard_map.68 = (f32[64,16,256]{2,1,0:T(8,128)S(1)}, bf16[64,16,256]{2,1,0:T(8,128)(2,1)S(1)}, bf16[8,288,256]{2,1,0:T(8,128)(2,1)}) custom-call(s32[3]{0:T(128)S(1)} %pad_add_fusion.meta_ref, s32[6,8]{1,0:T(8,128)S(1)} %copy-done.1, s32[192]{0:T(256)S(1)} %shard_map.64.place_ref, bf16[192,16,256]{2,1,0:T(8,128)(2,1)} %bitcast.9.chunks_ref, ...), custom_call_target="tpu_custom_call" | custom-call | flops 536870912 | bytes 8388608 | tf_op jit(solution)/shard_map/pallas_call | solution.py:369
  127.3 5.0 %all-to-all-start.4 = ((bf16[8,288,256]{2,1,0:T(8,128)(2,1)}), bf16[8,288,256]{2,1,0:T(8,128)(2,1)S(1)}, u32[]{:S(2)}, u32[]{:S(2)}) async-start(bf16[8,288,256]{2,1,0:T(8,128)(2,1)} %get-tuple-element.23), calls=%async_computation.4 | async-start | bytes 2359296 | tf_op jit(solution)/shard_map/all_to_all | solution.py:295
  132.4 14.5 %collective-permute-start.8 = (bf16[64,16,256]{2,1,0:T(8,128)(2,1)S(1)}, bf16[64,16,256]{2,1,0:T(8,128)(2,1)}, u32[]{:S(2)}, u32[]{:S(2)}) collective-permute-start(bf16[64,16,256]{2,1,0:T(8,128)(2,1)S(1)} %get-tuple-element.24), channel_id=1, source_target_pairs={{0,8},{8,0},{16,24},{24,16},{32,40},{40,32},{48,56},{56,48},{1,9},... | collective-permute-start | bytes 1572872 | tf_op jit(solution)/shard_map/ppermute | solution.py:299
  149.0 13.6 %collective-permute-done.8 = bf16[64,16,256]{2,1,0:T(8,128)(2,1)} collective-permute-done((bf16[64,16,256]{2,1,0:T(8,128)(2,1)S(1)}, bf16[64,16,256]{2,1,0:T(8,128)(2,1)}, u32[]{:S(2)}, u32[]{:S(2)}) %collective-permute-start.8) | collective-permute-done | bytes 524320 | tf_op jit(solution)/shard_map/ppermute | solution.py:299
  162.6 12.0 %collective-permute-start.9 = (bf16[160,256]{1,0:T(8,128)(2,1)S(1)}, bf16[160,256]{1,0:T(8,128)(2,1)S(1)}, u32[]{:S(2)}, u32[]{:S(2)}) collective-permute-start(bf16[160,256]{1,0:T(8,128)(2,1)S(1)} %slice.30), channel_id=1, source_target_pairs={{0,8},{8,0},{16,24},{24,16},{32,40},{40,32},{48,56},{56,48},{1,9},... | collective-permute-start | bytes 245768 | tf_op jit(solution)/shard_map/ppermute | solution.py:299
  175.9 25.8 %collective-permute-done.9 = bf16[160,256]{1,0:T(8,128)(2,1)S(1)} collective-permute-done((bf16[160,256]{1,0:T(8,128)(2,1)S(1)}, bf16[160,256]{1,0:T(8,128)(2,1)S(1)}, u32[]{:S(2)}, u32[]{:S(2)}) %collective-permute-start.9) | collective-permute-done | bytes 81952 | tf_op jit(solution)/shard_map/ppermute | solution.py:299
  201.8 27.3 %all_to_all.36 = bf16[16,104,256]{2,1,0:T(8,128)(2,1)S(1)} all-to-all(bf16[16,104,256]{2,1,0:T(8,128)(2,1)S(1)} %pad_maximum_fusion), channel_id=1, replica_groups={{0,16,32,48,64,80,96,112,128,144,160,176,192,208,224,240},{8,24,40,56,7..., dimensions={0} | all-to-all | bytes 1703936 | tf_op jit(solution)/shard_map/all_to_all | solution.py:284
  229.9 8.6 %all-to-all-start.6 = ((bf16[8,16,8,256]{3,2,1,0:T(8,128)(2,1)}), bf16[8,16,8,256]{3,2,1,0:T(8,128)(2,1)S(1)}, u32[]{:S(2)}, u32[]{:S(2)}) async-start(bf16[8,16,8,256]{3,2,1,0:T(8,128)(2,1)} %broadcast_in_dim.39), calls=%async_computation.6 | async-start | bytes 1048576 | tf_op jit(solution)/shard_map/all_to_all | solution.py:295
  238.5 9.3 %shard_map.69.solved_ref = bf16[256,256]{1,0:T(8,128)(2,1)S(1)} custom-call(s32[3]{0:T(128)S(1)} %pad_add_fusion.meta_ref, f32[6,256]{1,0:T(8,128)S(1)} %copy-done.7, bf16[16,2,16,256]{3,2,1,0:T(8,128)(2,1)S(1)} %bitcast.34), custom_call_target="tpu_custom_call" | custom-call | flops 536870912 | bytes 4194304 | tf_op jit(solution)/shard_map/pallas_call | solution.py:196
  (62 shorter events, 25.5 us)
Async XLA Ops:
  0.1 1.4 copy-start
  1.5 0.7 copy-start.2
  2.2 0.7 copy-start.4
  22.7 12.9 %copy-start.1 = (s32[6,8]{1,0:T(8,128)S(1)}, s32[6,8]{1,0:T(8,128)}, u32[]{:S(2)}) copy-start(s32[6,8]{1,0:T(8,128)} %slots_ref.3) | copy-start | bytes 580
  22.7 44.9 %all-to-all-start.1 = ((bf16[16,12,16,256]{3,2,1,0:T(8,128)(2,1)}), bf16[16,12,16,256]{3,2,1,0:T(8,128)(2,1)}, u32[]{:S(2)}, u32[]{:S(2)}) async-start(bf16[16,12,16,256]{3,2,1,0:T(8,128)(2,1)} %copy.11), calls=%async_computation.1 | async-start | bytes 3145728 | tf_op jit(solution)/shard_map/all_to_all | solution.py:284
  31.5 5.6 %collective-permute-start = (bf16[8,32,256]{2,1,0:T(8,128)(2,1)S(1)}, bf16[8,32,256]{2,1,0:T(8,128)(2,1)S(1)}, u32[]{:S(2)}, u32[]{:S(2)}) collective-permute-start(bf16[8,32,256]{2,1,0:T(8,128)(2,1)S(1)} %shard_map.66), channel_id=1, source_target_pairs={{0,1},{1,0},{2,3},{3,2},{4,5},{5,4},{6,7},{7,6},{8,9},{9,8},{10,11... | collective-permute-start | bytes 393224 | tf_op jit(solution)/shard_map/ppermute | solution.py:299
  37.1 7.1 %collective-permute-start.1 = (bf16[8,32,256]{2,1,0:T(8,128)(2,1)S(1)}, bf16[8,32,256]{2,1,0:T(8,128)(2,1)S(1)}, u32[]{:S(2)}, u32[]{:S(2)}) collective-permute-start(bf16[8,32,256]{2,1,0:T(8,128)(2,1)S(1)} %broadcast_select_fusion), channel_id=1, source_target_pairs={{0,2},{1,3},{2,0},{3,1},{4,6},{5,7},{6,4},{7,5},{8,10},{9,11},{10,... | collective-permute-start | bytes 393224 | tf_op jit(solution)/shard_map/ppermute | solution.py:299
  44.3 7.9 %collective-permute-start.2 = (bf16[8,32,256]{2,1,0:T(8,128)(2,1)S(1)}, bf16[8,32,256]{2,1,0:T(8,128)(2,1)S(1)}, u32[]{:S(2)}, u32[]{:S(2)}) collective-permute-start(bf16[8,32,256]{2,1,0:T(8,128)(2,1)S(1)} %broadcast_select_fusion.1), channel_id=1, source_target_pairs={{0,4},{1,5},{2,6},{3,7},{4,0},{5,1},{6,2},{7,3},{8,12},{9,13},{10,... | collective-permute-start | bytes 393224 | tf_op jit(solution)/shard_map/ppermute | solution.py:299
  52.2 15.4 %collective-permute-start.3 = (bf16[2,32,256]{2,1,0:T(8,128)(2,1)S(1)}, bf16[2,32,256]{2,1,0:T(8,128)(2,1)S(1)}, u32[]{:S(2)}, u32[]{:S(2)}) collective-permute-start(bf16[2,32,256]{2,1,0:T(8,128)(2,1)S(1)} %pad_maximum_fusion.4), channel_id=1, source_target_pairs={{0,8},{8,0},{16,24},{24,16},{32,40},{40,32},{48,56},{56,48},{1,9},... | collective-permute-start | bytes 98312 | tf_op jit(solution)/shard_map/ppermute | solution.py:299
  67.6 28.0 %all-to-all-start.2 = ((bf16[8,384,256]{2,1,0:T(8,128)(2,1)}), bf16[8,384,256]{2,1,0:T(8,128)(2,1)S(1)}, u32[]{:S(2)}, u32[]{:S(2)}) async-start(bf16[8,384,256]{2,1,0:T(8,128)(2,1)} %bitcast.6), calls=%async_computation.2 | async-start | bytes 3145728 | tf_op jit(solution)/shard_map/all_to_all | solution.py:295
  74.9 5.0 %collective-permute-start.4 = (bf16[1,2,32,256]{3,2,1,0:T(8,128)(2,1)S(1)}, bf16[1,2,32,256]{3,2,1,0:T(8,128)(2,1)S(1)}, u32[]{:S(2)}, u32[]{:S(2)}) collective-permute-start(bf16[1,2,32,256]{3,2,1,0:T(8,128)(2,1)S(1)} %bitcast.38), channel_id=1, source_target_pairs={{0,16},{8,24},{16,0},{24,8},{32,48},{40,56},{48,32},{56,40},{1,17}... | collective-permute-start | bytes 98312 | tf_op jit(solution)/shard_map/ppermute | solution.py:299
  80.0 6.5 %collective-permute-start.5 = (bf16[2,2,32,256]{3,2,1,0:T(8,128)(2,1)S(1)}, bf16[2,2,32,256]{3,2,1,0:T(8,128)(2,1)S(1)}, u32[]{:S(2)}, u32[]{:S(2)}) collective-permute-start(bf16[2,2,32,256]{3,2,1,0:T(8,128)(2,1)S(1)} %pad_maximum_fusion.3), channel_id=1, source_target_pairs={{0,32},{8,40},{16,48},{24,56},{32,0},{40,8},{48,16},{56,24},{1,33}... | collective-permute-start | bytes 196616 | tf_op jit(solution)/shard_map/ppermute | solution.py:299
  86.5 6.0 %collective-permute-start.6 = (bf16[4,2,32,256]{3,2,1,0:T(8,128)(2,1)S(1)}, bf16[4,2,32,256]{3,2,1,0:T(8,128)(2,1)S(1)}, u32[]{:S(2)}, u32[]{:S(2)}) collective-permute-start(bf16[4,2,32,256]{3,2,1,0:T(8,128)(2,1)S(1)} %pad_maximum_fusion.2), channel_id=1, source_target_pairs={{0,64},{64,0},{128,192},{192,128},{256,320},{320,256},{384,448},{4... | collective-permute-start | bytes 393224 | tf_op jit(solution)/shard_map/ppermute | solution.py:299
  96.9 4.6 %copy-start.7 = (f32[6,256]{1,0:T(8,128)S(1)}, f32[6,256]{1,0:T(8,128)}, u32[]{:S(2)}) copy-start(f32[6,256]{1,0:T(8,128)} %diag_ref.3) | copy-start | bytes 18436
  96.9 25.5 %all-to-all-start.3 = ((bf16[8,384,256]{2,1,0:T(8,128)(2,1)}), bf16[8,384,256]{2,1,0:T(8,128)(2,1)S(1)}, u32[]{:S(2)}, u32[]{:S(2)}) async-start(bf16[8,384,256]{2,1,0:T(8,128)(2,1)} %broadcast_in_dim.22), calls=%async_computation.3 | async-start | bytes 3145728 | tf_op jit(solution)/shard_map/all_to_all | solution.py:295
  101.5 14.2 %copy-start.3 = (s32[8,96]{1,0:T(8,128)S(1)}, s32[8,96]{1,0:T(8,128)}, u32[]{:S(2)}) copy-start(s32[8,96]{1,0:T(8,128)} %leaf_maps_ref.3) | copy-start | bytes 9220
  101.5 14.2 %copy-start.5 = (s32[8]{0:T(128)S(1)}, s32[8]{0:T(128)}, u32[]{:S(2)}) copy-start(s32[8]{0:T(128)} %tiles_ref.3) | copy-start | bytes 100
  101.6 14.2 %copy-start.6 = (s32[4,128]{1,0:T(4,128)S(1)}, s32[4,128]{1,0:T(4,128)}, u32[]{:S(2)}) copy-start(s32[4,128]{1,0:T(4,128)} %upper_maps_ref.1) | copy-start | bytes 6148
  111.0 11.4 %collective-permute-start.7 = (bf16[256,256]{1,0:T(8,128)(2,1)S(1)}, bf16[256,256]{1,0:T(8,128)(2,1)S(1)}, u32[]{:S(2)}, u32[]{:S(2)}) collective-permute-start(bf16[256,256]{1,0:T(8,128)(2,1)S(1)} %shard_map.67), channel_id=1, source_target_pairs={{0,128},{64,192},{128,0},{192,64},{256,384},{320,448},{384,256},{4... | collective-permute-start | bytes 393224 | tf_op jit(solution)/shard_map/ppermute | solution.py:299
  127.3 21.6 %all-to-all-start.4 = ((bf16[8,288,256]{2,1,0:T(8,128)(2,1)}), bf16[8,288,256]{2,1,0:T(8,128)(2,1)S(1)}, u32[]{:S(2)}, u32[]{:S(2)}) async-start(bf16[8,288,256]{2,1,0:T(8,128)(2,1)} %get-tuple-element.23), calls=%async_computation.4 | async-start | bytes 2359296 | tf_op jit(solution)/shard_map/all_to_all | solution.py:295
  132.4 30.2 %collective-permute-start.8 = (bf16[64,16,256]{2,1,0:T(8,128)(2,1)S(1)}, bf16[64,16,256]{2,1,0:T(8,128)(2,1)}, u32[]{:S(2)}, u32[]{:S(2)}) collective-permute-start(bf16[64,16,256]{2,1,0:T(8,128)(2,1)S(1)} %get-tuple-element.24), channel_id=1, source_target_pairs={{0,8},{8,0},{16,24},{24,16},{32,40},{40,32},{48,56},{56,48},{1,9},... | collective-permute-start | bytes 1572872 | tf_op jit(solution)/shard_map/ppermute | solution.py:299
  162.6 39.0 %collective-permute-start.9 = (bf16[160,256]{1,0:T(8,128)(2,1)S(1)}, bf16[160,256]{1,0:T(8,128)(2,1)S(1)}, u32[]{:S(2)}, u32[]{:S(2)}) collective-permute-start(bf16[160,256]{1,0:T(8,128)(2,1)S(1)} %slice.30), channel_id=1, source_target_pairs={{0,8},{8,0},{16,24},{24,16},{32,40},{40,32},{48,56},{56,48},{1,9},... | collective-permute-start | bytes 245768 | tf_op jit(solution)/shard_map/ppermute | solution.py:299
  229.9 18.0 %all-to-all-start.6 = ((bf16[8,16,8,256]{3,2,1,0:T(8,128)(2,1)}), bf16[8,16,8,256]{3,2,1,0:T(8,128)(2,1)S(1)}, u32[]{:S(2)}, u32[]{:S(2)}) async-start(bf16[8,16,8,256]{3,2,1,0:T(8,128)(2,1)} %broadcast_in_dim.39), calls=%async_computation.6 | async-start | bytes 1048576 | tf_op jit(solution)/shard_map/all_to_all | solution.py:295
